TPU v7x, 32 devices: a whole 2x2x4 slice. The times are simulated.
32 devices in a mesh: grp: 2 (over y), row: 4 (over z), rhs: 2 (over x), sub: 2 (over core).
Axes of the slice: x: 2, y: 2, z: 4, core: 2. Of those that a mesh axis runs over, the one named last changes fastest.
Arguments:
- right_sides: float32 [8, 512, 256], P('grp', ('row', 'sub'), 'rhs'), parts along dimension 0, may hold values from -6 to 6
- diag_inverse: float32 [8, 512, 512], P('grp', ('row', 'sub')), parts along dimension 0, may hold values from -1 to 3, as said below
- factor_below: float32 [6, 512, 256], P('grp', ('row', 'sub')), parts along dimension 0, may hold values from -0.375 to 0.375
- block_lists: int32 [6, 4, 2], P('grp', 'row'), parts along dimension 0, may hold values from 0 to 11, as said below
Outputs:
- solution: float32 [8, 512, 256], P('grp', ('row', 'sub'), 'rhs'), parts along dimension 0
There are 2 independent parts, one for each index of `grp`. A program takes and returns all parts, laid end to end along the dimension named above; each array names one. Nothing has to cross between parts.
Inputs may be any that keep to these rules, and one draw needn't show every extreme that they name: `diag_inverse`: upper triangular with diagonal entries between 0.5 and 3. block_lists[t - 1, i, :] names 2 different blocks of supernodes 0 to t - 1; entry 0 is block i of supernode t - 1.
All inputs are finite; a program needn't handle non-finite values.
Results may differ from a plain program's by a relative error of at most 0.00017.
Values sent between devices are 32-bit elements; how exact they have to be, the bound alone decides.
No kernel may reach another device: no remote copies, remote signals or barrier semaphores. Data moves between devices by JAX's collectives and lax.ppermute only.
A program may use at most 64 MiB of HBM per device.

v0:
```python
import jax
import jax.numpy as jnp
from jax import lax
from jax.sharding import PartitionSpec as P

S = 4
BS = 128


def body(right_sides, diag_inverse, factor_below, block_lists):
    highest = lax.Precision.HIGHEST
    local_rows = right_sides.shape[1]
    columns = right_sides.shape[2]
    block_count = diag_inverse.shape[2] // BS
    listed = block_lists.shape[2]
    first_row = lax.axis_index(("row", "sub")) * local_rows
    contract_first = (((0,), (0,)), ((), ()))
    results = []
    stored = jnp.zeros((S * block_count, BS, columns), jnp.float32)
    for t in range(S):
        residual = right_sides[t]
        if t > 0:
            picked = jnp.take(stored, block_lists[t - 1, 0], axis=0).reshape(listed * BS, columns)
            residual = residual - jnp.dot(
                factor_below[t - 1], picked, precision=highest, preferred_element_type=jnp.float32
            )
        term = lax.dot_general(
            diag_inverse[t],
            residual,
            contract_first,
            precision=highest,
            preferred_element_type=jnp.float32,
        )
        panel = lax.psum(term, ("row", "sub"))
        own_rows = lax.dynamic_slice_in_dim(panel, first_row, local_rows, 0)
        own_rows, panel = (own_rows, panel)
        if t + 1 < S:
            stored = stored.at[t * block_count : (t + 1) * block_count].set(
                panel.reshape(block_count, BS, columns)
            )
        results.append(own_rows)
    return jnp.stack(results)


def solution(mesh):
    in_specs = (
        P("grp", ("row", "sub"), "rhs"),
        P("grp", ("row", "sub"), None),
        P("grp", ("row", "sub"), None),
        P("grp", "row", None),
    )
    out_specs = P("grp", ("row", "sub"), "rhs")
    return jax.shard_map(body, mesh=mesh, in_specs=in_specs, out_specs=out_specs, check_vma=False)
```

profile of v0, /device:TPU:0, one launch (start us, length us, event | category | flops | bytes accessed | tf_op | source)
XLA Modules:
  0.0 247.1 jit_solution(12368694856875894360)
XLA Ops:
  6.5 2.2 fusion.6
  8.8 0.0 all-reduce.8.cloned.1.call-start
  8.8 0.6 copy-done.3
  9.4 0.2 slice_reduce_fusion
  9.7 57.6 %all-reduce.6.cloned.1.call-done = f32[512,128]{1,0:T(8,128)} async-done(((f32[512,128]{1,0:T(8,128)}), f32[512,128]{1,0:T(8,128)}) %all-reduce.6.cloned.1.call-update) | async-done | bytes 262160 | tf_op jit(solution)/shard_map/psum | solution.py:34
  67.3 1.1 scatter.10
  68.4 0.6 gather_fusion
  69.0 0.1 broadcast_select_fusion.2
  69.1 0.2 fusion.2
  69.3 0.1 copy-done
  69.5 1.1 convolution_bitcast_fusion.2
  70.7 53.9 %all-reduce.8.cloned.1.call-done = f32[512,128]{0,1:T(8,128)} async-done(((f32[512,128]{0,1:T(8,128)}), f32[512,128]{0,1:T(8,128)}) %all-reduce.8.cloned.1.call-update) | async-done | bytes 262160 | tf_op jit(solution)/shard_map/psum | solution.py:34
  124.6 1.1 copy.12
  125.7 0.6 gather_fusion.1
  126.3 0.1 broadcast_select_fusion.1
  126.4 0.2 fusion.1
  126.6 1.1 convolution_bitcast_fusion.1
  127.8 0.8 dynamic-slice_bitcast_fusion
  128.6 53.2 %all-reduce.10.cloned.1.call-done = f32[512,128]{0,1:T(8,128)} async-done(((f32[512,128]{0,1:T(8,128)}), f32[512,128]{0,1:T(8,128)}) %all-reduce.10.cloned.1.call-update) | async-done | bytes 262160 | tf_op jit(solution)/shard_map/psum | solution.py:34
  181.8 1.1 copy.13
  182.9 0.6 gather_fusion.2
  183.4 0.1 broadcast_select_fusion
  183.5 0.2 fusion
  183.8 1.1 convolution_bitcast_fusion
  184.9 0.9 constant_dynamic-slice_fusion.2
  185.8 0.1 copy.7
  185.9 0.9 constant_dynamic-slice_fusion.1
  186.8 0.1 copy.9
  186.9 52.0 %all-reduce.12.cloned.1.call-done = f32[512,128]{0,1:T(8,128)} async-done(((f32[512,128]{0,1:T(8,128)}), f32[512,128]{0,1:T(8,128)}) %all-reduce.12.cloned.1.call-update) | async-done | bytes 262160 | tf_op jit(solution)/shard_map/psum | solution.py:34
  238.9 0.9 constant_dynamic-slice_fusion
  239.8 0.1 copy.11
  239.9 0.7 pad_maximum_fusion
  (23 shorter events, 0.2 us)
Async XLA Ops:
  6.5 60.8 %all-reduce.6.cloned.1.call-start = ((), (), s32[]{:S(2)}) async-start(), calls=%async_computation | async-start | bytes 524288 | tf_op jit(solution)/shard_map/psum | solution.py:34
  8.7 0.7 copy-start.3
  8.8 115.9 %all-reduce.8.cloned.1.call-start = ((), (), s32[]{:S(2)}) async-start(), calls=%async_computation.1 | async-start | bytes 524288 | tf_op jit(solution)/shard_map/psum | solution.py:34
  67.3 1.8 copy-start.1
  67.3 1.8 copy-start.2
  68.4 1.0 copy-start
  70.6 111.2 %all-reduce.10.cloned.1.call-start = ((), (), s32[]{:S(2)}) async-start(), calls=%async_computation.2 | async-start | bytes 524288 | tf_op jit(solution)/shard_map/psum | solution.py:34
  127.8 111.1 %all-reduce.12.cloned.1.call-start = ((), (), s32[]{:S(2)}) async-start(), calls=%async_computation.3 | async-start | bytes 524288 | tf_op jit(solution)/shard_map/psum | solution.py:34
Sparse Core Ops, SparseCore 0:
  9.7 57.6 all-reduce.5
  70.7 53.8 all-reduce.7
  127.9 53.8 all-reduce.9
  185.0 53.8 all-reduce.11
where the time goes:
time: 248 us; the launch traced here: 247 us
  waiting for transfers between devices  217 us (88%)
  between operations  13.3 us (5%)
  local copies, waits for them, and re-layouts  9.65 us (4%)
  matrix products  6.23 us (3%)
    psum x4, waiting for transfers between devices, body(): panel = lax.psum(term, ('row', 'sub'))  217 us
    dot_general x4, matrix products, body(): lax.dot_general(diag_inverse[t], residual, contract_first, precision=high...  5.58 us
  transfers between devices with their start and end apart: 4, of which 4 were waited for; matrix products, arithmetic and copies ran while one was open for 1% of the time, Pallas kernels for 0%

commit v1 on v0

v1 whole, which is shorter than its diff:
```python
import functools

import jax
import jax.numpy as jnp
from jax import lax
from jax.experimental import pallas as pl
from jax.experimental.pallas import tpu as pltpu
from jax.sharding import PartitionSpec as P

S = 4
BS = 128
LANES = 128
VMEM = pl.BlockSpec(memory_space=pltpu.VMEM)
SMEM = pl.BlockSpec(memory_space=pltpu.SMEM)


def split(a):
    high = a.astype(jnp.bfloat16)
    return high, (a - high.astype(jnp.float32)).astype(jnp.bfloat16)


def dot(a, b):
    return jnp.dot(a, b, preferred_element_type=jnp.float32)


def product(a, b_high, b_low):
    a_high, a_low = split(a)
    rows = a.shape[0]
    both = dot(jnp.concatenate([a_high, a_low], axis=0), b_high)
    return both[:rows] + both[rows:] + dot(a_high, b_low)


def call(kernel, outs, scratch=()):
    return functools.partial(
        pl.pallas_call,
        kernel,
        out_shape=outs,
        scratch_shapes=list(scratch),
        compiler_params=pltpu.CompilerParams(vmem_limit_bytes=40 * 1024 * 1024),
    )


def first_kernel(quarter, ids, own, other, keep, send, turned, terms):
    width = own.shape[1] - LANES
    blocks = width // BS
    turned[...] = jnp.concatenate([own[:, width:], other[:, width:]], axis=0).T
    sides = turned[pl.ds(pl.multiple_of(ids[0] * 2 * quarter, 2 * quarter), 2 * quarter), :]
    high, low = split(jnp.concatenate([own[:, :width], other[:, :width]], axis=0))
    share = product(sides, high, low)
    for i in range(blocks):
        terms[i] = share[:, i * BS : (i + 1) * BS]
    keep[...] = terms[:, pl.ds(pl.multiple_of(ids[1] * quarter, quarter), quarter), :]
    send[...] = terms[:, pl.ds(pl.multiple_of((1 - ids[1]) * quarter, quarter), quarter), :]


def prepare_kernel(quarter, ids, a0, a1, a2, a3, diag_high, diag_low, below_high, below_low, sides, turned):
    width = diag_high.shape[1]
    depth = below_high.shape[1]
    first = pl.multiple_of(ids[0] * 2 * quarter + ids[1] * quarter, quarter)
    for j, (one, two) in enumerate(((a0, a1), (a2, a3))):
        high, low = split(jnp.concatenate([one[:, :width], two[:, :width]], axis=0))
        diag_high[j * BS : (j + 1) * BS, :] = high
        diag_low[j * BS : (j + 1) * BS, :] = low
        below = jnp.concatenate([one[:, width : width + depth], two[:, width : width + depth]], axis=0)
        high, low = split(below.T)
        below_high[j] = high
        below_low[j] = low
        turned[...] = jnp.concatenate([one[:, width + depth :], two[:, width + depth :]], axis=0).T
        sides[j] = turned[pl.ds(first, quarter), :]


def step_kernel(listed, lists, *refs):
    stored = refs[:-9]
    keep, recv, diag_high, diag_low, below_high, below_low, sides, solved, share = refs[-9:]
    blocks = keep.shape[0]
    before = solved.shape[0] - blocks
    if before:
        solved[:before] = stored[0][...]
    solved[before:] = keep[...] + recv[...]
    residuals = []
    for j in range(2):
        picked = jnp.concatenate([solved[lists[j * listed + k]] for k in range(listed)], axis=1)
        residuals.append(sides[j] - product(picked, below_high[j], below_low[j]))
    result = product(jnp.concatenate(residuals, axis=1), diag_high[...], diag_low[...])
    for i in range(blocks):
        share[i] = result[:, i * BS : (i + 1) * BS]


def last_kernel(ids, stored, keep, recv, own, send):
    blocks = keep.shape[0]
    for t in range(S - 1):
        own[t] = stored[t * blocks + ids[2]]
        send[t] = stored[t * blocks + ids[3]]
    own[S - 1] = keep[ids[2]] + recv[ids[2]]
    send[S - 1] = keep[ids[3]] + recv[ids[3]]


def place_kernel(quarter, ids, a0, a1, a2, a3, out, whole):
    core, half = ids[0], ids[1]
    rows = out.shape[1]
    for t in range(S):
        for a, c, h in ((a0, core, half), (a1, core, 1 - half), (a2, 1 - core, half), (a3, 1 - core, 1 - half)):
            whole[pl.ds(pl.multiple_of((2 * c + h) * quarter, quarter), quarter), :] = a[t]
        turned = whole[...].T
        out[t] = jnp.where(core == 0, turned[:rows], turned[rows:])


def body(count, right_sides, diag_inverse, factor_below, block_lists):
    half_count = count // 2
    quarter = right_sides.shape[2] // 4
    blocks = diag_inverse.shape[2] // BS
    width = diag_inverse.shape[2]
    depth = factor_below.shape[2]
    listed = block_lists.shape[2]
    row, core = lax.axis_index("row"), lax.axis_index("sub")
    half = row // half_count
    team = lax.rem(row + half_count, count)
    ids = jnp.stack([core, half, row, team]).astype(jnp.int32)

    def to_core(a):
        return lax.ppermute(a, "sub", [(0, 1), (1, 0)])

    def to_row(a, bit):
        return lax.ppermute(a, "row", [(i, i ^ bit) for i in range(count)])

    f32, bf16 = jnp.float32, jnp.bfloat16
    shape = jax.ShapeDtypeStruct
    piece = shape((blocks, quarter, BS), f32)

    first = jnp.concatenate([diag_inverse[0], right_sides[0]], axis=1)
    keep, send = call(
        functools.partial(first_kernel, quarter),
        (piece, piece),
        [pltpu.VMEM((4 * quarter, BS), f32), pltpu.VMEM((blocks, 2 * quarter, BS), f32)],
    )(in_specs=[SMEM, VMEM, VMEM])(ids, first, to_core(first))

    lists = jnp.concatenate([block_lists[:, 0], to_row(block_lists[:, 0], half_count)], axis=1)
    rest = [
        jnp.concatenate([diag_inverse[t], factor_below[t - 1], right_sides[t]], axis=1) for t in range(1, S)
    ]
    prepared = []
    for own in rest:
        other = to_row(own, half_count)
        prepared.append(
            call(
                functools.partial(prepare_kernel, quarter),
                (
                    shape((2 * BS, width), bf16),
                    shape((2 * BS, width), bf16),
                    shape((2, depth, BS), bf16),
                    shape((2, depth, BS), bf16),
                    shape((2, quarter, BS), f32),
                ),
                [pltpu.VMEM((4 * quarter, BS), f32)],
            )(in_specs=[SMEM] + [VMEM] * 4)(ids, own, to_core(own), other, to_core(other))
        )

    def shares(a):
        bit = half_count // 2
        while bit > 1:
            a = a + to_row(a, bit)
            bit //= 2
        return a, to_row(a, 1)

    keep, recv = shares(keep + to_row(send, half_count))
    stored = ()
    for t in range(1, S):
        solved, share = call(
            functools.partial(step_kernel, listed),
            (shape((t * blocks, quarter, BS), f32), piece),
        )(in_specs=[SMEM] + [VMEM] * (len(stored) + 7))(
            lists[t - 1], *stored, keep, recv, *prepared[t - 1]
        )
        stored = (solved,)
        keep, recv = shares(share)
    block = shape((S, quarter, BS), f32)
    own, send = call(last_kernel, (block, block))(in_specs=[SMEM] + [VMEM] * 3)(ids, *stored, keep, recv)
    other = to_row(send, half_count)
    return call(
        functools.partial(place_kernel, quarter),
        shape((S, BS // 2, 4 * quarter), f32),
        [pltpu.VMEM((4 * quarter, BS), f32)],
    )(in_specs=[SMEM] + [VMEM] * 4)(ids, own, other, to_core(own), to_core(other))


def solution(mesh):
    in_specs = (
        P("grp", ("row", "sub"), "rhs"),
        P("grp", ("row", "sub"), None),
        P("grp", ("row", "sub"), None),
        P("grp", "row", None),
    )
    out_specs = P("grp", ("row", "sub"), "rhs")
    step = functools.partial(body, mesh.shape["row"])
    return jax.shard_map(step, mesh=mesh, in_specs=in_specs, out_specs=out_specs, check_vma=False)
```

time: 248 us -> 73.3 us (0.30)
  waiting for transfers between devices: 217 us -> 51.4 us
  between operations: 13.3 us -> 0.14 us
  starting transfers between devices: 0.13 us -> 10.8 us
  Pallas kernels: 0 us -> 7.63 us
  local copies, waits for them, and re-layouts: 9.65 us -> 2.87 us
  matrix products: 6.23 us -> 0 us
    psum x4 -> x0, waiting for transfers between devices: 217 us -> none  [body(): panel = lax.psum(term, ('row', 'sub'))]
    ppermute x0 -> x19, waiting for transfers between devices: none -> 51.4 us  [the longest x10 50.2 us: to_row(): return lax.ppermute(a, 'row', [(i, i ^ bit) for i in range(count)])]
    ppermute x0 -> x19, starting transfers between devices: none -> 10.8 us  [the longest x10 8.98 us: to_row(): return lax.ppermute(a, 'row', [(i, i ^ bit) for i in range(count)])]
    pallas_call x0 -> x9, Pallas kernels: none -> 7.63 us  [the longest x3 2.6 us: body(): call(functools.partial(step_kernel, listed), (shape((t * blocks, quarter,...]
    dot_general x7 -> x0, matrix products: 6.23 us -> none  [the longest x4 5.58 us: body(): lax.dot_general(diag_inverse[t], residual, contract_first, precision=high...]
    dynamic_slice x6 -> x0, local copies, waits for them, and re-layouts: 2.98 us -> none  [body(): own_rows = lax.dynamic_slice_in_dim(panel, first_row, local_rows, 0)]
    another operation x3 -> x0, local copies, waits for them, and re-layouts: 2.91 us -> none
  transfers between devices with their start and end apart: 4 -> 19, of which waited for: 4 -> 9; matrix products, arithmetic and copies ran while one was open for 1% -> 0% of each run, Pallas kernels for 0% -> 7%
where the time goes in v1:
time: 73.3 us; the launch traced here: 73 us
  waiting for transfers between devices  51.4 us (70%)
  starting transfers between devices  10.8 us (15%)
  Pallas kernels  7.63 us (10%)
  local copies, waits for them, and re-layouts  2.87 us (4%)
    ppermute x10, waiting for transfers between devices, to_row(): return lax.ppermute(a, 'row', [(i, i ^ bit) for i in range(count)])  50.2 us
    ppermute x10, starting transfers between devices, to_row(): return lax.ppermute(a, 'row', [(i, i ^ bit) for i in range(count)])  8.98 us
    pallas_call x3, Pallas kernels, body(): call(functools.partial(step_kernel, listed), (shape((t * blocks, quarter,...  2.6 us
    pallas_call x3, Pallas kernels, body(): call(functools.partial(prepare_kernel, quarter), (shape((2 * BS, width),...  2.3 us
    ppermute x9, starting transfers between devices, to_core(): return lax.ppermute(a, 'sub', [(0, 1), (1, 0)])  1.82 us
  transfers between devices with their start and end apart: 19, of which 9 were waited for; matrix products, arithmetic and copies ran while one was open for 0% of the time, Pallas kernels for 7%

profile of v1, /device:TPU:0, one launch (start us, length us, event | category | flops | bytes accessed | tf_op | source)
XLA Modules:
  0.0 73.0 jit_solution(5235497996407154561)
XLA Ops:
  0.0 0.8 %slice_bitcast_fusion.7 = (f32[64,128]{1,0:T(8,128)S(1)}, f32[64,128]{1,0:T(8,128)S(1)}, f32[64,128]{1,0:T(8,128)S(1)}, f32[64,128]{1,0:T(8,128)S(1)}) fusion(f32[4,64,128]{2,1,0:T(8,128)} %param.4), kind=kLoop, calls=%fused_computation.11 | loop fusion | bytes 262144 | tf_op jit(solution)/shard_map/squeeze | solution.py:139
  0.8 1.2 %slice_bitcast_fusion = (f32[64,512]{1,0:T(8,128)S(1)}, f32[64,512]{1,0:T(8,128)S(1)}, f32[64,512]{1,0:T(8,128)S(1)}, f32[64,512]{1,0:T(8,128)S(1)}) fusion(f32[4,64,512]{2,1,0:T(8,128)} %param.5), kind=kLoop, calls=%fused_computation.4 | loop fusion | bytes 1048576 | tf_op jit(solution)/shard_map/squeeze | solution.py:139
  2.1 0.5 collective-permute-start.4
  2.6 3.7 %collective-permute-start.5 = (f32[64,896]{1,0:T(8,128)S(1)}, f32[64,896]{1,0:T(8,128)S(1)}, u32[]{:S(2)}, u32[]{:S(2)}) collective-permute-start(f32[64,896]{1,0:T(8,128)S(1)} %pad_maximum_fusion.a0), channel_id=1, source_target_pairs={{0,8},{4,12},{8,0},{12,4},{1,9},{5,13},{9,1},{13,5},{2,10},{6,14},... | collective-permute-start | bytes 688136 | tf_op jit(solution)/shard_map/ppermute | solution.py:124
  6.3 0.2 collective-permute-start.1
  6.5 0.3 collective-permute-start.9
  6.9 2.7 %collective-permute-start.13 = (f32[64,896]{1,0:T(8,128)S(1)}, f32[64,896]{1,0:T(8,128)S(1)}, u32[]{:S(2)}, u32[]{:S(2)}) collective-permute-start(f32[64,896]{1,0:T(8,128)S(1)} %pad_maximum_fusion.2.a0), channel_id=1, source_target_pairs={{0,8},{4,12},{8,0},{12,4},{1,9},{5,13},{9,1},{13,5},{2,10},{6,14},... | collective-permute-start | bytes 688136 | tf_op jit(solution)/shard_map/ppermute | solution.py:124
  9.6 17.9 %collective-permute-done.5.a2 = f32[64,896]{1,0:T(8,128)S(1)} collective-permute-done((f32[64,896]{1,0:T(8,128)S(1)}, f32[64,896]{1,0:T(8,128)S(1)}, u32[]{:S(2)}, u32[]{:S(2)}) %collective-permute-start.5) | collective-permute-done | bytes 229408 | tf_op jit(solution)/shard_map/ppermute | solution.py:124
  27.5 0.7 copy-done.1
  28.2 0.8 %shard_map.46 = (f32[4,32,128]{2,1,0:T(8,128)S(1)}, f32[4,32,128]{2,1,0:T(8,128)S(1)}) custom-call(s32[4]{0:T(128)S(1)} %pad_add_fusion.1.ids, f32[64,640]{1,0:T(8,128)S(1)} %pad_maximum_fusion.3.own, f32[64,640]{1,0:T(8,128)S(1)} %collective-permute-done.1.other), custom_call_target="tpu_custom_call" | custom-call | tf_op jit(solution)/shard_map/pallas_call | solution.py:131
  29.0 8.1 %collective-permute-done = s32[3,2]{0,1:T(2,128)S(1)} collective-permute-done((s32[3,2]{0,1:T(2,128)S(1)}, s32[3,2]{0,1:T(2,128)S(1)}, u32[]{:S(2)}, u32[]{:S(2)}) %collective-permute-start) | collective-permute-done | bytes 56 | tf_op jit(solution)/shard_map/ppermute | solution.py:124
  37.1 6.5 %collective-permute-done.2 = f32[4,32,128]{2,1,0:T(8,128)S(1)} collective-permute-done((f32[4,32,128]{2,1,0:T(8,128)S(1)}, f32[4,32,128]{2,1,0:T(8,128)S(1)}, u32[]{:S(2)}, u32[]{:S(2)}) %collective-permute-start.2) | collective-permute-done | bytes 65568 | tf_op jit(solution)/shard_map/ppermute | solution.py:124
  43.6 0.5 collective-permute-start.10
  44.4 0.5 collective-permute-start.14
  45.0 0.8 %shard_map.47 = (bf16[256,512]{1,0:T(8,128)(2,1)S(1)}, bf16[256,512]{1,0:T(8,128)(2,1)S(1)}, bf16[2,256,128]{2,1,0:T(8,128)(2,1)S(1)}, bf16[2,256,128]{2,1,0:T(8,128)(2,1)S(1)}, f32[2,32,128]{2,1,0:T(8,128)S(1)}) custom-call(s32[4]{0:T(128)S(1)} %pad_add_fusion.1.ids, f32[64,896]{1,0:T(8,128)S(1)} %pad_maximum_fusion.a0, ...), custom_call_target="tpu_custom_call" | custom-call | tf_op jit(solution)/shard_map/pallas_call | solution.py:145
  45.8 3.0 %collective-permute-done.3.refs_1_ = f32[4,32,128]{2,1,0:T(8,128)S(1)} collective-permute-done((f32[4,32,128]{2,1,0:T(8,128)S(1)}, f32[4,32,128]{2,1,0:T(8,128)S(1)}, u32[]{:S(2)}, u32[]{:S(2)}) %collective-permute-start.3) | collective-permute-done | bytes 65568 | tf_op jit(solution)/shard_map/ppermute | solution.py:124
  48.8 0.9 %shard_map.48 = (f32[4,32,128]{2,1,0:T(8,128)S(1)}, f32[4,32,128]{2,1,0:T(8,128)S(1)}) custom-call(s32[4]{0:T(128)S(1)} %get-tuple-element.55.lists, f32[4,32,128]{2,1,0:T(8,128)S(1)} %add.8.refs_0_, f32[4,32,128]{2,1,0:T(8,128)S(1)} %collective-permute-done.3.refs_1_, bf16[256,512]{1,0:T(8,128)(2,1)S(1)} %get-tuple-element.32.refs_2_, ...), custom_call_target="tpu_custom_call" | custom-call | tf_op jit(solution)/shard_map/pallas_call | solution.py:168
  49.6 0.3 collective-permute-start.7
  49.9 0.8 %shard_map.49 = (bf16[256,512]{1,0:T(8,128)(2,1)S(1)}, bf16[256,512]{1,0:T(8,128)(2,1)S(1)}, bf16[2,256,128]{2,1,0:T(8,128)(2,1)S(1)}, bf16[2,256,128]{2,1,0:T(8,128)(2,1)S(1)}, f32[2,32,128]{2,1,0:T(8,128)S(1)}) custom-call(s32[4]{0:T(128)S(1)} %pad_add_fusion.1.ids, f32[64,896]{1,0:T(8,128)S(1)} %pad_maximum_fusion.1.a0, ...), custom_call_target="tpu_custom_call" | custom-call | tf_op jit(solution)/shard_map/pallas_call | solution.py:145
  50.7 3.2 %collective-permute-done.7.refs_2_ = f32[4,32,128]{2,1,0:T(8,128)S(1)} collective-permute-done((f32[4,32,128]{2,1,0:T(8,128)S(1)}, f32[4,32,128]{2,1,0:T(8,128)S(1)}, u32[]{:S(2)}, u32[]{:S(2)}) %collective-permute-start.7) | collective-permute-done | bytes 65568 | tf_op jit(solution)/shard_map/ppermute | solution.py:124
  53.9 0.9 %shard_map.50 = (f32[8,32,128]{2,1,0:T(8,128)S(1)}, f32[4,32,128]{2,1,0:T(8,128)S(1)}) custom-call(s32[4]{0:T(128)S(1)} %get-tuple-element.56.lists, f32[4,32,128]{2,1,0:T(8,128)S(1)} %get-tuple-element.37.refs_0_, f32[4,32,128]{2,1,0:T(8,128)S(1)} %get-tuple-element.38.refs_1_, f32[4,32,128]{2,1,0:T(8,128)S(1)} %collective-permute-done.7.refs_2_, ...), custom_call_target="tpu_custom_call" | custom-call | tf_op jit(solution)/shard_map/pallas_call | solution.py:168
  54.8 0.3 collective-permute-start.11
  55.1 0.8 %shard_map.51 = (bf16[256,512]{1,0:T(8,128)(2,1)S(1)}, bf16[256,512]{1,0:T(8,128)(2,1)S(1)}, bf16[2,256,128]{2,1,0:T(8,128)(2,1)S(1)}, bf16[2,256,128]{2,1,0:T(8,128)(2,1)S(1)}, f32[2,32,128]{2,1,0:T(8,128)S(1)}) custom-call(s32[4]{0:T(128)S(1)} %pad_add_fusion.1.ids, f32[64,896]{1,0:T(8,128)S(1)} %pad_maximum_fusion.2.a0, ...), custom_call_target="tpu_custom_call" | custom-call | tf_op jit(solution)/shard_map/pallas_call | solution.py:145
  55.9 3.2 %collective-permute-done.11.refs_2_ = f32[4,32,128]{2,1,0:T(8,128)S(1)} collective-permute-done((f32[4,32,128]{2,1,0:T(8,128)S(1)}, f32[4,32,128]{2,1,0:T(8,128)S(1)}, u32[]{:S(2)}, u32[]{:S(2)}) %collective-permute-start.11) | collective-permute-done | bytes 65568 | tf_op jit(solution)/shard_map/ppermute | solution.py:124
  59.1 0.9 %shard_map.52 = (f32[12,32,128]{2,1,0:T(8,128)S(1)}, f32[4,32,128]{2,1,0:T(8,128)S(1)}) custom-call(s32[4]{0:T(128)S(1)} %get-tuple-element.57.lists, f32[8,32,128]{2,1,0:T(8,128)S(1)} %get-tuple-element.44.refs_0_, f32[4,32,128]{2,1,0:T(8,128)S(1)} %get-tuple-element.45.refs_1_, f32[4,32,128]{2,1,0:T(8,128)S(1)} %collective-permute-done.11.refs_2_, ...), custom_call_target="tpu_custom_call" | custom-call | tf_op jit(solution)/shard_map/pallas_call | solution.py:168
  60.0 0.3 collective-permute-start.15
  60.2 4.0 %collective-permute-done.15.recv = f32[4,32,128]{2,1,0:T(8,128)S(1)} collective-permute-done((f32[4,32,128]{2,1,0:T(8,128)S(1)}, f32[4,32,128]{2,1,0:T(8,128)S(1)}, u32[]{:S(2)}, u32[]{:S(2)}) %collective-permute-start.15) | collective-permute-done | bytes 65568 | tf_op jit(solution)/shard_map/ppermute | solution.py:124
  64.2 0.6 shard_map.53
  64.8 1.3 %collective-permute-start.16 = (f32[4,32,128]{2,1,0:T(8,128)S(1)}, f32[4,32,128]{2,1,0:T(8,128)S(1)}, u32[]{:S(2)}, u32[]{:S(2)}) collective-permute-start(f32[4,32,128]{2,1,0:T(8,128)S(1)} %get-tuple-element.54), channel_id=1, source_target_pairs={{0,8},{4,12},{8,0},{12,4},{1,9},{5,13},{9,1},{13,5},{2,10},{6,14},... | collective-permute-start | bytes 196616 | tf_op jit(solution)/shard_map/ppermute | solution.py:124
  66.1 4.3 %collective-permute-done.16.a1 = f32[4,32,128]{2,1,0:T(8,128)S(1)} collective-permute-done((f32[4,32,128]{2,1,0:T(8,128)S(1)}, f32[4,32,128]{2,1,0:T(8,128)S(1)}, u32[]{:S(2)}, u32[]{:S(2)}) %collective-permute-start.16) | collective-permute-done | bytes 65568 | tf_op jit(solution)/shard_map/ppermute | solution.py:124
  70.4 1.2 %collective-permute-done.18.a3 = f32[4,32,128]{2,1,0:T(8,128)S(1)} collective-permute-done((f32[4,32,128]{2,1,0:T(8,128)S(1)}, f32[4,32,128]{2,1,0:T(8,128)S(1)}, u32[]{:S(2)}, u32[]{:S(2)}) %collective-permute-start.18) | collective-permute-done | bytes 65568 | tf_op jit(solution)/shard_map/ppermute | solution.py:121
  71.7 1.4 %shard_map.54 = f32[4,64,128]{2,1,0:T(8,128)} custom-call(s32[4]{0:T(128)S(1)} %pad_add_fusion.1.ids, f32[4,32,128]{2,1,0:T(8,128)S(1)} %get-tuple-element.53.a0, f32[4,32,128]{2,1,0:T(8,128)S(1)} %collective-permute-done.16.a1, f32[4,32,128]{2,1,0:T(8,128)S(1)} %collective-permute-done.17.a2, f32[4,32,128]{2,1,0:T(8,128)S(1)} %collective-permute-done.18.a3), custom_call_target="tpu_custom_call" | custom-call | tf_op jit(solution)/shard_map/pallas_call | solution.py:179
  (30 shorter events, 0.6 us)
Async XLA Ops:
  0.8 1.2 %copy-start = (f32[3,64,256]{2,1,0:T(8,128)S(1)}, f32[3,64,256]{2,1,0:T(8,128)}, u32[]{:S(2)}) copy-start(f32[3,64,256]{2,1,0:T(8,128)} %param.6) | copy-start | bytes 589828
  2.1 42.1 %collective-permute-start.4 = (f32[64,896]{1,0:T(8,128)S(1)}, f32[64,896]{1,0:T(8,128)S(1)}, u32[]{:S(2)}, u32[]{:S(2)}) collective-permute-start(f32[64,896]{1,0:T(8,128)S(1)} %pad_maximum_fusion.a0), channel_id=1, source_target_pairs={{0,1},{1,0},{2,3},{3,2},{4,5},{5,4},{6,7},{7,6},{8,9},{9,8},{10,11... | collective-permute-start | bytes 688136 | tf_op jit(solution)/shard_map/ppermute | solution.py:121
  2.6 24.9 %collective-permute-start.5 = (f32[64,896]{1,0:T(8,128)S(1)}, f32[64,896]{1,0:T(8,128)S(1)}, u32[]{:S(2)}, u32[]{:S(2)}) collective-permute-start(f32[64,896]{1,0:T(8,128)S(1)} %pad_maximum_fusion.a0), channel_id=1, source_target_pairs={{0,8},{4,12},{8,0},{12,4},{1,9},{5,13},{9,1},{13,5},{2,10},{6,14},... | collective-permute-start | bytes 688136 | tf_op jit(solution)/shard_map/ppermute | solution.py:124
  6.3 21.3 %collective-permute-start.1 = (f32[64,640]{1,0:T(8,128)S(1)}, f32[64,640]{1,0:T(8,128)S(1)}, u32[]{:S(2)}, u32[]{:S(2)}) collective-permute-start(f32[64,640]{1,0:T(8,128)S(1)} %pad_maximum_fusion.3.own), channel_id=1, source_target_pairs={{0,1},{1,0},{2,3},{3,2},{4,5},{5,4},{6,7},{7,6},{8,9},{9,8},{10,11... | collective-permute-start | bytes 491528 | tf_op jit(solution)/shard_map/ppermute | solution.py:121
  6.5 37.1 %collective-permute-start.9 = (f32[64,896]{1,0:T(8,128)S(1)}, f32[64,896]{1,0:T(8,128)S(1)}, u32[]{:S(2)}, u32[]{:S(2)}) collective-permute-start(f32[64,896]{1,0:T(8,128)S(1)} %pad_maximum_fusion.1.a0), channel_id=1, source_target_pairs={{0,8},{4,12},{8,0},{12,4},{1,9},{5,13},{9,1},{13,5},{2,10},{6,14},... | collective-permute-start | bytes 688136 | tf_op jit(solution)/shard_map/ppermute | solution.py:124
  6.9 37.4 %collective-permute-start.13 = (f32[64,896]{1,0:T(8,128)S(1)}, f32[64,896]{1,0:T(8,128)S(1)}, u32[]{:S(2)}, u32[]{:S(2)}) collective-permute-start(f32[64,896]{1,0:T(8,128)S(1)} %pad_maximum_fusion.2.a0), channel_id=1, source_target_pairs={{0,8},{4,12},{8,0},{12,4},{1,9},{5,13},{9,1},{13,5},{2,10},{6,14},... | collective-permute-start | bytes 688136 | tf_op jit(solution)/shard_map/ppermute | solution.py:124
  27.4 16.9 %collective-permute-start.6 = (f32[64,896]{1,0:T(8,128)S(1)}, f32[64,896]{1,0:T(8,128)S(1)}, u32[]{:S(2)}, u32[]{:S(2)}) collective-permute-start(f32[64,896]{1,0:T(8,128)S(1)} %collective-permute-done.5.a2), channel_id=1, source_target_pairs={{0,1},{1,0},{2,3},{3,2},{4,5},{5,4},{6,7},{7,6},{8,9},{9,8},{10,11... | collective-permute-start | bytes 688136 | tf_op jit(solution)/shard_map/ppermute | solution.py:121
  27.5 0.7 copy-start.1
  28.2 8.9 %collective-permute-start = (s32[3,2]{0,1:T(2,128)S(1)}, s32[3,2]{0,1:T(2,128)S(1)}, u32[]{:S(2)}, u32[]{:S(2)}) collective-permute-start(s32[3,2]{0,1:T(2,128)S(1)} %bitcast.27), channel_id=1, source_target_pairs={{0,8},{4,12},{8,0},{12,4},{1,9},{5,13},{9,1},{13,5},{2,10},{6,14},... | collective-permute-start | bytes 80 | tf_op jit(solution)/shard_map/ppermute | solution.py:124
  37.1 6.5 %collective-permute-start.2 = (f32[4,32,128]{2,1,0:T(8,128)S(1)}, f32[4,32,128]{2,1,0:T(8,128)S(1)}, u32[]{:S(2)}, u32[]{:S(2)}) collective-permute-start(f32[4,32,128]{2,1,0:T(8,128)S(1)} %get-tuple-element.31), channel_id=1, source_target_pairs={{0,8},{4,12},{8,0},{12,4},{1,9},{5,13},{9,1},{13,5},{2,10},{6,14},... | collective-permute-start | bytes 196616 | tf_op jit(solution)/shard_map/ppermute | solution.py:124
  43.6 6.3 %collective-permute-start.8 = (f32[64,896]{1,0:T(8,128)S(1)}, f32[64,896]{1,0:T(8,128)S(1)}, u32[]{:S(2)}, u32[]{:S(2)}) collective-permute-start(f32[64,896]{1,0:T(8,128)S(1)} %pad_maximum_fusion.1.a0), channel_id=1, source_target_pairs={{0,1},{1,0},{2,3},{3,2},{4,5},{5,4},{6,7},{7,6},{8,9},{9,8},{10,11... | collective-permute-start | bytes 688136 | tf_op jit(solution)/shard_map/ppermute | solution.py:121
  43.6 6.3 %collective-permute-start.10 = (f32[64,896]{1,0:T(8,128)S(1)}, f32[64,896]{1,0:T(8,128)S(1)}, u32[]{:S(2)}, u32[]{:S(2)}) collective-permute-start(f32[64,896]{1,0:T(8,128)S(1)} %collective-permute-done.9.a2), channel_id=1, source_target_pairs={{0,1},{1,0},{2,3},{3,2},{4,5},{5,4},{6,7},{7,6},{8,9},{9,8},{10,11... | collective-permute-start | bytes 688136 | tf_op jit(solution)/shard_map/ppermute | solution.py:121
  44.2 10.9 %collective-permute-start.12 = (f32[64,896]{1,0:T(8,128)S(1)}, f32[64,896]{1,0:T(8,128)S(1)}, u32[]{:S(2)}, u32[]{:S(2)}) collective-permute-start(f32[64,896]{1,0:T(8,128)S(1)} %pad_maximum_fusion.2.a0), channel_id=1, source_target_pairs={{0,1},{1,0},{2,3},{3,2},{4,5},{5,4},{6,7},{7,6},{8,9},{9,8},{10,11... | collective-permute-start | bytes 688136 | tf_op jit(solution)/shard_map/ppermute | solution.py:121
  44.3 4.5 %collective-permute-start.3 = (f32[4,32,128]{2,1,0:T(8,128)S(1)}, f32[4,32,128]{2,1,0:T(8,128)S(1)}, u32[]{:S(2)}, u32[]{:S(2)}) collective-permute-start(f32[4,32,128]{2,1,0:T(8,128)S(1)} %add.8.refs_0_), channel_id=1, source_target_pairs={{0,4},{4,0},{8,12},{12,8},{1,5},{5,1},{9,13},{13,9},{2,6},{6,2},{1... | collective-permute-start | bytes 196616 | tf_op jit(solution)/shard_map/ppermute | solution.py:124
  44.4 10.7 %collective-permute-start.14 = (f32[64,896]{1,0:T(8,128)S(1)}, f32[64,896]{1,0:T(8,128)S(1)}, u32[]{:S(2)}, u32[]{:S(2)}) collective-permute-start(f32[64,896]{1,0:T(8,128)S(1)} %collective-permute-done.13.a2), channel_id=1, source_target_pairs={{0,1},{1,0},{2,3},{3,2},{4,5},{5,4},{6,7},{7,6},{8,9},{9,8},{10,11... | collective-permute-start | bytes 688136 | tf_op jit(solution)/shard_map/ppermute | solution.py:121
  49.6 4.3 %collective-permute-start.7 = (f32[4,32,128]{2,1,0:T(8,128)S(1)}, f32[4,32,128]{2,1,0:T(8,128)S(1)}, u32[]{:S(2)}, u32[]{:S(2)}) collective-permute-start(f32[4,32,128]{2,1,0:T(8,128)S(1)} %get-tuple-element.38.refs_1_), channel_id=1, source_target_pairs={{0,4},{4,0},{8,12},{12,8},{1,5},{5,1},{9,13},{13,9},{2,6},{6,2},{1... | collective-permute-start | bytes 196616 | tf_op jit(solution)/shard_map/ppermute | solution.py:124
  54.8 4.3 %collective-permute-start.11 = (f32[4,32,128]{2,1,0:T(8,128)S(1)}, f32[4,32,128]{2,1,0:T(8,128)S(1)}, u32[]{:S(2)}, u32[]{:S(2)}) collective-permute-start(f32[4,32,128]{2,1,0:T(8,128)S(1)} %get-tuple-element.45.refs_1_), channel_id=1, source_target_pairs={{0,4},{4,0},{8,12},{12,8},{1,5},{5,1},{9,13},{13,9},{2,6},{6,2},{1... | collective-permute-start | bytes 196616 | tf_op jit(solution)/shard_map/ppermute | solution.py:124
  60.0 4.3 %collective-permute-start.15 = (f32[4,32,128]{2,1,0:T(8,128)S(1)}, f32[4,32,128]{2,1,0:T(8,128)S(1)}, u32[]{:S(2)}, u32[]{:S(2)}) collective-permute-start(f32[4,32,128]{2,1,0:T(8,128)S(1)} %get-tuple-element.52.keep), channel_id=1, source_target_pairs={{0,4},{4,0},{8,12},{12,8},{1,5},{5,1},{9,13},{13,9},{2,6},{6,2},{1... | collective-permute-start | bytes 196616 | tf_op jit(solution)/shard_map/ppermute | solution.py:124
  64.8 5.6 %collective-permute-start.16 = (f32[4,32,128]{2,1,0:T(8,128)S(1)}, f32[4,32,128]{2,1,0:T(8,128)S(1)}, u32[]{:S(2)}, u32[]{:S(2)}) collective-permute-start(f32[4,32,128]{2,1,0:T(8,128)S(1)} %get-tuple-element.54), channel_id=1, source_target_pairs={{0,8},{4,12},{8,0},{12,4},{1,9},{5,13},{9,1},{13,5},{2,10},{6,14},... | collective-permute-start | bytes 196616 | tf_op jit(solution)/shard_map/ppermute | solution.py:124
  66.1 4.3 %collective-permute-start.17 = (f32[4,32,128]{2,1,0:T(8,128)S(1)}, f32[4,32,128]{2,1,0:T(8,128)S(1)}, u32[]{:S(2)}, u32[]{:S(2)}) collective-permute-start(f32[4,32,128]{2,1,0:T(8,128)S(1)} %get-tuple-element.53.a0), channel_id=1, source_target_pairs={{0,1},{1,0},{2,3},{3,2},{4,5},{5,4},{6,7},{7,6},{8,9},{9,8},{10,11... | collective-permute-start | bytes 196616 | tf_op jit(solution)/shard_map/ppermute | solution.py:121
  70.4 1.3 %collective-permute-start.18 = (f32[4,32,128]{2,1,0:T(8,128)S(1)}, f32[4,32,128]{2,1,0:T(8,128)S(1)}, u32[]{:S(2)}, u32[]{:S(2)}) collective-permute-start(f32[4,32,128]{2,1,0:T(8,128)S(1)} %collective-permute-done.16.a1), channel_id=1, source_target_pairs={{0,1},{1,0},{2,3},{3,2},{4,5},{5,4},{6,7},{7,6},{8,9},{9,8},{10,11... | collective-permute-start | bytes 196616 | tf_op jit(solution)/shard_map/ppermute | solution.py:121

commit v2 on v1

v2 whole, which is shorter than its diff:
```python
import functools

import jax
import jax.numpy as jnp
from jax import lax
from jax.experimental import pallas as pl
from jax.experimental.pallas import tpu as pltpu
from jax.sharding import PartitionSpec as P

K = {'first': 0.3, 'prep': [1, 16, 16], 'step': [4, 1, 0.3], 'bulk': ['send', 'share0', 'recv0'], 'swap': ['recv0', 'recv0', 'recv1']}
S = 4
BS = 128
LANES = 128
VMEM = pl.BlockSpec(memory_space=pltpu.VMEM)
SMEM = pl.BlockSpec(memory_space=pltpu.SMEM)


def split(a):
    high = a.astype(jnp.bfloat16)
    return high, (a - high.astype(jnp.float32)).astype(jnp.bfloat16)


def dot(a, b):
    return jnp.dot(a, b, preferred_element_type=jnp.float32)


def product(a, b_high, b_low):
    a_high, a_low = split(a)
    rows = a.shape[0]
    both = dot(jnp.concatenate([a_high, a_low], axis=0), b_high)
    return both[:rows] + both[rows:] + dot(a_high, b_low)


def call(kernel, outs, scratch=(), cost=0):
    return functools.partial(
        pl.pallas_call,
        kernel,
        out_shape=outs,
        scratch_shapes=list(scratch),
        compiler_params=pltpu.CompilerParams(vmem_limit_bytes=40 * 1024 * 1024),
        cost_estimate=pl.CostEstimate(flops=int(cost * 1e9), bytes_accessed=1000, transcendentals=0),
    )


def first_kernel(quarter, ids, lists, own, other, keep, send, turned, terms):
    width = own.shape[1] - LANES
    blocks = width // BS
    turned[...] = jnp.concatenate([own[:, width:], other[:, width:]], axis=0).T
    sides = turned[pl.ds(pl.multiple_of(ids[0] * 2 * quarter, 2 * quarter), 2 * quarter), :]
    high, low = split(jnp.concatenate([own[:, :width], other[:, :width]], axis=0))
    share = product(sides, high, low)
    for i in range(blocks):
        terms[i] = share[:, i * BS : (i + 1) * BS]
    keep[...] = terms[:, pl.ds(pl.multiple_of(ids[1] * quarter, quarter), quarter), :]
    send[:blocks] = terms[:, pl.ds(pl.multiple_of((1 - ids[1]) * quarter, quarter), quarter), :]
    lane = lax.broadcasted_iota(jnp.int32, (quarter, BS), 1)
    told = jnp.zeros((quarter, BS), jnp.float32)
    for i in range(lists.shape[0]):
        for k in range(lists.shape[1]):
            told = jnp.where(lane == i * lists.shape[1] + k, lists[i, k].astype(jnp.float32), told)
    send[blocks] = told


def prepare_kernel(quarter, ids, a0, a1, a2, a3, diag_high, diag_low, below_high, below_low, sides, turned):
    width = diag_high.shape[1]
    depth = below_high.shape[1]
    first = pl.multiple_of(ids[0] * 2 * quarter + ids[1] * quarter, quarter)
    for j, (one, two) in enumerate(((a0, a1), (a2, a3))):
        high, low = split(jnp.concatenate([one[:, :width], two[:, :width]], axis=0))
        diag_high[j * BS : (j + 1) * BS, :] = high
        diag_low[j * BS : (j + 1) * BS, :] = low
        below = jnp.concatenate([one[:, width : width + depth], two[:, width : width + depth]], axis=0)
        high, low = split(below.T)
        below_high[j] = high
        below_low[j] = low
        turned[...] = jnp.concatenate([one[:, width + depth :], two[:, width + depth :]], axis=0).T
        sides[j] = turned[pl.ds(first, quarter), :]


def advance(listed, lists, stored, refs, solved):
    keep, recv, diag_high, diag_low, below_high, below_low, sides = refs
    before = solved.shape[0] - keep.shape[0]
    if before:
        solved[:before] = stored[0][...]
    solved[before:] = keep[...] + recv[...]
    residuals = []
    for j in range(2):
        picked = jnp.concatenate([solved[lists[j, k]] for k in range(listed)], axis=1)
        residuals.append(sides[j] - product(picked, below_high[j], below_low[j]))
    return product(jnp.concatenate(residuals, axis=1), diag_high[...], diag_low[...])


def step_kernel(listed, lists, *refs):
    solved, share = refs[-2:]
    result = advance(listed, lists, refs[:-9], refs[-9:-2], solved)
    for i in range(share.shape[0]):
        share[i] = result[:, i * BS : (i + 1) * BS]


def give(ids, solved, share, own, near, far, both):
    blocks = share.shape[0]
    for t in range(S - 1):
        own[t] = solved[t * blocks + ids[2]]
        near[t] = solved[t * blocks + ids[3]]
    own[S - 1] = share[ids[2]]
    near[S - 1] = share[ids[3]]
    far[...] = share[ids[4]]
    both[...] = share[ids[5]]


def last_kernel(listed, ids, lists, *refs):
    own, near, far, both, solved, share = refs[-6:]
    result = advance(listed, lists, refs[:-13], refs[-13:-6], solved)
    for i in range(share.shape[0]):
        share[i] = result[:, i * BS : (i + 1) * BS]
    give(ids, solved, share, own, near, far, both)


def place_kernel(quarter, ids, *refs):
    quarters, out, whole = refs[:-2], refs[-2], refs[-1]
    core, half = ids[0], ids[1]
    rows = out.shape[1]
    places = ((core, half), (core, 1 - half), (1 - core, half), (1 - core, 1 - half))
    for t in range(S):
        for i, (c, h) in enumerate(places):
            part = quarters[2 * i][t]
            if t == S - 1:
                part = part + quarters[2 * i + 1][...]
            whole[pl.ds(pl.multiple_of((2 * c + h) * quarter, quarter), quarter), :] = part
        mine = jnp.where(core == 0, whole[:, :rows], whole[:, rows:])
        out[t] = mine.T


def body(count, right_sides, diag_inverse, factor_below, block_lists):
    quarter = right_sides.shape[2] // 4
    blocks = diag_inverse.shape[2] // BS
    width = diag_inverse.shape[2]
    depth = factor_below.shape[2]
    listed = block_lists.shape[2]
    top = count // 2
    row, core = lax.axis_index("row"), lax.axis_index("sub")
    half = lax.rem(row, 2)
    team = row + 1 - 2 * half
    far = lax.rem(row + top, count)
    ids = jnp.stack([core, half, row, team, far, far + 1 - 2 * half]).astype(jnp.int32)

    def to_core(a):
        return lax.ppermute(a, "sub", [(0, 1), (1, 0)])

    def to_row(a, bit):
        return lax.ppermute(a, "row", [(i, i ^ bit) for i in range(count)])

    def after(a, *others):
        return lax.optimization_barrier((a, *others))[0]

    f32, bf16 = jnp.float32, jnp.bfloat16
    shape = jax.ShapeDtypeStruct
    piece = shape((blocks, quarter, BS), f32)

    def total(a):
        bit = 2
        while bit < top:
            a = a + to_row(a, bit)
            bit *= 2
        return a, to_row(a, top)

    def prepare(t, own, own_core, other, other_core):
        return call(
            functools.partial(prepare_kernel, quarter),
            (
                shape((2 * BS, width), bf16),
                shape((2 * BS, width), bf16),
                shape((2, depth, BS), bf16),
                shape((2, depth, BS), bf16),
                shape((2, quarter, BS), f32),
            ),
            [pltpu.VMEM((4 * quarter, BS), f32)],
            K["prep"][t - 1],
        )(in_specs=[SMEM] + [VMEM] * 4)(ids, own, own_core, other, other_core)

    first = jnp.concatenate([diag_inverse[0], right_sides[0]], axis=1)
    first_core = to_core(first)
    keep, send = call(
        functools.partial(first_kernel, quarter),
        (piece, shape((blocks + 1, quarter, BS), f32)),
        [pltpu.VMEM((4 * quarter, BS), f32), pltpu.VMEM((blocks, 2 * quarter, BS), f32)],
        K["first"],
    )(in_specs=[SMEM, SMEM, VMEM, VMEM])(ids, block_lists[:, 0], first, first_core)
    got = to_row(send, 1)

    diag, below, sides, _ = lax.optimization_barrier((diag_inverse, factor_below, right_sides, send))
    rest = [jnp.concatenate([diag[t], below[t - 1], sides[t]], axis=1) for t in range(1, S)]
    rest_core = [to_core(a) for a in rest]

    share = keep + got[:blocks]
    told = got[blocks, 0, : (S - 1) * listed].reshape(S - 1, listed).astype(jnp.int32)
    lists = jnp.stack([block_lists[:, 0], told], axis=1)

    gates = {"send": send, "share0": share, "core1": rest_core[0], "core2": rest_core[1], "core3": rest_core[2]}
    stored = ()
    others = {}

    def bulk(u):
        if u not in others and K["bulk"][u - 1] in gates:
            others[u] = to_row(after(rest[u - 1], gates[K["bulk"][u - 1]]), 1)

    for t in range(1, S):
        for u in range(1, S):
            bulk(u)
        keep, recv = total(share)
        gates[f"recv{t - 1}"] = recv
        for u in range(1, S):
            bulk(u)
        other = others[t]
        g = K["swap"][t - 1]
        other_core = to_core(after(other, gates[g]) if g else other)
        gates[f"other{t}"] = other_core
        for u in range(1, S):
            bulk(u)
        operands = (*stored, keep, recv, *prepare(t, rest[t - 1], rest_core[t - 1], other, other_core))
        gates[f"prep{t}"] = operands[-1]
        for u in range(1, S):
            bulk(u)
        solved_shape = shape((t * blocks, quarter, BS), f32)
        if t < S - 1 or top > 2:
            solved, share = call(functools.partial(step_kernel, listed), (solved_shape, piece), (), K["step"][t - 1])(
                in_specs=[SMEM] + [VMEM] * len(operands)
            )(lists[t - 1], *operands)
            stored = (solved,)
            gates[f"share{t}"] = share

    block = shape((quarter, BS), f32)
    kept = shape((S, quarter, BS), f32)
    gifts = (kept, kept, block, block)
    if top > 2:
        bit = 2
        while bit < top:
            share = share + to_row(share, bit)
            bit *= 2
        own, *sent = call(give, gifts)(in_specs=[SMEM, VMEM, VMEM])(ids, solved, share)
    else:
        own, *sent = call(
            functools.partial(last_kernel, listed),
            gifts,
            [pltpu.VMEM(solved_shape.shape, f32), pltpu.VMEM(piece.shape, f32)],
            K["step"][S - 2],
        )(in_specs=[SMEM, SMEM] + [VMEM] * len(operands))(ids, lists[S - 2], *operands)
    near, far, both = [to_row(a, bit) for a, bit in zip(sent, (1, top, top + 1))]
    near, far, both = lax.optimization_barrier((near, far, both))
    quarters = [own, far, near, both]
    quarters += [to_core(a) for a in quarters]
    return call(
        functools.partial(place_kernel, quarter),
        shape((S, BS // 2, 4 * quarter), f32),
        [pltpu.VMEM((4 * quarter, BS), f32)],
    )(in_specs=[SMEM] + [VMEM] * 8)(ids, *quarters)


def solution(mesh):
    in_specs = (
        P("grp", ("row", "sub"), "rhs"),
        P("grp", ("row", "sub"), None),
        P("grp", ("row", "sub"), None),
        P("grp", "row", None),
    )
    out_specs = P("grp", ("row", "sub"), "rhs")
    step = functools.partial(body, mesh.shape["row"])
    return jax.shard_map(step, mesh=mesh, in_specs=in_specs, out_specs=out_specs, check_vma=False)
```

time: 73.3 us -> 51.7 us (0.71)
  waiting for transfers between devices: 51.4 us -> 19.7 us
  starting transfers between devices: 10.8 us -> 21.5 us
    ppermute x10, waiting for transfers between devices: 50.2 us -> 18.4 us  [to_row(): return lax.ppermute(a, 'row', [(i, i ^ bit) for i in range(count)])]
    ppermute x10, starting transfers between devices: 8.98 us -> 20.1 us  [to_row(): return lax.ppermute(a, 'row', [(i, i ^ bit) for i in range(count)])]
    pallas_call x8 -> x7, Pallas kernels: 6.28 us -> 5.82 us  [the longest x3 2.31 us: prepare(): call(functools.partial(prepare_kernel, quarter), (shape((2 * BS, width),...]
    ppermute x9 -> x11, starting transfers between devices: 1.82 us -> 1.41 us  [to_core(): return lax.ppermute(a, 'sub', [(0, 1), (1, 0)])]
    squeeze x3 -> x6, local copies, waits for them, and re-layouts: 2 us -> 1.82 us  [the longest x2 1.67 us: body(): first = jnp.concatenate([diag_inverse[0], right_sides[0]], axis=1)]
  transfers between devices with their start and end apart: 19 -> 21, of which waited for: 9 -> 11; matrix products, arithmetic and copies ran while one was open for 0% -> 1% of each run, Pallas kernels for 7% -> 8%
where the time goes in v2:
time: 51.7 us; the launch traced here: 51.5 us
  starting transfers between devices  21.5 us (42%)
  waiting for transfers between devices  19.7 us (38%)
  Pallas kernels  7.24 us (14%)
  local copies, waits for them, and re-layouts  2.77 us (5%)
    ppermute x10, starting transfers between devices, to_row(): return lax.ppermute(a, 'row', [(i, i ^ bit) for i in range(count)])  20.1 us
    ppermute x10, waiting for transfers between devices, to_row(): return lax.ppermute(a, 'row', [(i, i ^ bit) for i in range(count)])  18.4 us
    pallas_call x3, Pallas kernels, prepare(): call(functools.partial(prepare_kernel, quarter), (shape((2 * BS, width),...  2.31 us
    pallas_call x2, Pallas kernels, body(): call(functools.partial(step_kernel, listed), (solved_shape, piece), (), K...  1.76 us
    squeeze x2, local copies, waits for them, and re-layouts, body(): first = jnp.concatenate([diag_inverse[0], right_sides[0]], axis=1)  1.67 us
    pallas_call x1, Pallas kernels, body(): call(functools.partial(place_kernel, quarter), shape((S, BS // 2, 4 * qua...  1.42 us
    ppermute x11, starting transfers between devices, to_core(): return lax.ppermute(a, 'sub', [(0, 1), (1, 0)])  1.41 us
    ppermute x11, waiting for transfers between devices, to_core(): return lax.ppermute(a, 'sub', [(0, 1), (1, 0)])  1.28 us
  transfers between devices with their start and end apart: 21, of which 11 were waited for; matrix products, arithmetic and copies ran while one was open for 1% of the time, Pallas kernels for 8%

profile of v2, /device:TPU:0, one launch (start us, length us, event | category | flops | bytes accessed | tf_op | source)
XLA Modules:
  0.0 51.5 jit_solution(6428530892920994177)
XLA Ops:
  0.0 0.8 %slice_bitcast_fusion.10 = f32[64,128]{1,0:T(8,128)S(1)} fusion(f32[4,64,128]{2,1,0:T(8,128)} %param.4), kind=kLoop, calls=%fused_computation.15 | loop fusion | bytes 65536 | tf_op jit(solution)/shard_map/squeeze | solution.py:181
  0.8 0.9 %slice_bitcast_fusion.3 = f32[64,512]{1,0:T(8,128)S(1)} fusion(f32[4,64,512]{2,1,0:T(8,128)} %param.5), kind=kLoop, calls=%fused_computation.7 | loop fusion | bytes 262144 | tf_op jit(solution)/shard_map/squeeze | solution.py:181
  1.7 0.5 %collective-permute-start = (f32[64,640]{1,0:T(8,128)S(1)}, f32[64,640]{1,0:T(8,128)S(1)}, u32[]{:S(2)}, u32[]{:S(2)}) collective-permute-start(f32[64,640]{1,0:T(8,128)S(1)} %pad_maximum_fusion.3.own), channel_id=1, source_target_pairs={{0,1},{1,0},{2,3},{3,2},{4,5},{5,4},{6,7},{7,6},{8,9},{9,8},{10,11... | collective-permute-start | bytes 491528 | tf_op jit(solution)/shard_map/ppermute | solution.py:148
  2.2 0.7 %copy-done.3 = s32[3,1,2]{0,2,1:T(2,128)S(1)} copy-done((s32[3,1,2]{0,2,1:T(2,128)S(1)}, s32[3,1,2]{0,2,1:T(2,128)}, u32[]{:S(2)}) %copy-start.3) | copy-done | bytes 48
  3.2 0.9 %shard_map.46 = (f32[4,32,128]{2,1,0:T(8,128)S(1)}, f32[5,32,128]{2,1,0:T(8,128)S(1)}) custom-call(s32[6]{0:T(128)S(1)} %stack.31.ids, s32[3,2]{1,0:T(4,128)S(1)} %copy.7.lists, f32[64,640]{1,0:T(8,128)S(1)} %pad_maximum_fusion.3.own, f32[64,640]{1,0:T(8,128)S(1)} %collective-permute-done.other), custom_call_target="tpu_custom_call" | custom-call | flops 300000000 | bytes 1000 | tf_op jit(solution)/shard_map/pallas_call | solution.py:183
  4.1 3.0 %collective-permute-start.1 = (f32[5,32,128]{2,1,0:T(8,128)S(1)}, f32[5,32,128]{2,1,0:T(8,128)S(1)}, u32[]{:S(2)}, u32[]{:S(2)}) collective-permute-start(f32[5,32,128]{2,1,0:T(8,128)S(1)} %get-tuple-element.42), channel_id=1, source_target_pairs={{0,4},{4,0},{8,12},{12,8},{1,5},{5,1},{9,13},{13,9},{2,6},{6,2},{1... | collective-permute-start | bytes 245768 | tf_op jit(solution)/shard_map/ppermute | solution.py:151
  7.3 1.1 %collective-permute-start.4 = (f32[64,896]{1,0:T(8,128)S(1)}, f32[64,896]{1,0:T(8,128)S(1)}, u32[]{:S(2)}, u32[]{:S(2)}) collective-permute-start(f32[64,896]{1,0:T(8,128)S(1)} %pad_maximum_fusion.a0), channel_id=1, source_target_pairs={{0,4},{4,0},{8,12},{12,8},{1,5},{5,1},{9,13},{13,9},{2,6},{6,2},{1... | collective-permute-start | bytes 688136 | tf_op jit(solution)/shard_map/ppermute | solution.py:151
  8.4 1.5 %collective-permute-done.1 = f32[5,32,128]{2,1,0:T(8,128)S(1)} collective-permute-done((f32[5,32,128]{2,1,0:T(8,128)S(1)}, f32[5,32,128]{2,1,0:T(8,128)S(1)}, u32[]{:S(2)}, u32[]{:S(2)}) %collective-permute-start.1) | collective-permute-done | bytes 81952 | tf_op jit(solution)/shard_map/ppermute | solution.py:151
  9.9 2.8 %collective-permute-start.2 = (f32[4,32,128]{2,1,0:T(8,128)S(1)}, f32[4,32,128]{2,1,0:T(8,128)S(1)}, u32[]{:S(2)}, u32[]{:S(2)}) collective-permute-start(f32[4,32,128]{2,1,0:T(8,128)S(1)} %slice_add_fusion.refs_0_), channel_id=1, source_target_pairs={{0,8},{4,12},{8,0},{12,4},{1,9},{5,13},{9,1},{13,5},{2,10},{6,14},... | collective-permute-start | bytes 196616 | tf_op jit(solution)/shard_map/ppermute | solution.py:151
  12.8 2.0 %collective-permute-start.8 = (f32[64,896]{1,0:T(8,128)S(1)}, f32[64,896]{1,0:T(8,128)S(1)}, u32[]{:S(2)}, u32[]{:S(2)}) collective-permute-start(f32[64,896]{1,0:T(8,128)S(1)} %pad_maximum_fusion.1.a0), channel_id=1, source_target_pairs={{0,4},{4,0},{8,12},{12,8},{1,5},{5,1},{9,13},{13,9},{2,6},{6,2},{1... | collective-permute-start | bytes 688136 | tf_op jit(solution)/shard_map/ppermute | solution.py:151
  14.8 0.7 %collective-permute-done.2.refs_1_ = f32[4,32,128]{2,1,0:T(8,128)S(1)} collective-permute-done((f32[4,32,128]{2,1,0:T(8,128)S(1)}, f32[4,32,128]{2,1,0:T(8,128)S(1)}, u32[]{:S(2)}, u32[]{:S(2)}) %collective-permute-start.2) | collective-permute-done | bytes 65568 | tf_op jit(solution)/shard_map/ppermute | solution.py:151
  15.5 1.7 %collective-permute-done.4.a2 = f32[64,896]{1,0:T(8,128)S(1)} collective-permute-done((f32[64,896]{1,0:T(8,128)S(1)}, f32[64,896]{1,0:T(8,128)S(1)}, u32[]{:S(2)}, u32[]{:S(2)}) %collective-permute-start.4) | collective-permute-done | bytes 229408 | tf_op jit(solution)/shard_map/ppermute | solution.py:151
  17.3 2.6 %collective-permute-start.12 = (f32[64,896]{1,0:T(8,128)S(1)}, f32[64,896]{1,0:T(8,128)S(1)}, u32[]{:S(2)}, u32[]{:S(2)}) collective-permute-start(f32[64,896]{1,0:T(8,128)S(1)} %pad_maximum_fusion.2.a0), channel_id=1, source_target_pairs={{0,4},{4,0},{8,12},{12,8},{1,5},{5,1},{9,13},{13,9},{2,6},{6,2},{1... | collective-permute-start | bytes 688136 | tf_op jit(solution)/shard_map/ppermute | solution.py:151
  20.0 2.0 %collective-permute-done.8.a2 = f32[64,896]{1,0:T(8,128)S(1)} collective-permute-done((f32[64,896]{1,0:T(8,128)S(1)}, f32[64,896]{1,0:T(8,128)S(1)}, u32[]{:S(2)}, u32[]{:S(2)}) %collective-permute-start.8) | collective-permute-done | bytes 229408 | tf_op jit(solution)/shard_map/ppermute | solution.py:151
  21.9 0.8 %shard_map.47 = (bf16[256,512]{1,0:T(8,128)(2,1)S(1)}, bf16[256,512]{1,0:T(8,128)(2,1)S(1)}, bf16[2,256,128]{2,1,0:T(8,128)(2,1)S(1)}, bf16[2,256,128]{2,1,0:T(8,128)(2,1)S(1)}, f32[2,32,128]{2,1,0:T(8,128)S(1)}) custom-call(s32[6]{0:T(128)S(1)} %stack.31.ids, f32[64,896]{1,0:T(8,128)S(1)} %pad_maximum_fusion.a0, f32[64,896]{1,0:T(8,128)S(1)} %collective-permute-done.3.a1, ...), custom_call_target="tpu_custom_call" | custom-call | flops 1000000000 | bytes 1000 | tf_op jit(solution)/shard_map/pallas_call | solution.py:168
  22.7 0.9 %shard_map.48 = (f32[4,32,128]{2,1,0:T(8,128)S(1)}, f32[4,32,128]{2,1,0:T(8,128)S(1)}) custom-call(s32[2,2]{1,0:T(2,128)S(1)} %bitcast.34, f32[4,32,128]{2,1,0:T(8,128)S(1)} %slice_add_fusion.refs_0_, f32[4,32,128]{2,1,0:T(8,128)S(1)} %collective-permute-done.2.refs_1_, bf16[256,512]{1,0:T(8,128)(2,1)S(1)} %get-tuple-element.49.refs_2_, ...), custom_call_target="tpu_custom_call" | custom-call | flops 4000000000 | bytes 1000 | tf_op jit(solution)/shard_map/pallas_call | solution.py:226
  23.6 2.8 %collective-permute-start.6 = (f32[4,32,128]{2,1,0:T(8,128)S(1)}, f32[4,32,128]{2,1,0:T(8,128)S(1)}, u32[]{:S(2)}, u32[]{:S(2)}) collective-permute-start(f32[4,32,128]{2,1,0:T(8,128)S(1)} %get-tuple-element.55.refs_1_), channel_id=1, source_target_pairs={{0,8},{4,12},{8,0},{12,4},{1,9},{5,13},{9,1},{13,5},{2,10},{6,14},... | collective-permute-start | bytes 196616 | tf_op jit(solution)/shard_map/ppermute | solution.py:151
  26.6 3.9 %collective-permute-done.6.refs_2_ = f32[4,32,128]{2,1,0:T(8,128)S(1)} collective-permute-done((f32[4,32,128]{2,1,0:T(8,128)S(1)}, f32[4,32,128]{2,1,0:T(8,128)S(1)}, u32[]{:S(2)}, u32[]{:S(2)}) %collective-permute-start.6) | collective-permute-done | bytes 65568 | tf_op jit(solution)/shard_map/ppermute | solution.py:151
  30.6 0.8 %shard_map.49 = (bf16[256,512]{1,0:T(8,128)(2,1)S(1)}, bf16[256,512]{1,0:T(8,128)(2,1)S(1)}, bf16[2,256,128]{2,1,0:T(8,128)(2,1)S(1)}, bf16[2,256,128]{2,1,0:T(8,128)(2,1)S(1)}, f32[2,32,128]{2,1,0:T(8,128)S(1)}) custom-call(s32[6]{0:T(128)S(1)} %stack.31.ids, f32[64,896]{1,0:T(8,128)S(1)} %pad_maximum_fusion.1.a0, f32[64,896]{1,0:T(8,128)S(1)} %collective-permute-done.7.a1, ...), custom_call_target="tpu_custom_call" | custom-call | flops 16000000000 | bytes 1000 | tf_op jit(solution)/shard_map/pallas_call | solution.py:168
  31.3 0.9 %shard_map.50 = (f32[8,32,128]{2,1,0:T(8,128)S(1)}, f32[4,32,128]{2,1,0:T(8,128)S(1)}) custom-call(s32[2,2]{1,0:T(2,128)S(1)} %bitcast.33, f32[4,32,128]{2,1,0:T(8,128)S(1)} %get-tuple-element.54.refs_0_, f32[4,32,128]{2,1,0:T(8,128)S(1)} %get-tuple-element.55.refs_1_, f32[4,32,128]{2,1,0:T(8,128)S(1)} %collective-permute-done.6.refs_2_, ...), custom_call_target="tpu_custom_call" | custom-call | flops 1000000000 | bytes 1000 | tf_op jit(solution)/shard_map/pallas_call | solution.py:226
  32.2 1.4 %collective-permute-start.10 = (f32[4,32,128]{2,1,0:T(8,128)S(1)}, f32[4,32,128]{2,1,0:T(8,128)S(1)}, u32[]{:S(2)}, u32[]{:S(2)}) collective-permute-start(f32[4,32,128]{2,1,0:T(8,128)S(1)} %get-tuple-element.64.refs_1_), channel_id=1, source_target_pairs={{0,8},{4,12},{8,0},{12,4},{1,9},{5,13},{9,1},{13,5},{2,10},{6,14},... | collective-permute-start | bytes 196616 | tf_op jit(solution)/shard_map/ppermute | solution.py:151
  33.6 0.8 %shard_map.51 = (bf16[256,512]{1,0:T(8,128)(2,1)S(1)}, bf16[256,512]{1,0:T(8,128)(2,1)S(1)}, bf16[2,256,128]{2,1,0:T(8,128)(2,1)S(1)}, bf16[2,256,128]{2,1,0:T(8,128)(2,1)S(1)}, f32[2,32,128]{2,1,0:T(8,128)S(1)}) custom-call(s32[6]{0:T(128)S(1)} %stack.31.ids, f32[64,896]{1,0:T(8,128)S(1)} %pad_maximum_fusion.2.a0, ...), custom_call_target="tpu_custom_call" | custom-call | flops 16000000000 | bytes 1000 | tf_op jit(solution)/shard_map/pallas_call | solution.py:168
  34.4 4.7 %collective-permute-done.10.refs_2_ = f32[4,32,128]{2,1,0:T(8,128)S(1)} collective-permute-done((f32[4,32,128]{2,1,0:T(8,128)S(1)}, f32[4,32,128]{2,1,0:T(8,128)S(1)}, u32[]{:S(2)}, u32[]{:S(2)}) %collective-permute-start.10) | collective-permute-done | bytes 65568 | tf_op jit(solution)/shard_map/ppermute | solution.py:151
  39.0 0.9 %shard_map.52 = (f32[4,32,128]{2,1,0:T(8,128)S(1)}, f32[4,32,128]{2,1,0:T(8,128)S(1)}, f32[32,128]{1,0:T(8,128)S(1)}, f32[32,128]{1,0:T(8,128)S(1)}) custom-call(s32[6]{0:T(128)S(1)} %stack.31.ids, s32[2,2]{1,0:T(2,128)S(1)} %bitcast.32, f32[8,32,128]{2,1,0:T(8,128)S(1)} %get-tuple-element.63.refs_0_, f32[4,32,128]{2,1,0:T(8,128)S(1)} %get-tuple-element.64.refs_1_, ...), custom_call_target="tpu_custom_call" | custom-call | flops 300000000 | bytes 1000 | tf_op jit(solution)/shard_map/pallas_call | solution.py:242
  40.0 2.8 %collective-permute-start.15 = (f32[32,128]{1,0:T(8,128)S(1)}, f32[32,128]{1,0:T(8,128)S(1)}, u32[]{:S(2)}, u32[]{:S(2)}) collective-permute-start(f32[32,128]{1,0:T(8,128)S(1)} %get-tuple-element.74), channel_id=1, source_target_pairs={{0,8},{4,12},{8,0},{12,4},{1,9},{5,13},{9,1},{13,5},{2,10},{6,14},... | collective-permute-start | bytes 49160 | tf_op jit(solution)/shard_map/ppermute | solution.py:151
  42.8 1.6 %collective-permute-start.16 = (f32[32,128]{1,0:T(8,128)S(1)}, f32[32,128]{1,0:T(8,128)S(1)}, u32[]{:S(2)}, u32[]{:S(2)}) collective-permute-start(f32[32,128]{1,0:T(8,128)S(1)} %get-tuple-element.75), channel_id=1, source_target_pairs={{0,12},{4,8},{8,4},{12,0},{1,13},{5,9},{9,5},{13,1},{2,14},{6,10},... | collective-permute-start | bytes 49160 | tf_op jit(solution)/shard_map/ppermute | solution.py:151
  44.4 0.5 collective-permute-done.15.refs_1_
  44.9 3.5 %collective-permute-done.16.refs_3_ = f32[32,128]{1,0:T(8,128)S(1)} collective-permute-done((f32[32,128]{1,0:T(8,128)S(1)}, f32[32,128]{1,0:T(8,128)S(1)}, u32[]{:S(2)}, u32[]{:S(2)}) %collective-permute-start.16) | collective-permute-done | bytes 16416 | tf_op jit(solution)/shard_map/ppermute | solution.py:151
  48.4 0.5 collective-permute-start.18
  48.9 0.8 %collective-permute-done.18.refs_5_ = f32[32,128]{1,0:T(8,128)S(1)} collective-permute-done((f32[32,128]{1,0:T(8,128)S(1)}, f32[32,128]{1,0:T(8,128)S(1)}, u32[]{:S(2)}, u32[]{:S(2)}) %collective-permute-start.18) | collective-permute-done | bytes 16416 | tf_op jit(solution)/shard_map/ppermute | solution.py:148
  49.7 0.3 collective-permute-done.20.refs_7_
  50.1 1.4 %shard_map.53 = f32[4,64,128]{2,1,0:T(8,128)} custom-call(s32[6]{0:T(128)S(1)} %stack.31.ids, f32[4,32,128]{2,1,0:T(8,128)S(1)} %get-tuple-element.72.refs_0_, f32[32,128]{1,0:T(8,128)S(1)} %collective-permute-done.15.refs_1_, f32[4,32,128]{2,1,0:T(8,128)S(1)} %collective-permute-done.14.refs_2_, f32[32,128]{1,0:T(8,128)S(1)} %collective-permute-done.16.refs_3_, ...), custom_call_target="tpu_custom_call" | custom-call | bytes 1000 | tf_op jit(solution)/shard_map/pallas_call | solution.py:252
  (42 shorter events, 1.1 us)
Async XLA Ops:
  1.7 1.5 %collective-permute-start = (f32[64,640]{1,0:T(8,128)S(1)}, f32[64,640]{1,0:T(8,128)S(1)}, u32[]{:S(2)}, u32[]{:S(2)}) collective-permute-start(f32[64,640]{1,0:T(8,128)S(1)} %pad_maximum_fusion.3.own), channel_id=1, source_target_pairs={{0,1},{1,0},{2,3},{3,2},{4,5},{5,4},{6,7},{7,6},{8,9},{9,8},{10,11... | collective-permute-start | bytes 491528 | tf_op jit(solution)/shard_map/ppermute | solution.py:148
  2.2 0.7 %copy-start.3 = (s32[3,1,2]{0,2,1:T(2,128)S(1)}, s32[3,1,2]{0,2,1:T(2,128)}, u32[]{:S(2)}) copy-start(s32[3,1,2]{0,2,1:T(2,128)} %param.7) | copy-start | bytes 76
  3.2 4.0 %copy-start.2 = (f32[4,64,128]{2,1,0:T(8,128)S(1)}, f32[4,64,128]{2,1,0:T(8,128)}, u32[]{:S(2)}) copy-start(f32[4,64,128]{2,1,0:T(8,128)} %param.4) | copy-start | bytes 393220
  3.2 3.9 %copy-start.1 = (f32[3,64,256]{2,1,0:T(8,128)S(1)}, f32[3,64,256]{2,1,0:T(8,128)}, u32[]{:S(2)}) copy-start(f32[3,64,256]{2,1,0:T(8,128)} %param.6) | copy-start | bytes 589828
  4.1 3.1 %copy-start = (f32[4,64,512]{2,1,0:T(8,128)S(1)}, f32[4,64,512]{2,1,0:T(8,128)}, u32[]{:S(2)}) copy-start(f32[4,64,512]{2,1,0:T(8,128)} %param.5) | copy-start | bytes 1572868
  4.1 5.8 %collective-permute-start.1 = (f32[5,32,128]{2,1,0:T(8,128)S(1)}, f32[5,32,128]{2,1,0:T(8,128)S(1)}, u32[]{:S(2)}, u32[]{:S(2)}) collective-permute-start(f32[5,32,128]{2,1,0:T(8,128)S(1)} %get-tuple-element.42), channel_id=1, source_target_pairs={{0,4},{4,0},{8,12},{12,8},{1,5},{5,1},{9,13},{13,9},{2,6},{6,2},{1... | collective-permute-start | bytes 245768 | tf_op jit(solution)/shard_map/ppermute | solution.py:151
  7.2 14.7 %collective-permute-start.3 = (f32[64,896]{1,0:T(8,128)S(1)}, f32[64,896]{1,0:T(8,128)S(1)}, u32[]{:S(2)}, u32[]{:S(2)}) collective-permute-start(f32[64,896]{1,0:T(8,128)S(1)} %pad_maximum_fusion.a0), channel_id=1, source_target_pairs={{0,1},{1,0},{2,3},{3,2},{4,5},{5,4},{6,7},{7,6},{8,9},{9,8},{10,11... | collective-permute-start | bytes 688136 | tf_op jit(solution)/shard_map/ppermute | solution.py:148
  7.3 9.9 %collective-permute-start.4 = (f32[64,896]{1,0:T(8,128)S(1)}, f32[64,896]{1,0:T(8,128)S(1)}, u32[]{:S(2)}, u32[]{:S(2)}) collective-permute-start(f32[64,896]{1,0:T(8,128)S(1)} %pad_maximum_fusion.a0), channel_id=1, source_target_pairs={{0,4},{4,0},{8,12},{12,8},{1,5},{5,1},{9,13},{13,9},{2,6},{6,2},{1... | collective-permute-start | bytes 688136 | tf_op jit(solution)/shard_map/ppermute | solution.py:151
  9.9 5.6 %collective-permute-start.2 = (f32[4,32,128]{2,1,0:T(8,128)S(1)}, f32[4,32,128]{2,1,0:T(8,128)S(1)}, u32[]{:S(2)}, u32[]{:S(2)}) collective-permute-start(f32[4,32,128]{2,1,0:T(8,128)S(1)} %slice_add_fusion.refs_0_), channel_id=1, source_target_pairs={{0,8},{4,12},{8,0},{12,4},{1,9},{5,13},{9,1},{13,5},{2,10},{6,14},... | collective-permute-start | bytes 196616 | tf_op jit(solution)/shard_map/ppermute | solution.py:151
  12.7 17.8 %collective-permute-start.7 = (f32[64,896]{1,0:T(8,128)S(1)}, f32[64,896]{1,0:T(8,128)S(1)}, u32[]{:S(2)}, u32[]{:S(2)}) collective-permute-start(f32[64,896]{1,0:T(8,128)S(1)} %pad_maximum_fusion.1.a0), channel_id=1, source_target_pairs={{0,1},{1,0},{2,3},{3,2},{4,5},{5,4},{6,7},{7,6},{8,9},{9,8},{10,11... | collective-permute-start | bytes 688136 | tf_op jit(solution)/shard_map/ppermute | solution.py:148
  12.8 9.1 %collective-permute-start.8 = (f32[64,896]{1,0:T(8,128)S(1)}, f32[64,896]{1,0:T(8,128)S(1)}, u32[]{:S(2)}, u32[]{:S(2)}) collective-permute-start(f32[64,896]{1,0:T(8,128)S(1)} %pad_maximum_fusion.1.a0), channel_id=1, source_target_pairs={{0,4},{4,0},{8,12},{12,8},{1,5},{5,1},{9,13},{13,9},{2,6},{6,2},{1... | collective-permute-start | bytes 688136 | tf_op jit(solution)/shard_map/ppermute | solution.py:151
  17.2 4.7 %collective-permute-start.5 = (f32[64,896]{1,0:T(8,128)S(1)}, f32[64,896]{1,0:T(8,128)S(1)}, u32[]{:S(2)}, u32[]{:S(2)}) collective-permute-start(f32[64,896]{1,0:T(8,128)S(1)} %collective-permute-done.4.a2), channel_id=1, source_target_pairs={{0,1},{1,0},{2,3},{3,2},{4,5},{5,4},{6,7},{7,6},{8,9},{9,8},{10,11... | collective-permute-start | bytes 688136 | tf_op jit(solution)/shard_map/ppermute | solution.py:148
  17.3 9.3 %collective-permute-start.12 = (f32[64,896]{1,0:T(8,128)S(1)}, f32[64,896]{1,0:T(8,128)S(1)}, u32[]{:S(2)}, u32[]{:S(2)}) collective-permute-start(f32[64,896]{1,0:T(8,128)S(1)} %pad_maximum_fusion.2.a0), channel_id=1, source_target_pairs={{0,4},{4,0},{8,12},{12,8},{1,5},{5,1},{9,13},{13,9},{2,6},{6,2},{1... | collective-permute-start | bytes 688136 | tf_op jit(solution)/shard_map/ppermute | solution.py:151
  21.9 8.6 %collective-permute-start.9 = (f32[64,896]{1,0:T(8,128)S(1)}, f32[64,896]{1,0:T(8,128)S(1)}, u32[]{:S(2)}, u32[]{:S(2)}) collective-permute-start(f32[64,896]{1,0:T(8,128)S(1)} %collective-permute-done.8.a2), channel_id=1, source_target_pairs={{0,1},{1,0},{2,3},{3,2},{4,5},{5,4},{6,7},{7,6},{8,9},{9,8},{10,11... | collective-permute-start | bytes 688136 | tf_op jit(solution)/shard_map/ppermute | solution.py:148
  23.6 6.9 %collective-permute-start.6 = (f32[4,32,128]{2,1,0:T(8,128)S(1)}, f32[4,32,128]{2,1,0:T(8,128)S(1)}, u32[]{:S(2)}, u32[]{:S(2)}) collective-permute-start(f32[4,32,128]{2,1,0:T(8,128)S(1)} %get-tuple-element.55.refs_1_), channel_id=1, source_target_pairs={{0,8},{4,12},{8,0},{12,4},{1,9},{5,13},{9,1},{13,5},{2,10},{6,14},... | collective-permute-start | bytes 196616 | tf_op jit(solution)/shard_map/ppermute | solution.py:151
  26.4 7.2 %collective-permute-start.11 = (f32[64,896]{1,0:T(8,128)S(1)}, f32[64,896]{1,0:T(8,128)S(1)}, u32[]{:S(2)}, u32[]{:S(2)}) collective-permute-start(f32[64,896]{1,0:T(8,128)S(1)} %pad_maximum_fusion.2.a0), channel_id=1, source_target_pairs={{0,1},{1,0},{2,3},{3,2},{4,5},{5,4},{6,7},{7,6},{8,9},{9,8},{10,11... | collective-permute-start | bytes 688136 | tf_op jit(solution)/shard_map/ppermute | solution.py:148
  30.6 3.0 %collective-permute-start.13 = (f32[64,896]{1,0:T(8,128)S(1)}, f32[64,896]{1,0:T(8,128)S(1)}, u32[]{:S(2)}, u32[]{:S(2)}) collective-permute-start(f32[64,896]{1,0:T(8,128)S(1)} %collective-permute-done.12.a2), channel_id=1, source_target_pairs={{0,1},{1,0},{2,3},{3,2},{4,5},{5,4},{6,7},{7,6},{8,9},{9,8},{10,11... | collective-permute-start | bytes 688136 | tf_op jit(solution)/shard_map/ppermute | solution.py:148
  32.2 6.8 %collective-permute-start.10 = (f32[4,32,128]{2,1,0:T(8,128)S(1)}, f32[4,32,128]{2,1,0:T(8,128)S(1)}, u32[]{:S(2)}, u32[]{:S(2)}) collective-permute-start(f32[4,32,128]{2,1,0:T(8,128)S(1)} %get-tuple-element.64.refs_1_), channel_id=1, source_target_pairs={{0,8},{4,12},{8,0},{12,4},{1,9},{5,13},{9,1},{13,5},{2,10},{6,14},... | collective-permute-start | bytes 196616 | tf_op jit(solution)/shard_map/ppermute | solution.py:151
  40.0 8.4 %collective-permute-start.14 = (f32[4,32,128]{2,1,0:T(8,128)S(1)}, f32[4,32,128]{2,1,0:T(8,128)S(1)}, u32[]{:S(2)}, u32[]{:S(2)}) collective-permute-start(f32[4,32,128]{2,1,0:T(8,128)S(1)} %get-tuple-element.73), channel_id=1, source_target_pairs={{0,4},{4,0},{8,12},{12,8},{1,5},{5,1},{9,13},{13,9},{2,6},{6,2},{1... | collective-permute-start | bytes 196616 | tf_op jit(solution)/shard_map/ppermute | solution.py:151
  40.0 4.9 %collective-permute-start.15 = (f32[32,128]{1,0:T(8,128)S(1)}, f32[32,128]{1,0:T(8,128)S(1)}, u32[]{:S(2)}, u32[]{:S(2)}) collective-permute-start(f32[32,128]{1,0:T(8,128)S(1)} %get-tuple-element.74), channel_id=1, source_target_pairs={{0,8},{4,12},{8,0},{12,4},{1,9},{5,13},{9,1},{13,5},{2,10},{6,14},... | collective-permute-start | bytes 49160 | tf_op jit(solution)/shard_map/ppermute | solution.py:151
  42.8 5.5 %collective-permute-start.16 = (f32[32,128]{1,0:T(8,128)S(1)}, f32[32,128]{1,0:T(8,128)S(1)}, u32[]{:S(2)}, u32[]{:S(2)}) collective-permute-start(f32[32,128]{1,0:T(8,128)S(1)} %get-tuple-element.75), channel_id=1, source_target_pairs={{0,12},{4,8},{8,4},{12,0},{1,13},{5,9},{9,5},{13,1},{2,14},{6,10},... | collective-permute-start | bytes 49160 | tf_op jit(solution)/shard_map/ppermute | solution.py:151
  44.4 4.5 %collective-permute-start.17 = (f32[4,32,128]{2,1,0:T(8,128)S(1)}, f32[4,32,128]{2,1,0:T(8,128)S(1)}, u32[]{:S(2)}, u32[]{:S(2)}) collective-permute-start(f32[4,32,128]{2,1,0:T(8,128)S(1)} %get-tuple-element.72.refs_0_), channel_id=1, source_target_pairs={{0,1},{1,0},{2,3},{3,2},{4,5},{5,4},{6,7},{7,6},{8,9},{9,8},{10,11... | collective-permute-start | bytes 196616 | tf_op jit(solution)/shard_map/ppermute | solution.py:148
  48.4 1.7 %collective-permute-start.19 = (f32[4,32,128]{2,1,0:T(8,128)S(1)}, f32[4,32,128]{2,1,0:T(8,128)S(1)}, u32[]{:S(2)}, u32[]{:S(2)}) collective-permute-start(f32[4,32,128]{2,1,0:T(8,128)S(1)} %collective-permute-done.14.refs_2_), channel_id=1, source_target_pairs={{0,1},{1,0},{2,3},{3,2},{4,5},{5,4},{6,7},{7,6},{8,9},{9,8},{10,11... | collective-permute-start | bytes 196616 | tf_op jit(solution)/shard_map/ppermute | solution.py:148
  48.4 1.3 %collective-permute-start.18 = (f32[32,128]{1,0:T(8,128)S(1)}, f32[32,128]{1,0:T(8,128)S(1)}, u32[]{:S(2)}, u32[]{:S(2)}) collective-permute-start(f32[32,128]{1,0:T(8,128)S(1)} %collective-permute-done.15.refs_1_), channel_id=1, source_target_pairs={{0,1},{1,0},{2,3},{3,2},{4,5},{5,4},{6,7},{7,6},{8,9},{9,8},{10,11... | collective-permute-start | bytes 49160 | tf_op jit(solution)/shard_map/ppermute | solution.py:148
  48.9 1.2 %collective-permute-start.20 = (f32[32,128]{1,0:T(8,128)S(1)}, f32[32,128]{1,0:T(8,128)S(1)}, u32[]{:S(2)}, u32[]{:S(2)}) collective-permute-start(f32[32,128]{1,0:T(8,128)S(1)} %collective-permute-done.16.refs_3_), channel_id=1, source_target_pairs={{0,1},{1,0},{2,3},{3,2},{4,5},{5,4},{6,7},{7,6},{8,9},{9,8},{10,11... | collective-permute-start | bytes 49160 | tf_op jit(solution)/shard_map/ppermute | solution.py:148

commit v3 on v2

v3 whole, which is shorter than its diff:
```python
import functools

import jax
import jax.numpy as jnp
from jax import lax
from jax.experimental import pallas as pl
from jax.experimental.pallas import tpu as pltpu
from jax.sharding import PartitionSpec as P

K = {'first': 0.3, 'prep': [2, 0, 0], 'step': [0, 0.1, 0], 'bulk': ['send', 'share0', 'share0'], 'swap': ['recv0', 'share1', 'share2'], 'rest': ['send', 'send', 'send'], 'groups': [[1], [2], [3]], 'meet': 1, 'early': 2, 'cut': [4, 4, 2]}
S = 4
BS = 128
LANES = 128
VMEM = pl.BlockSpec(memory_space=pltpu.VMEM)
SMEM = pl.BlockSpec(memory_space=pltpu.SMEM)


def split(a):
    high = a.astype(jnp.bfloat16)
    return high, (a - high.astype(jnp.float32)).astype(jnp.bfloat16)


def dot(a, b):
    return jnp.dot(a, b, preferred_element_type=jnp.float32)


def product(a, b_high, b_low):
    a_high, a_low = split(a)
    rows = a.shape[0]
    both = dot(jnp.concatenate([a_high, a_low], axis=0), b_high)
    return both[:rows] + both[rows:] + dot(a_high, b_low)


def call(kernel, outs, scratch=(), cost=0):
    return functools.partial(
        pl.pallas_call,
        kernel,
        out_shape=outs,
        scratch_shapes=list(scratch),
        compiler_params=pltpu.CompilerParams(vmem_limit_bytes=40 * 1024 * 1024),
        cost_estimate=pl.CostEstimate(flops=int(cost * 1e9), bytes_accessed=1000, transcendentals=0),
    )


def first_kernel(quarter, ids, lists, own, other, own_sides, other_sides, keep, send, turned, terms):
    blocks = own.shape[1] // BS
    turned[...] = jnp.concatenate([own_sides[0], other_sides[0]], axis=0).T
    sides = turned[pl.ds(pl.multiple_of(ids[0] * 2 * quarter, 2 * quarter), 2 * quarter), :]
    high, low = split(jnp.concatenate([own[...], other[...]], axis=0))
    share = product(sides, high, low)
    for i in range(blocks):
        terms[i] = share[:, i * BS : (i + 1) * BS]
    keep[...] = terms[:, pl.ds(pl.multiple_of(ids[1] * quarter, quarter), quarter), :]
    send[:blocks] = terms[:, pl.ds(pl.multiple_of((1 - ids[1]) * quarter, quarter), quarter), :]
    lane = lax.broadcasted_iota(jnp.int32, (quarter, BS), 1)
    told = jnp.zeros((quarter, BS), jnp.float32)
    for i in range(lists.shape[0]):
        for k in range(lists.shape[2]):
            told = jnp.where(lane == i * lists.shape[2] + k, lists[i, 0, k].astype(jnp.float32), told)
    send[blocks] = told


def prepare_kernel(quarter, place, ids, a0, a1, a2, *refs):
    a3 = jnp.concatenate([a[...] for a in refs[:-6]], axis=0)
    diag_high, diag_low, below_high, below_low, sides, turned = refs[-6:]
    width = diag_high.shape[1]
    depth = below_high.shape[1]
    first = pl.multiple_of(ids[0] * 2 * quarter + ids[1] * quarter, quarter)
    mine = slice(place * BS // 2, (place + 1) * BS // 2)
    for j, (one, two) in enumerate(((a0, a1), (a2, a3))):
        high, low = split(jnp.concatenate([one[mine, :width], two[mine, :width]], axis=0))
        diag_high[j * BS : (j + 1) * BS, :] = high
        diag_low[j * BS : (j + 1) * BS, :] = low
        below = jnp.concatenate([one[mine, width : width + depth], two[mine, width : width + depth]], axis=0)
        high, low = split(below.T)
        below_high[j] = high
        below_low[j] = low
        turned[...] = jnp.concatenate([one[mine, width + depth :], two[mine, width + depth :]], axis=0).T
        sides[j] = turned[pl.ds(first, quarter), :]


def advance(t, lists, told, stored, refs, solved):
    keep, recv, diag_high, diag_low, below_high, below_low, sides = refs
    before = solved.shape[0] - keep.shape[0]
    if before:
        solved[:before] = stored[0][...]
    solved[before:] = keep[...] + recv[...]
    listed = lists.shape[2]
    residuals = []
    for j in range(2):
        wanted = [told[t - 1, k] if j else lists[t - 1, 0, k] for k in range(listed)]
        picked = jnp.concatenate([solved[i] for i in wanted], axis=1)
        residuals.append(sides[j] - product(picked, below_high[j], below_low[j]))
    return product(jnp.concatenate(residuals, axis=1), diag_high[...], diag_low[...])


def step_kernel(t, lists, told, *refs):
    solved, share = refs[-2:]
    result = advance(t, lists, told, refs[:-9], refs[-9:-2], solved)
    for i in range(share.shape[0]):
        share[i] = result[:, i * BS : (i + 1) * BS]


def early_kernel(ids, solved, own, near):
    blocks = solved.shape[0] // own.shape[0]
    for t in range(own.shape[0]):
        own[t] = solved[t * blocks + ids[2]]
        near[t] = solved[t * blocks + ids[3]]


def give(first, ids, solved, share, own, near, far, both):
    blocks = share.shape[0]
    for t in range(first, S - 1):
        own[t - first] = solved[t * blocks + ids[2]]
        near[t - first] = solved[t * blocks + ids[3]]
    own[S - 1 - first] = share[ids[2]]
    near[S - 1 - first] = share[ids[3]]
    far[...] = share[ids[4]]
    both[...] = share[ids[5]]


def last_kernel(first, ids, lists, told, *refs):
    own, near, far, both, solved, share = refs[-6:]
    result = advance(S - 1, lists, told, refs[:-13], refs[-13:-6], solved)
    for i in range(share.shape[0]):
        share[i] = result[:, i * BS : (i + 1) * BS]
    give(first, ids, solved, share, own, near, far, both)


def place(quarter, ids, parts, whole):
    core, half = ids[0], ids[1]
    places = ((core, half), (core, 1 - half), (1 - core, half), (1 - core, 1 - half))
    for part, (c, h) in zip(parts, places):
        whole[pl.ds(pl.multiple_of((2 * c + h) * quarter, quarter), quarter), :] = part
    rows = whole.shape[1] // 2
    return jnp.where(core == 0, whole[:, :rows], whole[:, rows:]).T


def place_early_kernel(quarter, ids, a0, a1, a2, a3, out, whole):
    for t in range(out.shape[0]):
        out[t] = place(quarter, ids, (a0[t], a1[t], a2[t], a3[t]), whole)


def place_kernel(quarter, first, ids, *refs):
    quarters, out, whole = refs[:8], refs[-2], refs[-1]
    if first:
        out[:first] = refs[8][...]
    for t in range(first, S):
        parts = [quarters[2 * i][t - first] for i in range(4)]
        if t == S - 1:
            parts = [part + quarters[2 * i + 1][...] for i, part in enumerate(parts)]
        out[t] = place(quarter, ids, parts, whole)


def body(count, right_sides, diag_inverse, factor_below, block_lists):
    quarter = right_sides.shape[2] // 4
    blocks = diag_inverse.shape[2] // BS
    width = diag_inverse.shape[2]
    depth = factor_below.shape[2]
    listed = block_lists.shape[2]
    top = count // 2
    row, core = lax.axis_index("row"), lax.axis_index("sub")
    half = lax.rem(row, 2)
    team = row + 1 - 2 * half
    far = lax.rem(row + top, count)
    ids = jnp.stack([core, half, row, team, far, far + 1 - 2 * half]).astype(jnp.int32)

    def to_core(a):
        return lax.ppermute(a, "sub", [(0, 1), (1, 0)])

    def to_row(a, bit):
        return lax.ppermute(a, "row", [(i, i ^ bit) for i in range(count)])

    def after(a, *others):
        return lax.optimization_barrier((a, *others))[0]

    f32, bf16 = jnp.float32, jnp.bfloat16
    shape = jax.ShapeDtypeStruct
    piece = shape((blocks, quarter, BS), f32)

    def total(a):
        bit = 2
        while bit < top:
            a = a + to_row(a, bit)
            bit *= 2
        return a, to_row(a, top)

    def prepare(t, place, own, own_core, other, other_core):
        return call(
            functools.partial(prepare_kernel, quarter, place),
            (
                shape((2 * BS, width), bf16),
                shape((2 * BS, width), bf16),
                shape((2, depth, BS), bf16),
                shape((2, depth, BS), bf16),
                shape((2, quarter, BS), f32),
            ),
            [pltpu.VMEM((4 * quarter, BS), f32)],
            K["prep"][t - 1],
        )(in_specs=[SMEM] + [VMEM] * (3 + len(other_core)))(ids, own, own_core, other, *other_core)

    diag_first = diag_inverse[0]
    keep, send = call(
        functools.partial(first_kernel, quarter),
        (piece, shape((blocks + 1, quarter, BS), f32)),
        [pltpu.VMEM((4 * quarter, BS), f32), pltpu.VMEM((blocks, 2 * quarter, BS), f32)],
        K["first"],
    )(in_specs=[SMEM, SMEM, VMEM, VMEM, VMEM, VMEM])(
        ids, block_lists, diag_first, to_core(diag_first), right_sides, to_core(right_sides)
    )
    got = to_row(send, 1)

    groups = K["groups"]
    rest = []
    for g, group in enumerate(groups):
        diag, below, sides, _ = lax.optimization_barrier(
            (diag_inverse, factor_below, right_sides, {"first": diag_first, "send": send}[K["rest"][g]])
        )
        rows = [jnp.concatenate([diag[t], below[t - 1], sides[t]], axis=1) for t in group]
        rest.append(jnp.concatenate(rows, axis=0))
    rest_core = [to_core(a) for a in rest]

    share = keep + got[:blocks]
    told = got[blocks, 0, : (S - 1) * listed].reshape(S - 1, listed).astype(jnp.int32)

    gates = {"none": None, "send": send, "share0": share, "core1": rest_core[0]}
    stored, first = (), K["early"]
    others, other_cores = {}, {}

    def bulk():
        for u, name in enumerate(K["bulk"][: len(groups)]):
            if u not in others and name in gates:
                g = gates[name]
                others[u] = to_row(after(rest[u], g) if g is not None else rest[u], 1)

    for t in range(1, S):
        bulk()
        keep, recv = total(share)
        gates[f"recv{t - 1}"] = recv
        bulk()
        u = [t in group for group in groups].index(True)
        if u not in other_cores:
            g = K["swap"][u]
            gated = after(others[u], gates[g]) if g else others[u]
            rows = gated.shape[0] // K["cut"][u]
            other_cores[u] = [to_core(gated[i : i + rows]) for i in range(0, gated.shape[0], rows)]
        gates[f"other{t}"] = other_cores[u][-1]
        bulk()
        ready = prepare(t, groups[u].index(t), rest[u], rest_core[u], others[u], other_cores[u])
        operands = (*stored, keep, recv, *ready)
        gates[f"prep{t}"] = operands[-1]
        bulk()
        solved_shape = shape((t * blocks, quarter, BS), f32)
        if t < S - 1 or top > 2:
            solved, share = call(
                functools.partial(step_kernel, t), (solved_shape, piece), (), K["step"][t - 1]
            )(in_specs=[SMEM, SMEM] + [VMEM] * len(operands))(block_lists, told, *operands)
            stored = (solved,)
            gates[f"share{t}"] = share
            if t == S - 2 and first:
                early = shape((first, quarter, BS), f32)
                own, near = call(early_kernel, (early, early))(in_specs=[SMEM, VMEM])(ids, solved)
                near = to_row(near, 1)
                placed = call(
                    functools.partial(place_early_kernel, quarter),
                    shape((first, BS // 2, 4 * quarter), f32),
                    [pltpu.VMEM((4 * quarter, BS), f32)],
                )(in_specs=[SMEM] + [VMEM] * 4)(ids, own, near, to_core(own), to_core(near))

    block = shape((quarter, BS), f32)
    kept = shape((S - first, quarter, BS), f32)
    gifts = (kept, kept, block, block)
    if top > 2:
        bit = 2
        while bit < top:
            share = share + to_row(share, bit)
            bit *= 2
        own, *sent = call(functools.partial(give, first), gifts)(in_specs=[SMEM, VMEM, VMEM])(ids, solved, share)
    else:
        own, *sent = call(
            functools.partial(last_kernel, first),
            gifts,
            [pltpu.VMEM(solved_shape.shape, f32), pltpu.VMEM(piece.shape, f32)],
            K["step"][S - 2],
        )(in_specs=[SMEM] * 3 + [VMEM] * len(operands))(ids, block_lists, told, *operands)
    near, far, both = [to_row(a, bit) for a, bit in zip(sent, (1, top, top + 1))]
    if K["meet"]:
        near, far, both = lax.optimization_barrier((near, far, both))
    quarters = [own, far, near, both]
    quarters += [to_core(a) for a in quarters]
    if first:
        quarters.append(placed)
    return call(
        functools.partial(place_kernel, quarter, first),
        shape((S, BS // 2, 4 * quarter), f32),
        [pltpu.VMEM((4 * quarter, BS), f32)],
    )(in_specs=[SMEM] + [VMEM] * len(quarters))(ids, *quarters)


def solution(mesh):
    in_specs = (
        P("grp", ("row", "sub"), "rhs"),
        P("grp", ("row", "sub"), None),
        P("grp", ("row", "sub"), None),
        P("grp", "row", None),
    )
    out_specs = P("grp", ("row", "sub"), "rhs")
    step = functools.partial(body, mesh.shape["row"])
    return jax.shard_map(step, mesh=mesh, in_specs=in_specs, out_specs=out_specs, check_vma=False)
```

time: 51.7 us -> 48 us (0.928)
  waiting for transfers between devices: 19.7 us -> 12.2 us
  starting transfers between devices: 21.5 us -> 24.8 us
  Pallas kernels: 7.24 us -> 8.57 us
  local copies, waits for them, and re-layouts: 2.77 us -> 2.01 us
    ppermute x10 -> x11, waiting for transfers between devices: 18.4 us -> 10.3 us  [to_row(): return lax.ppermute(a, 'row', [(i, i ^ bit) for i in range(count)])]
    ppermute x11 -> x21, starting transfers between devices: 1.41 us -> 4.53 us  [to_core(): return lax.ppermute(a, 'sub', [(0, 1), (1, 0)])]
    pallas_call x7 -> x9, Pallas kernels: 6.39 us -> 7.72 us  [the longest x3 2.31 us: prepare(): call(functools.partial(prepare_kernel, quarter, place), (shape((2 * BS, w...]
    squeeze x3 -> x1, local copies, waits for them, and re-layouts: 1.76 us -> 0.95 us  [body(): diag_first = diag_inverse[0]]
    ppermute x11 -> x21, waiting for transfers between devices: 1.28 us -> 1.91 us  [to_core(): return lax.ppermute(a, 'sub', [(0, 1), (1, 0)])]
    ppermute x10 -> x11, starting transfers between devices: 20.1 us -> 20.2 us  [to_row(): return lax.ppermute(a, 'row', [(i, i ^ bit) for i in range(count)])]
  transfers between devices with their start and end apart: 21 -> 32, of which waited for: 11 -> 13; matrix products, arithmetic and copies ran while one was open for 1% -> 1% of each run, Pallas kernels for 8% -> 13%
where the time goes in v3:
time: 48 us; the launch traced here: 47.9 us
  starting transfers between devices  24.8 us (52%)
  waiting for transfers between devices  12.2 us (25%)
  Pallas kernels  8.57 us (18%)
  local copies, waits for them, and re-layouts  2.01 us (4%)
    ppermute x11, starting transfers between devices, to_row(): return lax.ppermute(a, 'row', [(i, i ^ bit) for i in range(count)])  20.2 us
    ppermute x11, waiting for transfers between devices, to_row(): return lax.ppermute(a, 'row', [(i, i ^ bit) for i in range(count)])  10.3 us
    ppermute x21, starting transfers between devices, to_core(): return lax.ppermute(a, 'sub', [(0, 1), (1, 0)])  4.53 us
    pallas_call x3, Pallas kernels, prepare(): call(functools.partial(prepare_kernel, quarter, place), (shape((2 * BS, w...  2.31 us
    ppermute x21, waiting for transfers between devices, to_core(): return lax.ppermute(a, 'sub', [(0, 1), (1, 0)])  1.91 us
    pallas_call x2, Pallas kernels, body(): call(functools.partial(step_kernel, t), (solved_shape, piece), (), K['ste...  1.83 us
    pallas_call x1, Pallas kernels, body(): call(functools.partial(place_kernel, quarter, first), shape((S, BS // 2,...  1.38 us
  transfers between devices with their start and end apart: 32, of which 13 were waited for; matrix products, arithmetic and copies ran while one was open for 1% of the time, Pallas kernels for 13%

profile of v3, /device:TPU:0, one launch (start us, length us, event | category | flops | bytes accessed | tf_op | source)
XLA Modules:
  0.0 47.9 jit_solution(7833685330847468212)
XLA Ops:
  0.0 0.9 %slice_bitcast_fusion.3.own = f32[64,512]{1,0:T(8,128)S(1)} fusion(f32[4,64,512]{2,1,0:T(8,128)} %param.5), kind=kLoop, calls=%fused_computation.6 | loop fusion | bytes 262144 | tf_op jit(solution)/shard_map/squeeze | solution.py:202
  1.0 0.5 %collective-permute-start = (f32[64,512]{1,0:T(8,128)S(1)}, f32[64,512]{1,0:T(8,128)S(1)}, u32[]{:S(2)}, u32[]{:S(2)}) collective-permute-start(f32[64,512]{1,0:T(8,128)S(1)} %slice_bitcast_fusion.3.own), channel_id=1, source_target_pairs={{0,1},{1,0},{2,3},{3,2},{4,5},{5,4},{6,7},{7,6},{8,9},{9,8},{10,11... | collective-permute-start | bytes 393224 | tf_op jit(solution)/shard_map/ppermute | solution.py:169
  1.6 0.7 %copy-done.3 = s32[3,1,2]{0,2,1:T(2,128)S(1)} copy-done((s32[3,1,2]{0,2,1:T(2,128)S(1)}, s32[3,1,2]{0,2,1:T(2,128)}, u32[]{:S(2)}) %copy-start.3) | copy-done | bytes 48
  2.8 0.8 %shard_map.46 = (f32[4,32,128]{2,1,0:T(8,128)S(1)}, f32[5,32,128]{2,1,0:T(8,128)S(1)}) custom-call(s32[6]{0:T(128)S(1)} %stack.27.ids, s32[3,1,2]{2,1,0:T(1,128)S(1)} %copy.12.lists, f32[64,512]{1,0:T(8,128)S(1)} %slice_bitcast_fusion.3.own, f32[64,512]{1,0:T(8,128)S(1)} %collective-permute-done.other, f32[4,64,128]{2,1,0:T(8,128)S(1)} %copy-done, ...), custom_call_target="tpu_custom_call" | custom-call | flops 300000000 | bytes 1000 | tf_op jit(solution)/shard_map/pallas_call | solution.py:203
  3.7 2.8 %collective-permute-start.2 = (f32[5,32,128]{2,1,0:T(8,128)S(1)}, f32[5,32,128]{2,1,0:T(8,128)S(1)}, u32[]{:S(2)}, u32[]{:S(2)}) collective-permute-start(f32[5,32,128]{2,1,0:T(8,128)S(1)} %get-tuple-element.44), channel_id=1, source_target_pairs={{0,4},{4,0},{8,12},{12,8},{1,5},{5,1},{9,13},{13,9},{2,6},{6,2},{1... | collective-permute-start | bytes 245768 | tf_op jit(solution)/shard_map/ppermute | solution.py:172
  6.7 1.2 %collective-permute-start.5 = (f32[64,896]{1,0:T(8,128)S(1)}, f32[64,896]{1,0:T(8,128)S(1)}, u32[]{:S(2)}, u32[]{:S(2)}) collective-permute-start(f32[64,896]{1,0:T(8,128)S(1)} %pad_maximum_fusion.a0), channel_id=1, source_target_pairs={{0,4},{4,0},{8,12},{12,8},{1,5},{5,1},{9,13},{13,9},{2,6},{6,2},{1... | collective-permute-start | bytes 688136 | tf_op jit(solution)/shard_map/ppermute | solution.py:172
  8.0 1.5 %collective-permute-done.2 = f32[5,32,128]{2,1,0:T(8,128)S(1)} collective-permute-done((f32[5,32,128]{2,1,0:T(8,128)S(1)}, f32[5,32,128]{2,1,0:T(8,128)S(1)}, u32[]{:S(2)}, u32[]{:S(2)}) %collective-permute-start.2) | collective-permute-done | bytes 81952 | tf_op jit(solution)/shard_map/ppermute | solution.py:172
  9.5 2.8 %collective-permute-start.3 = (f32[4,32,128]{2,1,0:T(8,128)S(1)}, f32[4,32,128]{2,1,0:T(8,128)S(1)}, u32[]{:S(2)}, u32[]{:S(2)}) collective-permute-start(f32[4,32,128]{2,1,0:T(8,128)S(1)} %slice_add_fusion.refs_0_), channel_id=1, source_target_pairs={{0,8},{4,12},{8,0},{12,4},{1,9},{5,13},{9,1},{13,5},{2,10},{6,14},... | collective-permute-start | bytes 196616 | tf_op jit(solution)/shard_map/ppermute | solution.py:172
  12.3 2.2 %collective-permute-start.12 = (f32[64,896]{1,0:T(8,128)S(1)}, f32[64,896]{1,0:T(8,128)S(1)}, u32[]{:S(2)}, u32[]{:S(2)}) collective-permute-start(f32[64,896]{1,0:T(8,128)S(1)} %pad_maximum_fusion.1.a0), channel_id=1, source_target_pairs={{0,4},{4,0},{8,12},{12,8},{1,5},{5,1},{9,13},{13,9},{2,6},{6,2},{1... | collective-permute-start | bytes 688136 | tf_op jit(solution)/shard_map/ppermute | solution.py:172
  14.5 1.1 %collective-permute-done.3.refs_1_ = f32[4,32,128]{2,1,0:T(8,128)S(1)} collective-permute-done((f32[4,32,128]{2,1,0:T(8,128)S(1)}, f32[4,32,128]{2,1,0:T(8,128)S(1)}, u32[]{:S(2)}, u32[]{:S(2)}) %collective-permute-start.3) | collective-permute-done | bytes 65568 | tf_op jit(solution)/shard_map/ppermute | solution.py:172
  15.6 1.0 %collective-permute-done.5.a2 = f32[64,896]{1,0:T(8,128)S(1)} collective-permute-done((f32[64,896]{1,0:T(8,128)S(1)}, f32[64,896]{1,0:T(8,128)S(1)}, u32[]{:S(2)}, u32[]{:S(2)}) %collective-permute-start.5) | collective-permute-done | bytes 229408 | tf_op jit(solution)/shard_map/ppermute | solution.py:172
  18.1 2.6 %collective-permute-start.19 = (f32[64,896]{1,0:T(8,128)S(1)}, f32[64,896]{1,0:T(8,128)S(1)}, u32[]{:S(2)}, u32[]{:S(2)}) collective-permute-start(f32[64,896]{1,0:T(8,128)S(1)} %pad_maximum_fusion.2.a0), channel_id=1, source_target_pairs={{0,4},{4,0},{8,12},{12,8},{1,5},{5,1},{9,13},{13,9},{2,6},{6,2},{1... | collective-permute-start | bytes 688136 | tf_op jit(solution)/shard_map/ppermute | solution.py:172
  20.7 0.8 %shard_map.47 = (bf16[256,512]{1,0:T(8,128)(2,1)S(1)}, bf16[256,512]{1,0:T(8,128)(2,1)S(1)}, bf16[2,256,128]{2,1,0:T(8,128)(2,1)S(1)}, bf16[2,256,128]{2,1,0:T(8,128)(2,1)S(1)}, f32[2,32,128]{2,1,0:T(8,128)S(1)}) custom-call(s32[6]{0:T(128)S(1)} %stack.27.ids, f32[64,896]{1,0:T(8,128)S(1)} %pad_maximum_fusion.a0, f32[64,896]{1,0:T(8,128)S(1)} %collective-permute-done.4.a1, ...), custom_call_target="tpu_custom_call" | custom-call | flops 2000000000 | bytes 1000 | tf_op jit(solution)/shard_map/pallas_call | solution.py:189
  21.4 0.9 %shard_map.48 = (f32[4,32,128]{2,1,0:T(8,128)S(1)}, f32[4,32,128]{2,1,0:T(8,128)S(1)}) custom-call(s32[3,1,2]{2,1,0:T(1,128)S(1)} %copy.12.lists, s32[3,2]{1,0:T(4,128)S(1)} %convert_element_type.6.told, f32[4,32,128]{2,1,0:T(8,128)S(1)} %slice_add_fusion.refs_0_, f32[4,32,128]{2,1,0:T(8,128)S(1)} %collective-permute-done.3.refs_1_, ...), custom_call_target="tpu_custom_call" | custom-call | bytes 1000 | tf_op jit(solution)/shard_map/pallas_call | solution.py:255
  22.5 1.5 %collective-permute-start.10 = (f32[4,32,128]{2,1,0:T(8,128)S(1)}, f32[4,32,128]{2,1,0:T(8,128)S(1)}, u32[]{:S(2)}, u32[]{:S(2)}) collective-permute-start(f32[4,32,128]{2,1,0:T(8,128)S(1)} %get-tuple-element.57.refs_1_), channel_id=1, source_target_pairs={{0,8},{4,12},{8,0},{12,4},{1,9},{5,13},{9,1},{13,5},{2,10},{6,14},... | collective-permute-start | bytes 196616 | tf_op jit(solution)/shard_map/ppermute | solution.py:172
  24.7 0.6 %collective-permute-done.15.refs_2_ = f32[16,896]{1,0:T(8,128)S(1)} collective-permute-done((f32[16,896]{1,0:T(8,128)S(1)}, f32[16,896]{1,0:T(8,128)S(1)}, u32[]{:S(2)}, u32[]{:S(2)}) %collective-permute-start.15) | collective-permute-done | bytes 57376 | tf_op jit(solution)/shard_map/ppermute | solution.py:169
  25.8 0.8 %shard_map.49 = (bf16[256,512]{1,0:T(8,128)(2,1)S(1)}, bf16[256,512]{1,0:T(8,128)(2,1)S(1)}, bf16[2,256,128]{2,1,0:T(8,128)(2,1)S(1)}, bf16[2,256,128]{2,1,0:T(8,128)(2,1)S(1)}, f32[2,32,128]{2,1,0:T(8,128)S(1)}) custom-call(s32[6]{0:T(128)S(1)} %stack.27.ids, f32[64,896]{1,0:T(8,128)S(1)} %pad_maximum_fusion.1.a0, ...), custom_call_target="tpu_custom_call" | custom-call | bytes 1000 | tf_op jit(solution)/shard_map/pallas_call | solution.py:189
  26.5 1.7 %collective-permute-done.10.refs_2_ = f32[4,32,128]{2,1,0:T(8,128)S(1)} collective-permute-done((f32[4,32,128]{2,1,0:T(8,128)S(1)}, f32[4,32,128]{2,1,0:T(8,128)S(1)}, u32[]{:S(2)}, u32[]{:S(2)}) %collective-permute-start.10) | collective-permute-done | bytes 65568 | tf_op jit(solution)/shard_map/ppermute | solution.py:172
  28.2 0.9 %shard_map.50 = (f32[8,32,128]{2,1,0:T(8,128)S(1)}, f32[4,32,128]{2,1,0:T(8,128)S(1)}) custom-call(s32[3,1,2]{2,1,0:T(1,128)S(1)} %copy.12.lists, s32[3,2]{1,0:T(4,128)S(1)} %convert_element_type.6.told, f32[4,32,128]{2,1,0:T(8,128)S(1)} %get-tuple-element.56.refs_0_, f32[4,32,128]{2,1,0:T(8,128)S(1)} %get-tuple-element.57.refs_1_, ...), custom_call_target="tpu_custom_call" | custom-call | flops 100000000 | bytes 1000 | tf_op jit(solution)/shard_map/pallas_call | solution.py:255
  29.7 2.6 %collective-permute-start.17 = (f32[4,32,128]{2,1,0:T(8,128)S(1)}, f32[4,32,128]{2,1,0:T(8,128)S(1)}, u32[]{:S(2)}, u32[]{:S(2)}) collective-permute-start(f32[4,32,128]{2,1,0:T(8,128)S(1)} %get-tuple-element.66.refs_1_), channel_id=1, source_target_pairs={{0,8},{4,12},{8,0},{12,4},{1,9},{5,13},{9,1},{13,5},{2,10},{6,14},... | collective-permute-start | bytes 196616 | tf_op jit(solution)/shard_map/ppermute | solution.py:172
  32.4 0.5 %shard_map.53 = (f32[2,32,128]{2,1,0:T(8,128)S(1)}, f32[2,32,128]{2,1,0:T(8,128)S(1)}) custom-call(s32[6]{0:T(128)S(1)} %stack.27.ids, f32[8,32,128]{2,1,0:T(8,128)S(1)} %get-tuple-element.65.refs_0_.solved), custom_call_target="tpu_custom_call" | custom-call | bytes 1000 | tf_op jit(solution)/shard_map/pallas_call | solution.py:262
  33.0 0.8 %shard_map.51 = (bf16[256,512]{1,0:T(8,128)(2,1)S(1)}, bf16[256,512]{1,0:T(8,128)(2,1)S(1)}, bf16[2,256,128]{2,1,0:T(8,128)(2,1)S(1)}, bf16[2,256,128]{2,1,0:T(8,128)(2,1)S(1)}, f32[2,32,128]{2,1,0:T(8,128)S(1)}) custom-call(s32[6]{0:T(128)S(1)} %stack.27.ids, f32[64,896]{1,0:T(8,128)S(1)} %pad_maximum_fusion.2.a0, ...), custom_call_target="tpu_custom_call" | custom-call | bytes 1000 | tf_op jit(solution)/shard_map/pallas_call | solution.py:189
  33.8 2.5 %collective-permute-done.17.refs_2_ = f32[4,32,128]{2,1,0:T(8,128)S(1)} collective-permute-done((f32[4,32,128]{2,1,0:T(8,128)S(1)}, f32[4,32,128]{2,1,0:T(8,128)S(1)}, u32[]{:S(2)}, u32[]{:S(2)}) %collective-permute-start.17) | collective-permute-done | bytes 65568 | tf_op jit(solution)/shard_map/ppermute | solution.py:172
  36.3 0.9 %shard_map.52 = (f32[2,32,128]{2,1,0:T(8,128)S(1)}, f32[2,32,128]{2,1,0:T(8,128)S(1)}, f32[32,128]{1,0:T(8,128)S(1)}, f32[32,128]{1,0:T(8,128)S(1)}) custom-call(s32[6]{0:T(128)S(1)} %stack.27.ids, s32[3,1,2]{2,1,0:T(1,128)S(1)} %copy.12.lists, s32[3,2]{1,0:T(4,128)S(1)} %convert_element_type.6.told, f32[8,32,128]{2,1,0:T(8,128)S(1)} %get-tuple-element.65.refs_0_.solved, ...), custom_call_target="tpu_custom_call" | custom-call | bytes 1000 | tf_op jit(solution)/shard_map/pallas_call | solution.py:280
  37.3 0.6 %collective-permute-start.22 = (f32[2,32,128]{2,1,0:T(8,128)S(1)}, f32[2,32,128]{2,1,0:T(8,128)S(1)}, u32[]{:S(2)}, u32[]{:S(2)}) collective-permute-start(f32[2,32,128]{2,1,0:T(8,128)S(1)} %get-tuple-element.75), channel_id=1, source_target_pairs={{0,4},{4,0},{8,12},{12,8},{1,5},{5,1},{9,13},{13,9},{2,6},{6,2},{1... | collective-permute-start | bytes 98312 | tf_op jit(solution)/shard_map/ppermute | solution.py:172
  37.8 1.4 %collective-permute-start.23 = (f32[32,128]{1,0:T(8,128)S(1)}, f32[32,128]{1,0:T(8,128)S(1)}, u32[]{:S(2)}, u32[]{:S(2)}) collective-permute-start(f32[32,128]{1,0:T(8,128)S(1)} %get-tuple-element.76), channel_id=1, source_target_pairs={{0,8},{4,12},{8,0},{12,4},{1,9},{5,13},{9,1},{13,5},{2,10},{6,14},... | collective-permute-start | bytes 49160 | tf_op jit(solution)/shard_map/ppermute | solution.py:172
  39.2 2.5 %collective-permute-start.24 = (f32[32,128]{1,0:T(8,128)S(1)}, f32[32,128]{1,0:T(8,128)S(1)}, u32[]{:S(2)}, u32[]{:S(2)}) collective-permute-start(f32[32,128]{1,0:T(8,128)S(1)} %get-tuple-element.77), channel_id=1, source_target_pairs={{0,12},{4,8},{8,4},{12,0},{1,13},{5,9},{9,5},{13,1},{2,14},{6,10},... | collective-permute-start | bytes 49160 | tf_op jit(solution)/shard_map/ppermute | solution.py:172
  41.7 0.5 %collective-permute-start.31 = (f32[2,32,128]{2,1,0:T(8,128)S(1)}, f32[2,32,128]{2,1,0:T(8,128)S(1)}, u32[]{:S(2)}, u32[]{:S(2)}) collective-permute-start(f32[2,32,128]{2,1,0:T(8,128)S(1)} %collective-permute-done.29.a1), channel_id=1, source_target_pairs={{0,1},{1,0},{2,3},{3,2},{4,5},{5,4},{6,7},{7,6},{8,9},{9,8},{10,11... | collective-permute-start | bytes 98312 | tf_op jit(solution)/shard_map/ppermute | solution.py:169
  42.5 2.3 %collective-permute-done.24.refs_3_ = f32[32,128]{1,0:T(8,128)S(1)} collective-permute-done((f32[32,128]{1,0:T(8,128)S(1)}, f32[32,128]{1,0:T(8,128)S(1)}, u32[]{:S(2)}, u32[]{:S(2)}) %collective-permute-start.24) | collective-permute-done | bytes 16416 | tf_op jit(solution)/shard_map/ppermute | solution.py:172
  44.8 0.5 %collective-permute-start.26 = (f32[32,128]{1,0:T(8,128)S(1)}, f32[32,128]{1,0:T(8,128)S(1)}, u32[]{:S(2)}, u32[]{:S(2)}) collective-permute-start(f32[32,128]{1,0:T(8,128)S(1)} %collective-permute-done.23.refs_1_), channel_id=1, source_target_pairs={{0,1},{1,0},{2,3},{3,2},{4,5},{5,4},{6,7},{7,6},{8,9},{9,8},{10,11... | collective-permute-start | bytes 49160 | tf_op jit(solution)/shard_map/ppermute | solution.py:169
  45.3 0.7 %shard_map.54.refs_8_ = f32[2,64,128]{2,1,0:T(8,128)S(1)} custom-call(s32[6]{0:T(128)S(1)} %stack.27.ids, f32[2,32,128]{2,1,0:T(8,128)S(1)} %get-tuple-element.81.a0, f32[2,32,128]{2,1,0:T(8,128)S(1)} %collective-permute-done.29.a1, f32[2,32,128]{2,1,0:T(8,128)S(1)} %collective-permute-done.30.a2, f32[2,32,128]{2,1,0:T(8,128)S(1)} %collective-permute-done.31.a3), custom_call_target="tpu_custom_call" | custom-call | bytes 1000 | tf_op jit(solution)/shard_map/pallas_call | solution.py:264
  46.5 1.4 %shard_map.55 = f32[4,64,128]{2,1,0:T(8,128)} custom-call(s32[6]{0:T(128)S(1)} %stack.27.ids, f32[2,32,128]{2,1,0:T(8,128)S(1)} %get-tuple-element.74.refs_0_, f32[32,128]{1,0:T(8,128)S(1)} %collective-permute-done.23.refs_1_, f32[2,32,128]{2,1,0:T(8,128)S(1)} %collective-permute-done.22.refs_2_, f32[32,128]{1,0:T(8,128)S(1)} %collective-permute-done.24.refs_3_, ...), custom_call_target="tpu_custom_call" | custom-call | bytes 1000 | tf_op jit(solution)/shard_map/pallas_call | solution.py:293
  (65 shorter events, 5.1 us)
Async XLA Ops:
  1.0 1.5 %collective-permute-start = (f32[64,512]{1,0:T(8,128)S(1)}, f32[64,512]{1,0:T(8,128)S(1)}, u32[]{:S(2)}, u32[]{:S(2)}) collective-permute-start(f32[64,512]{1,0:T(8,128)S(1)} %slice_bitcast_fusion.3.own), channel_id=1, source_target_pairs={{0,1},{1,0},{2,3},{3,2},{4,5},{5,4},{6,7},{7,6},{8,9},{9,8},{10,11... | collective-permute-start | bytes 393224 | tf_op jit(solution)/shard_map/ppermute | solution.py:169
  1.5 1.3 %collective-permute-start.1 = (f32[4,64,128]{2,1,0:T(8,128)S(1)}, f32[4,64,128]{2,1,0:T(8,128)S(1)}, u32[]{:S(2)}, u32[]{:S(2)}) collective-permute-start(f32[4,64,128]{2,1,0:T(8,128)S(1)} %copy-done), channel_id=1, source_target_pairs={{0,1},{1,0},{2,3},{3,2},{4,5},{5,4},{6,7},{7,6},{8,9},{9,8},{10,11... | collective-permute-start | bytes 393224 | tf_op jit(solution)/shard_map/ppermute | solution.py:169
  3.7 5.8 %collective-permute-start.2 = (f32[5,32,128]{2,1,0:T(8,128)S(1)}, f32[5,32,128]{2,1,0:T(8,128)S(1)}, u32[]{:S(2)}, u32[]{:S(2)}) collective-permute-start(f32[5,32,128]{2,1,0:T(8,128)S(1)} %get-tuple-element.44), channel_id=1, source_target_pairs={{0,4},{4,0},{8,12},{12,8},{1,5},{5,1},{9,13},{13,9},{2,6},{6,2},{1... | collective-permute-start | bytes 245768 | tf_op jit(solution)/shard_map/ppermute | solution.py:172
  6.6 10.6 %collective-permute-start.4 = (f32[64,896]{1,0:T(8,128)S(1)}, f32[64,896]{1,0:T(8,128)S(1)}, u32[]{:S(2)}, u32[]{:S(2)}) collective-permute-start(f32[64,896]{1,0:T(8,128)S(1)} %pad_maximum_fusion.a0), channel_id=1, source_target_pairs={{0,1},{1,0},{2,3},{3,2},{4,5},{5,4},{6,7},{7,6},{8,9},{9,8},{10,11... | collective-permute-start | bytes 688136 | tf_op jit(solution)/shard_map/ppermute | solution.py:169
  6.7 9.8 %collective-permute-start.5 = (f32[64,896]{1,0:T(8,128)S(1)}, f32[64,896]{1,0:T(8,128)S(1)}, u32[]{:S(2)}, u32[]{:S(2)}) collective-permute-start(f32[64,896]{1,0:T(8,128)S(1)} %pad_maximum_fusion.a0), channel_id=1, source_target_pairs={{0,4},{4,0},{8,12},{12,8},{1,5},{5,1},{9,13},{13,9},{2,6},{6,2},{1... | collective-permute-start | bytes 688136 | tf_op jit(solution)/shard_map/ppermute | solution.py:172
  9.5 6.1 %collective-permute-start.3 = (f32[4,32,128]{2,1,0:T(8,128)S(1)}, f32[4,32,128]{2,1,0:T(8,128)S(1)}, u32[]{:S(2)}, u32[]{:S(2)}) collective-permute-start(f32[4,32,128]{2,1,0:T(8,128)S(1)} %slice_add_fusion.refs_0_), channel_id=1, source_target_pairs={{0,8},{4,12},{8,0},{12,4},{1,9},{5,13},{9,1},{13,5},{2,10},{6,14},... | collective-permute-start | bytes 196616 | tf_op jit(solution)/shard_map/ppermute | solution.py:172
  12.3 10.1 %collective-permute-start.12 = (f32[64,896]{1,0:T(8,128)S(1)}, f32[64,896]{1,0:T(8,128)S(1)}, u32[]{:S(2)}, u32[]{:S(2)}) collective-permute-start(f32[64,896]{1,0:T(8,128)S(1)} %pad_maximum_fusion.1.a0), channel_id=1, source_target_pairs={{0,4},{4,0},{8,12},{12,8},{1,5},{5,1},{9,13},{13,9},{2,6},{6,2},{1... | collective-permute-start | bytes 688136 | tf_op jit(solution)/shard_map/ppermute | solution.py:172
  16.6 1.3 %collective-permute-start.9 = (f32[16,896]{1,0:T(8,128)S(1)}, f32[16,896]{1,0:T(8,128)S(1)}, u32[]{:S(2)}, u32[]{:S(2)}) collective-permute-start(f32[16,896]{1,0:T(8,128)S(1)} %get-tuple-element.92), channel_id=1, source_target_pairs={{0,1},{1,0},{2,3},{3,2},{4,5},{5,4},{6,7},{7,6},{8,9},{9,8},{10,11... | collective-permute-start | bytes 172040 | tf_op jit(solution)/shard_map/ppermute | solution.py:169
  16.7 1.4 %collective-permute-start.8 = (f32[16,896]{1,0:T(8,128)S(1)}, f32[16,896]{1,0:T(8,128)S(1)}, u32[]{:S(2)}, u32[]{:S(2)}) collective-permute-start(f32[16,896]{1,0:T(8,128)S(1)} %get-tuple-element.93), channel_id=1, source_target_pairs={{0,1},{1,0},{2,3},{3,2},{4,5},{5,4},{6,7},{7,6},{8,9},{9,8},{10,11... | collective-permute-start | bytes 172040 | tf_op jit(solution)/shard_map/ppermute | solution.py:169
  17.2 3.5 %collective-permute-start.7 = (f32[16,896]{1,0:T(8,128)S(1)}, f32[16,896]{1,0:T(8,128)S(1)}, u32[]{:S(2)}, u32[]{:S(2)}) collective-permute-start(f32[16,896]{1,0:T(8,128)S(1)} %get-tuple-element.94), channel_id=1, source_target_pairs={{0,1},{1,0},{2,3},{3,2},{4,5},{5,4},{6,7},{7,6},{8,9},{9,8},{10,11... | collective-permute-start | bytes 172040 | tf_op jit(solution)/shard_map/ppermute | solution.py:169
  17.3 3.4 %collective-permute-start.6 = (f32[16,896]{1,0:T(8,128)S(1)}, f32[16,896]{1,0:T(8,128)S(1)}, u32[]{:S(2)}, u32[]{:S(2)}) collective-permute-start(f32[16,896]{1,0:T(8,128)S(1)} %get-tuple-element.95), channel_id=1, source_target_pairs={{0,1},{1,0},{2,3},{3,2},{4,5},{5,4},{6,7},{7,6},{8,9},{9,8},{10,11... | collective-permute-start | bytes 172040 | tf_op jit(solution)/shard_map/ppermute | solution.py:169
  17.9 6.3 %collective-permute-start.11 = (f32[64,896]{1,0:T(8,128)S(1)}, f32[64,896]{1,0:T(8,128)S(1)}, u32[]{:S(2)}, u32[]{:S(2)}) collective-permute-start(f32[64,896]{1,0:T(8,128)S(1)} %pad_maximum_fusion.1.a0), channel_id=1, source_target_pairs={{0,1},{1,0},{2,3},{3,2},{4,5},{5,4},{6,7},{7,6},{8,9},{9,8},{10,11... | collective-permute-start | bytes 688136 | tf_op jit(solution)/shard_map/ppermute | solution.py:169
  18.1 11.0 %collective-permute-start.19 = (f32[64,896]{1,0:T(8,128)S(1)}, f32[64,896]{1,0:T(8,128)S(1)}, u32[]{:S(2)}, u32[]{:S(2)}) collective-permute-start(f32[64,896]{1,0:T(8,128)S(1)} %pad_maximum_fusion.2.a0), channel_id=1, source_target_pairs={{0,4},{4,0},{8,12},{12,8},{1,5},{5,1},{9,13},{13,9},{2,6},{6,2},{1... | collective-permute-start | bytes 688136 | tf_op jit(solution)/shard_map/ppermute | solution.py:172
  22.4 2.1 %collective-permute-start.16 = (f32[16,896]{1,0:T(8,128)S(1)}, f32[16,896]{1,0:T(8,128)S(1)}, u32[]{:S(2)}, u32[]{:S(2)}) collective-permute-start(f32[16,896]{1,0:T(8,128)S(1)} %get-tuple-element.88), channel_id=1, source_target_pairs={{0,1},{1,0},{2,3},{3,2},{4,5},{5,4},{6,7},{7,6},{8,9},{9,8},{10,11... | collective-permute-start | bytes 172040 | tf_op jit(solution)/shard_map/ppermute | solution.py:169
  22.5 5.7 %collective-permute-start.10 = (f32[4,32,128]{2,1,0:T(8,128)S(1)}, f32[4,32,128]{2,1,0:T(8,128)S(1)}, u32[]{:S(2)}, u32[]{:S(2)}) collective-permute-start(f32[4,32,128]{2,1,0:T(8,128)S(1)} %get-tuple-element.57.refs_1_), channel_id=1, source_target_pairs={{0,8},{4,12},{8,0},{12,4},{1,9},{5,13},{9,1},{13,5},{2,10},{6,14},... | collective-permute-start | bytes 196616 | tf_op jit(solution)/shard_map/ppermute | solution.py:172
  24.0 1.2 %collective-permute-start.15 = (f32[16,896]{1,0:T(8,128)S(1)}, f32[16,896]{1,0:T(8,128)S(1)}, u32[]{:S(2)}, u32[]{:S(2)}) collective-permute-start(f32[16,896]{1,0:T(8,128)S(1)} %get-tuple-element.89), channel_id=1, source_target_pairs={{0,1},{1,0},{2,3},{3,2},{4,5},{5,4},{6,7},{7,6},{8,9},{9,8},{10,11... | collective-permute-start | bytes 172040 | tf_op jit(solution)/shard_map/ppermute | solution.py:169
  24.2 1.2 %collective-permute-start.14 = (f32[16,896]{1,0:T(8,128)S(1)}, f32[16,896]{1,0:T(8,128)S(1)}, u32[]{:S(2)}, u32[]{:S(2)}) collective-permute-start(f32[16,896]{1,0:T(8,128)S(1)} %get-tuple-element.90), channel_id=1, source_target_pairs={{0,1},{1,0},{2,3},{3,2},{4,5},{5,4},{6,7},{7,6},{8,9},{9,8},{10,11... | collective-permute-start | bytes 172040 | tf_op jit(solution)/shard_map/ppermute | solution.py:169
  24.5 1.2 %collective-permute-start.13 = (f32[16,896]{1,0:T(8,128)S(1)}, f32[16,896]{1,0:T(8,128)S(1)}, u32[]{:S(2)}, u32[]{:S(2)}) collective-permute-start(f32[16,896]{1,0:T(8,128)S(1)} %get-tuple-element.91), channel_id=1, source_target_pairs={{0,1},{1,0},{2,3},{3,2},{4,5},{5,4},{6,7},{7,6},{8,9},{9,8},{10,11... | collective-permute-start | bytes 172040 | tf_op jit(solution)/shard_map/ppermute | solution.py:169
  25.2 7.8 %collective-permute-start.18 = (f32[64,896]{1,0:T(8,128)S(1)}, f32[64,896]{1,0:T(8,128)S(1)}, u32[]{:S(2)}, u32[]{:S(2)}) collective-permute-start(f32[64,896]{1,0:T(8,128)S(1)} %pad_maximum_fusion.2.a0), channel_id=1, source_target_pairs={{0,1},{1,0},{2,3},{3,2},{4,5},{5,4},{6,7},{7,6},{8,9},{9,8},{10,11... | collective-permute-start | bytes 688136 | tf_op jit(solution)/shard_map/ppermute | solution.py:169
  29.2 3.9 %collective-permute-start.21 = (f32[32,896]{1,0:T(8,128)S(1)}, f32[32,896]{1,0:T(8,128)S(1)}, u32[]{:S(2)}, u32[]{:S(2)}) collective-permute-start(f32[32,896]{1,0:T(8,128)S(1)} %get-tuple-element.86), channel_id=1, source_target_pairs={{0,1},{1,0},{2,3},{3,2},{4,5},{5,4},{6,7},{7,6},{8,9},{9,8},{10,11... | collective-permute-start | bytes 344072 | tf_op jit(solution)/shard_map/ppermute | solution.py:169
  29.2 3.8 %collective-permute-start.20 = (f32[32,896]{1,0:T(8,128)S(1)}, f32[32,896]{1,0:T(8,128)S(1)}, u32[]{:S(2)}, u32[]{:S(2)}) collective-permute-start(f32[32,896]{1,0:T(8,128)S(1)} %get-tuple-element.87), channel_id=1, source_target_pairs={{0,1},{1,0},{2,3},{3,2},{4,5},{5,4},{6,7},{7,6},{8,9},{9,8},{10,11... | collective-permute-start | bytes 344072 | tf_op jit(solution)/shard_map/ppermute | solution.py:169
  29.7 6.6 %collective-permute-start.17 = (f32[4,32,128]{2,1,0:T(8,128)S(1)}, f32[4,32,128]{2,1,0:T(8,128)S(1)}, u32[]{:S(2)}, u32[]{:S(2)}) collective-permute-start(f32[4,32,128]{2,1,0:T(8,128)S(1)} %get-tuple-element.66.refs_1_), channel_id=1, source_target_pairs={{0,8},{4,12},{8,0},{12,4},{1,9},{5,13},{9,1},{13,5},{2,10},{6,14},... | collective-permute-start | bytes 196616 | tf_op jit(solution)/shard_map/ppermute | solution.py:172
  32.9 8.8 %collective-permute-start.29 = (f32[2,32,128]{2,1,0:T(8,128)S(1)}, f32[2,32,128]{2,1,0:T(8,128)S(1)}, u32[]{:S(2)}, u32[]{:S(2)}) collective-permute-start(f32[2,32,128]{2,1,0:T(8,128)S(1)} %get-tuple-element.82), channel_id=1, source_target_pairs={{0,4},{4,0},{8,12},{12,8},{1,5},{5,1},{9,13},{13,9},{2,6},{6,2},{1... | collective-permute-start | bytes 98312 | tf_op jit(solution)/shard_map/ppermute | solution.py:172
  37.3 7.5 %collective-permute-start.22 = (f32[2,32,128]{2,1,0:T(8,128)S(1)}, f32[2,32,128]{2,1,0:T(8,128)S(1)}, u32[]{:S(2)}, u32[]{:S(2)}) collective-permute-start(f32[2,32,128]{2,1,0:T(8,128)S(1)} %get-tuple-element.75), channel_id=1, source_target_pairs={{0,4},{4,0},{8,12},{12,8},{1,5},{5,1},{9,13},{13,9},{2,6},{6,2},{1... | collective-permute-start | bytes 98312 | tf_op jit(solution)/shard_map/ppermute | solution.py:172
  37.8 4.6 %collective-permute-start.23 = (f32[32,128]{1,0:T(8,128)S(1)}, f32[32,128]{1,0:T(8,128)S(1)}, u32[]{:S(2)}, u32[]{:S(2)}) collective-permute-start(f32[32,128]{1,0:T(8,128)S(1)} %get-tuple-element.76), channel_id=1, source_target_pairs={{0,8},{4,12},{8,0},{12,4},{1,9},{5,13},{9,1},{13,5},{2,10},{6,14},... | collective-permute-start | bytes 49160 | tf_op jit(solution)/shard_map/ppermute | solution.py:172
  39.2 5.5 %collective-permute-start.24 = (f32[32,128]{1,0:T(8,128)S(1)}, f32[32,128]{1,0:T(8,128)S(1)}, u32[]{:S(2)}, u32[]{:S(2)}) collective-permute-start(f32[32,128]{1,0:T(8,128)S(1)} %get-tuple-element.77), channel_id=1, source_target_pairs={{0,12},{4,8},{8,4},{12,0},{1,13},{5,9},{9,5},{13,1},{2,14},{6,10},... | collective-permute-start | bytes 49160 | tf_op jit(solution)/shard_map/ppermute | solution.py:172
  41.7 3.6 %collective-permute-start.30 = (f32[2,32,128]{2,1,0:T(8,128)S(1)}, f32[2,32,128]{2,1,0:T(8,128)S(1)}, u32[]{:S(2)}, u32[]{:S(2)}) collective-permute-start(f32[2,32,128]{2,1,0:T(8,128)S(1)} %get-tuple-element.81.a0), channel_id=1, source_target_pairs={{0,1},{1,0},{2,3},{3,2},{4,5},{5,4},{6,7},{7,6},{8,9},{9,8},{10,11... | collective-permute-start | bytes 98312 | tf_op jit(solution)/shard_map/ppermute | solution.py:169
  41.7 3.6 %collective-permute-start.31 = (f32[2,32,128]{2,1,0:T(8,128)S(1)}, f32[2,32,128]{2,1,0:T(8,128)S(1)}, u32[]{:S(2)}, u32[]{:S(2)}) collective-permute-start(f32[2,32,128]{2,1,0:T(8,128)S(1)} %collective-permute-done.29.a1), channel_id=1, source_target_pairs={{0,1},{1,0},{2,3},{3,2},{4,5},{5,4},{6,7},{7,6},{8,9},{9,8},{10,11... | collective-permute-start | bytes 98312 | tf_op jit(solution)/shard_map/ppermute | solution.py:169
  42.5 3.6 %collective-permute-start.25 = (f32[2,32,128]{2,1,0:T(8,128)S(1)}, f32[2,32,128]{2,1,0:T(8,128)S(1)}, u32[]{:S(2)}, u32[]{:S(2)}) collective-permute-start(f32[2,32,128]{2,1,0:T(8,128)S(1)} %get-tuple-element.74.refs_0_), channel_id=1, source_target_pairs={{0,1},{1,0},{2,3},{3,2},{4,5},{5,4},{6,7},{7,6},{8,9},{9,8},{10,11... | collective-permute-start | bytes 98312 | tf_op jit(solution)/shard_map/ppermute | solution.py:169
  44.8 1.7 %collective-permute-start.27 = (f32[2,32,128]{2,1,0:T(8,128)S(1)}, f32[2,32,128]{2,1,0:T(8,128)S(1)}, u32[]{:S(2)}, u32[]{:S(2)}) collective-permute-start(f32[2,32,128]{2,1,0:T(8,128)S(1)} %collective-permute-done.22.refs_2_), channel_id=1, source_target_pairs={{0,1},{1,0},{2,3},{3,2},{4,5},{5,4},{6,7},{7,6},{8,9},{9,8},{10,11... | collective-permute-start | bytes 98312 | tf_op jit(solution)/shard_map/ppermute | solution.py:169
  44.8 1.3 %collective-permute-start.26 = (f32[32,128]{1,0:T(8,128)S(1)}, f32[32,128]{1,0:T(8,128)S(1)}, u32[]{:S(2)}, u32[]{:S(2)}) collective-permute-start(f32[32,128]{1,0:T(8,128)S(1)} %collective-permute-done.23.refs_1_), channel_id=1, source_target_pairs={{0,1},{1,0},{2,3},{3,2},{4,5},{5,4},{6,7},{7,6},{8,9},{9,8},{10,11... | collective-permute-start | bytes 49160 | tf_op jit(solution)/shard_map/ppermute | solution.py:169
  45.3 1.2 %collective-permute-start.28 = (f32[32,128]{1,0:T(8,128)S(1)}, f32[32,128]{1,0:T(8,128)S(1)}, u32[]{:S(2)}, u32[]{:S(2)}) collective-permute-start(f32[32,128]{1,0:T(8,128)S(1)} %collective-permute-done.24.refs_3_), channel_id=1, source_target_pairs={{0,1},{1,0},{2,3},{3,2},{4,5},{5,4},{6,7},{7,6},{8,9},{9,8},{10,11... | collective-permute-start | bytes 49160 | tf_op jit(solution)/shard_map/ppermute | solution.py:169
  (4 other events, 8.7 us)

commit v4 on v3

--- a/solution.py
+++ b/solution.py
@@ -7,7 +7,7 @@
 from jax.experimental.pallas import tpu as pltpu
 from jax.sharding import PartitionSpec as P
 
-K = {'first': 0.3, 'prep': [2, 0, 0], 'step': [0, 0.1, 0], 'bulk': ['send', 'share0', 'share0'], 'swap': ['recv0', 'share1', 'share2'], 'rest': ['send', 'send', 'send'], 'groups': [[1], [2], [3]], 'meet': 1, 'early': 2, 'cut': [4, 4, 2]}
+K = {'first': 0.3, 'prep': [2, 0, 0], 'step': [0, 0.1, 0], 'bulk': ['send', 'share0', 'share0'], 'swap': ['recv0', 'share1', 'share2'], 'rest': ['send', 'send', 'send'], 'groups': [[1], [2], [3]], 'meet': 1, 'early': 0, 'cut': [4, 4, 1]}
 S = 4
 BS = 128
 LANES = 128
@@ -51,13 +51,15 @@
     for i in range(blocks):
         terms[i] = share[:, i * BS : (i + 1) * BS]
     keep[...] = terms[:, pl.ds(pl.multiple_of(ids[1] * quarter, quarter), quarter), :]
-    send[:blocks] = terms[:, pl.ds(pl.multiple_of((1 - ids[1]) * quarter, quarter), quarter), :]
-    lane = lax.broadcasted_iota(jnp.int32, (quarter, BS), 1)
-    told = jnp.zeros((quarter, BS), jnp.float32)
+    away = pl.ds(pl.multiple_of((1 - ids[1]) * quarter, quarter), quarter)
+    for i in range(blocks):
+        send[i * quarter : (i + 1) * quarter] = terms[i, away, :]
+    lane = lax.broadcasted_iota(jnp.int32, (8, BS), 1)
+    told = jnp.zeros((8, BS), jnp.float32)
     for i in range(lists.shape[0]):
         for k in range(lists.shape[2]):
             told = jnp.where(lane == i * lists.shape[2] + k, lists[i, 0, k].astype(jnp.float32), told)
-    send[blocks] = told
+    send[blocks * quarter :] = told
 
 
 def prepare_kernel(quarter, place, ids, a0, a1, a2, *refs):
@@ -136,17 +138,13 @@
     return jnp.where(core == 0, whole[:, :rows], whole[:, rows:]).T
 
 
-def place_early_kernel(quarter, ids, a0, a1, a2, a3, out, whole):
-    for t in range(out.shape[0]):
-        out[t] = place(quarter, ids, (a0[t], a1[t], a2[t], a3[t]), whole)
-
-
 def place_kernel(quarter, first, ids, *refs):
-    quarters, out, whole = refs[:8], refs[-2], refs[-1]
-    if first:
-        out[:first] = refs[8][...]
-    for t in range(first, S):
-        parts = [quarters[2 * i][t - first] for i in range(4)]
+    quarters, early, out, whole = refs[:8], refs[8:-2], refs[-2], refs[-1]
+    for t in range(S):
+        if t < first:
+            parts = [a[t] for a in early]
+        else:
+            parts = [quarters[2 * i][t - first] for i in range(4)]
         if t == S - 1:
             parts = [part + quarters[2 * i + 1][...] for i, part in enumerate(parts)]
         out[t] = place(quarter, ids, parts, whole)
@@ -202,7 +200,7 @@
     diag_first = diag_inverse[0]
     keep, send = call(
         functools.partial(first_kernel, quarter),
-        (piece, shape((blocks + 1, quarter, BS), f32)),
+        (piece, shape((blocks * quarter + 8, BS), f32)),
         [pltpu.VMEM((4 * quarter, BS), f32), pltpu.VMEM((blocks, 2 * quarter, BS), f32)],
         K["first"],
     )(in_specs=[SMEM, SMEM, VMEM, VMEM, VMEM, VMEM])(
@@ -220,8 +218,8 @@
         rest.append(jnp.concatenate(rows, axis=0))
     rest_core = [to_core(a) for a in rest]
 
-    share = keep + got[:blocks]
-    told = got[blocks, 0, : (S - 1) * listed].reshape(S - 1, listed).astype(jnp.int32)
+    share = keep + got[: blocks * quarter].reshape(blocks, quarter, BS)
+    told = got[blocks * quarter, : (S - 1) * listed].reshape(S - 1, listed).astype(jnp.int32)
 
     gates = {"none": None, "send": send, "share0": share, "core1": rest_core[0]}
     stored, first = (), K["early"]
@@ -259,13 +257,9 @@
             gates[f"share{t}"] = share
             if t == S - 2 and first:
                 early = shape((first, quarter, BS), f32)
-                own, near = call(early_kernel, (early, early))(in_specs=[SMEM, VMEM])(ids, solved)
+                early_kept, near = call(early_kernel, (early, early))(in_specs=[SMEM, VMEM])(ids, solved)
                 near = to_row(near, 1)
-                placed = call(
-                    functools.partial(place_early_kernel, quarter),
-                    shape((first, BS // 2, 4 * quarter), f32),
-                    [pltpu.VMEM((4 * quarter, BS), f32)],
-                )(in_specs=[SMEM] + [VMEM] * 4)(ids, own, near, to_core(own), to_core(near))
+                placed = [early_kept, near, to_core(early_kept), to_core(near)]
 
     block = shape((quarter, BS), f32)
     kept = shape((S - first, quarter, BS), f32)
@@ -289,7 +283,7 @@
     quarters = [own, far, near, both]
     quarters += [to_core(a) for a in quarters]
     if first:
-        quarters.append(placed)
+        quarters += placed
     return call(
         functools.partial(place_kernel, quarter, first),
         shape((S, BS // 2, 4 * quarter), f32),

time: 48 us -> 47.1 us (0.981)
  waiting for transfers between devices: 12.2 us -> 13.8 us
  Pallas kernels: 8.57 us -> 7.34 us
  starting transfers between devices: 24.8 us -> 23.6 us
    pallas_call x3 -> x1, Pallas kernels: 2.1 us -> 0.85 us  [body(): call(functools.partial(first_kernel, quarter), (piece, shape((blocks * qu...]
    ppermute x21 -> x18, starting transfers between devices: 4.53 us -> 3.52 us  [to_core(): return lax.ppermute(a, 'sub', [(0, 1), (1, 0)])]
    ppermute x11 -> x10, waiting for transfers between devices: 10.3 us -> 11.2 us  [to_row(): return lax.ppermute(a, 'row', [(i, i ^ bit) for i in range(count)])]
    ppermute x21 -> x18, waiting for transfers between devices: 1.91 us -> 2.63 us  [to_core(): return lax.ppermute(a, 'sub', [(0, 1), (1, 0)])]
    ppermute x11 -> x10, starting transfers between devices: 20.2 us -> 20.1 us  [to_row(): return lax.ppermute(a, 'row', [(i, i ^ bit) for i in range(count)])]
  transfers between devices with their start and end apart: 32 -> 28, of which waited for: 13 -> 13; matrix products, arithmetic and copies ran while one was open for 1% -> 1% of each run, Pallas kernels for 13% -> 9%
where the time goes in v4:
time: 47.1 us; the launch traced here: 47 us
  starting transfers between devices  23.6 us (50%)
  waiting for transfers between devices  13.8 us (29%)
  Pallas kernels  7.34 us (16%)
  local copies, waits for them, and re-layouts  1.99 us (4%)
    ppermute x10, starting transfers between devices, to_row(): return lax.ppermute(a, 'row', [(i, i ^ bit) for i in range(count)])  20.1 us
    ppermute x10, waiting for transfers between devices, to_row(): return lax.ppermute(a, 'row', [(i, i ^ bit) for i in range(count)])  11.2 us
    ppermute x18, starting transfers between devices, to_core(): return lax.ppermute(a, 'sub', [(0, 1), (1, 0)])  3.52 us
    ppermute x18, waiting for transfers between devices, to_core(): return lax.ppermute(a, 'sub', [(0, 1), (1, 0)])  2.63 us
    pallas_call x3, Pallas kernels, prepare(): call(functools.partial(prepare_kernel, quarter, place), (shape((2 * BS, w...  2.3 us
    pallas_call x2, Pallas kernels, body(): call(functools.partial(step_kernel, t), (solved_shape, piece), (), K['ste...  1.83 us
    pallas_call x1, Pallas kernels, body(): call(functools.partial(place_kernel, quarter, first), shape((S, BS // 2,...  1.41 us
    squeeze x1, local copies, waits for them, and re-layouts, body(): diag_first = diag_inverse[0]  0.95 us
  transfers between devices with their start and end apart: 28, of which 13 were waited for; matrix products, arithmetic and copies ran while one was open for 1% of the time, Pallas kernels for 9%

profile of v4, /device:TPU:0, one launch (start us, length us, event | category | flops | bytes accessed | tf_op | source)
XLA Modules:
  0.0 47.0 jit_solution(12258231996341523639)
XLA Ops:
  0.0 0.9 %slice_bitcast_fusion.3.own = f32[64,512]{1,0:T(8,128)S(1)} fusion(f32[4,64,512]{2,1,0:T(8,128)} %param.5), kind=kLoop, calls=%fused_computation.6 | loop fusion | bytes 262144 | tf_op jit(solution)/shard_map/squeeze | solution.py:200
  1.0 0.5 %collective-permute-start = (f32[64,512]{1,0:T(8,128)S(1)}, f32[64,512]{1,0:T(8,128)S(1)}, u32[]{:S(2)}, u32[]{:S(2)}) collective-permute-start(f32[64,512]{1,0:T(8,128)S(1)} %slice_bitcast_fusion.3.own), channel_id=1, source_target_pairs={{0,1},{1,0},{2,3},{3,2},{4,5},{5,4},{6,7},{7,6},{8,9},{9,8},{10,11... | collective-permute-start | bytes 393224 | tf_op jit(solution)/shard_map/ppermute | solution.py:167
  1.6 0.7 %copy-done.3 = s32[3,1,2]{0,2,1:T(2,128)S(1)} copy-done((s32[3,1,2]{0,2,1:T(2,128)S(1)}, s32[3,1,2]{0,2,1:T(2,128)}, u32[]{:S(2)}) %copy-start.3) | copy-done | bytes 48
  2.8 0.8 %shard_map.46 = (f32[4,32,128]{2,1,0:T(8,128)S(1)}, f32[136,128]{1,0:T(8,128)S(1)}) custom-call(s32[6]{0:T(128)S(1)} %stack.27.ids, s32[3,1,2]{2,1,0:T(1,128)S(1)} %copy.12.lists, f32[64,512]{1,0:T(8,128)S(1)} %slice_bitcast_fusion.3.own, f32[64,512]{1,0:T(8,128)S(1)} %collective-permute-done.other, f32[4,64,128]{2,1,0:T(8,128)S(1)} %copy-done, ...), custom_call_target="tpu_custom_call" | custom-call | flops 300000000 | bytes 1000 | tf_op jit(solution)/shard_map/pallas_call | solution.py:201
  3.7 2.8 %collective-permute-start.2 = (f32[136,128]{1,0:T(8,128)S(1)}, f32[136,128]{1,0:T(8,128)S(1)}, u32[]{:S(2)}, u32[]{:S(2)}) collective-permute-start(f32[136,128]{1,0:T(8,128)S(1)} %get-tuple-element.42), channel_id=1, source_target_pairs={{0,4},{4,0},{8,12},{12,8},{1,5},{5,1},{9,13},{13,9},{2,6},{6,2},{1... | collective-permute-start | bytes 208904 | tf_op jit(solution)/shard_map/ppermute | solution.py:170
  6.7 1.2 %collective-permute-start.5 = (f32[64,896]{1,0:T(8,128)S(1)}, f32[64,896]{1,0:T(8,128)S(1)}, u32[]{:S(2)}, u32[]{:S(2)}) collective-permute-start(f32[64,896]{1,0:T(8,128)S(1)} %pad_maximum_fusion.a0), channel_id=1, source_target_pairs={{0,4},{4,0},{8,12},{12,8},{1,5},{5,1},{9,13},{13,9},{2,6},{6,2},{1... | collective-permute-start | bytes 688136 | tf_op jit(solution)/shard_map/ppermute | solution.py:170
  8.0 1.2 %collective-permute-done.2 = f32[136,128]{1,0:T(8,128)S(1)} collective-permute-done((f32[136,128]{1,0:T(8,128)S(1)}, f32[136,128]{1,0:T(8,128)S(1)}, u32[]{:S(2)}, u32[]{:S(2)}) %collective-permute-start.2) | collective-permute-done | bytes 69664 | tf_op jit(solution)/shard_map/ppermute | solution.py:170
  9.2 2.8 %collective-permute-start.3 = (f32[4,32,128]{2,1,0:T(8,128)S(1)}, f32[4,32,128]{2,1,0:T(8,128)S(1)}, u32[]{:S(2)}, u32[]{:S(2)}) collective-permute-start(f32[4,32,128]{2,1,0:T(8,128)S(1)} %add.15.refs_0_), channel_id=1, source_target_pairs={{0,8},{4,12},{8,0},{12,4},{1,9},{5,13},{9,1},{13,5},{2,10},{6,14},... | collective-permute-start | bytes 196616 | tf_op jit(solution)/shard_map/ppermute | solution.py:170
  12.0 1.9 %collective-permute-start.12 = (f32[64,896]{1,0:T(8,128)S(1)}, f32[64,896]{1,0:T(8,128)S(1)}, u32[]{:S(2)}, u32[]{:S(2)}) collective-permute-start(f32[64,896]{1,0:T(8,128)S(1)} %pad_maximum_fusion.1.a0), channel_id=1, source_target_pairs={{0,4},{4,0},{8,12},{12,8},{1,5},{5,1},{9,13},{13,9},{2,6},{6,2},{1... | collective-permute-start | bytes 688136 | tf_op jit(solution)/shard_map/ppermute | solution.py:170
  13.9 1.4 %collective-permute-done.3.refs_1_ = f32[4,32,128]{2,1,0:T(8,128)S(1)} collective-permute-done((f32[4,32,128]{2,1,0:T(8,128)S(1)}, f32[4,32,128]{2,1,0:T(8,128)S(1)}, u32[]{:S(2)}, u32[]{:S(2)}) %collective-permute-start.3) | collective-permute-done | bytes 65568 | tf_op jit(solution)/shard_map/ppermute | solution.py:170
  15.3 1.3 %collective-permute-done.5.a2 = f32[64,896]{1,0:T(8,128)S(1)} collective-permute-done((f32[64,896]{1,0:T(8,128)S(1)}, f32[64,896]{1,0:T(8,128)S(1)}, u32[]{:S(2)}, u32[]{:S(2)}) %collective-permute-start.5) | collective-permute-done | bytes 229408 | tf_op jit(solution)/shard_map/ppermute | solution.py:170
  16.7 0.5 %collective-permute-start.8 = (f32[16,896]{1,0:T(8,128)S(1)}, f32[16,896]{1,0:T(8,128)S(1)}, u32[]{:S(2)}, u32[]{:S(2)}) collective-permute-start(f32[16,896]{1,0:T(8,128)S(1)} %get-tuple-element.87), channel_id=1, source_target_pairs={{0,1},{1,0},{2,3},{3,2},{4,5},{5,4},{6,7},{7,6},{8,9},{9,8},{10,11... | collective-permute-start | bytes 172040 | tf_op jit(solution)/shard_map/ppermute | solution.py:167
  17.3 0.4 collective-permute-start.6
  18.1 2.6 %collective-permute-start.19 = (f32[64,896]{1,0:T(8,128)S(1)}, f32[64,896]{1,0:T(8,128)S(1)}, u32[]{:S(2)}, u32[]{:S(2)}) collective-permute-start(f32[64,896]{1,0:T(8,128)S(1)} %pad_maximum_fusion.2.a0), channel_id=1, source_target_pairs={{0,4},{4,0},{8,12},{12,8},{1,5},{5,1},{9,13},{13,9},{2,6},{6,2},{1... | collective-permute-start | bytes 688136 | tf_op jit(solution)/shard_map/ppermute | solution.py:170
  20.7 0.8 %shard_map.47 = (bf16[256,512]{1,0:T(8,128)(2,1)S(1)}, bf16[256,512]{1,0:T(8,128)(2,1)S(1)}, bf16[2,256,128]{2,1,0:T(8,128)(2,1)S(1)}, bf16[2,256,128]{2,1,0:T(8,128)(2,1)S(1)}, f32[2,32,128]{2,1,0:T(8,128)S(1)}) custom-call(s32[6]{0:T(128)S(1)} %stack.27.ids, f32[64,896]{1,0:T(8,128)S(1)} %pad_maximum_fusion.a0, f32[64,896]{1,0:T(8,128)S(1)} %collective-permute-done.4.a1, ...), custom_call_target="tpu_custom_call" | custom-call | flops 2000000000 | bytes 1000 | tf_op jit(solution)/shard_map/pallas_call | solution.py:187
  21.4 0.9 %shard_map.48 = (f32[4,32,128]{2,1,0:T(8,128)S(1)}, f32[4,32,128]{2,1,0:T(8,128)S(1)}) custom-call(s32[3,1,2]{2,1,0:T(1,128)S(1)} %copy.12.lists, s32[3,2]{1,0:T(4,128)S(1)} %convert_element_type.6.told, f32[4,32,128]{2,1,0:T(8,128)S(1)} %add.15.refs_0_, f32[4,32,128]{2,1,0:T(8,128)S(1)} %collective-permute-done.3.refs_1_, ...), custom_call_target="tpu_custom_call" | custom-call | bytes 1000 | tf_op jit(solution)/shard_map/pallas_call | solution.py:253
  22.5 1.7 %collective-permute-start.10 = (f32[4,32,128]{2,1,0:T(8,128)S(1)}, f32[4,32,128]{2,1,0:T(8,128)S(1)}, u32[]{:S(2)}, u32[]{:S(2)}) collective-permute-start(f32[4,32,128]{2,1,0:T(8,128)S(1)} %get-tuple-element.55.refs_1_), channel_id=1, source_target_pairs={{0,8},{4,12},{8,0},{12,4},{1,9},{5,13},{9,1},{13,5},{2,10},{6,14},... | collective-permute-start | bytes 196616 | tf_op jit(solution)/shard_map/ppermute | solution.py:170
  24.9 0.6 %collective-permute-done.15.refs_2_ = f32[16,896]{1,0:T(8,128)S(1)} collective-permute-done((f32[16,896]{1,0:T(8,128)S(1)}, f32[16,896]{1,0:T(8,128)S(1)}, u32[]{:S(2)}, u32[]{:S(2)}) %collective-permute-start.15) | collective-permute-done | bytes 57376 | tf_op jit(solution)/shard_map/ppermute | solution.py:167
  26.0 0.8 %shard_map.49 = (bf16[256,512]{1,0:T(8,128)(2,1)S(1)}, bf16[256,512]{1,0:T(8,128)(2,1)S(1)}, bf16[2,256,128]{2,1,0:T(8,128)(2,1)S(1)}, bf16[2,256,128]{2,1,0:T(8,128)(2,1)S(1)}, f32[2,32,128]{2,1,0:T(8,128)S(1)}) custom-call(s32[6]{0:T(128)S(1)} %stack.27.ids, f32[64,896]{1,0:T(8,128)S(1)} %pad_maximum_fusion.1.a0, ...), custom_call_target="tpu_custom_call" | custom-call | bytes 1000 | tf_op jit(solution)/shard_map/pallas_call | solution.py:187
  26.8 1.5 %collective-permute-done.10.refs_2_ = f32[4,32,128]{2,1,0:T(8,128)S(1)} collective-permute-done((f32[4,32,128]{2,1,0:T(8,128)S(1)}, f32[4,32,128]{2,1,0:T(8,128)S(1)}, u32[]{:S(2)}, u32[]{:S(2)}) %collective-permute-start.10) | collective-permute-done | bytes 65568 | tf_op jit(solution)/shard_map/ppermute | solution.py:170
  28.3 0.9 %shard_map.50 = (f32[8,32,128]{2,1,0:T(8,128)S(1)}, f32[4,32,128]{2,1,0:T(8,128)S(1)}) custom-call(s32[3,1,2]{2,1,0:T(1,128)S(1)} %copy.12.lists, s32[3,2]{1,0:T(4,128)S(1)} %convert_element_type.6.told, f32[4,32,128]{2,1,0:T(8,128)S(1)} %get-tuple-element.54.refs_0_, f32[4,32,128]{2,1,0:T(8,128)S(1)} %get-tuple-element.55.refs_1_, ...), custom_call_target="tpu_custom_call" | custom-call | flops 100000000 | bytes 1000 | tf_op jit(solution)/shard_map/pallas_call | solution.py:253
  29.3 2.6 %collective-permute-start.17 = (f32[4,32,128]{2,1,0:T(8,128)S(1)}, f32[4,32,128]{2,1,0:T(8,128)S(1)}, u32[]{:S(2)}, u32[]{:S(2)}) collective-permute-start(f32[4,32,128]{2,1,0:T(8,128)S(1)} %get-tuple-element.64.refs_1_), channel_id=1, source_target_pairs={{0,8},{4,12},{8,0},{12,4},{1,9},{5,13},{9,1},{13,5},{2,10},{6,14},... | collective-permute-start | bytes 196616 | tf_op jit(solution)/shard_map/ppermute | solution.py:170
  31.9 0.8 %shard_map.51 = (bf16[256,512]{1,0:T(8,128)(2,1)S(1)}, bf16[256,512]{1,0:T(8,128)(2,1)S(1)}, bf16[2,256,128]{2,1,0:T(8,128)(2,1)S(1)}, bf16[2,256,128]{2,1,0:T(8,128)(2,1)S(1)}, f32[2,32,128]{2,1,0:T(8,128)S(1)}) custom-call(s32[6]{0:T(128)S(1)} %stack.27.ids, f32[64,896]{1,0:T(8,128)S(1)} %pad_maximum_fusion.2.a0, ...), custom_call_target="tpu_custom_call" | custom-call | bytes 1000 | tf_op jit(solution)/shard_map/pallas_call | solution.py:187
  32.7 3.5 %collective-permute-done.17.refs_2_ = f32[4,32,128]{2,1,0:T(8,128)S(1)} collective-permute-done((f32[4,32,128]{2,1,0:T(8,128)S(1)}, f32[4,32,128]{2,1,0:T(8,128)S(1)}, u32[]{:S(2)}, u32[]{:S(2)}) %collective-permute-start.17) | collective-permute-done | bytes 65568 | tf_op jit(solution)/shard_map/ppermute | solution.py:170
  36.1 0.9 %shard_map.52 = (f32[4,32,128]{2,1,0:T(8,128)S(1)}, f32[4,32,128]{2,1,0:T(8,128)S(1)}, f32[32,128]{1,0:T(8,128)S(1)}, f32[32,128]{1,0:T(8,128)S(1)}) custom-call(s32[6]{0:T(128)S(1)} %stack.27.ids, s32[3,1,2]{2,1,0:T(1,128)S(1)} %copy.12.lists, s32[3,2]{1,0:T(4,128)S(1)} %convert_element_type.6.told, f32[8,32,128]{2,1,0:T(8,128)S(1)} %get-tuple-element.63.refs_0_, ...), custom_call_target="tpu_custom_call" | custom-call | bytes 1000 | tf_op jit(solution)/shard_map/pallas_call | solution.py:274
  37.5 0.9 %collective-permute-start.22 = (f32[32,128]{1,0:T(8,128)S(1)}, f32[32,128]{1,0:T(8,128)S(1)}, u32[]{:S(2)}, u32[]{:S(2)}) collective-permute-start(f32[32,128]{1,0:T(8,128)S(1)} %get-tuple-element.74), channel_id=1, source_target_pairs={{0,8},{4,12},{8,0},{12,4},{1,9},{5,13},{9,1},{13,5},{2,10},{6,14},... | collective-permute-start | bytes 49160 | tf_op jit(solution)/shard_map/ppermute | solution.py:170
  38.3 3.2 %collective-permute-start.23 = (f32[32,128]{1,0:T(8,128)S(1)}, f32[32,128]{1,0:T(8,128)S(1)}, u32[]{:S(2)}, u32[]{:S(2)}) collective-permute-start(f32[32,128]{1,0:T(8,128)S(1)} %get-tuple-element.75), channel_id=1, source_target_pairs={{0,12},{4,8},{8,4},{12,0},{1,13},{5,9},{9,5},{13,1},{2,14},{6,10},... | collective-permute-start | bytes 49160 | tf_op jit(solution)/shard_map/ppermute | solution.py:170
  41.6 0.6 %collective-permute-done.22.refs_1_ = f32[32,128]{1,0:T(8,128)S(1)} collective-permute-done((f32[32,128]{1,0:T(8,128)S(1)}, f32[32,128]{1,0:T(8,128)S(1)}, u32[]{:S(2)}, u32[]{:S(2)}) %collective-permute-start.22) | collective-permute-done | bytes 16416 | tf_op jit(solution)/shard_map/ppermute | solution.py:170
  42.1 1.7 %collective-permute-done.23.refs_3_ = f32[32,128]{1,0:T(8,128)S(1)} collective-permute-done((f32[32,128]{1,0:T(8,128)S(1)}, f32[32,128]{1,0:T(8,128)S(1)}, u32[]{:S(2)}, u32[]{:S(2)}) %collective-permute-start.23) | collective-permute-done | bytes 16416 | tf_op jit(solution)/shard_map/ppermute | solution.py:170
  43.9 0.5 %collective-permute-start.25 = (f32[32,128]{1,0:T(8,128)S(1)}, f32[32,128]{1,0:T(8,128)S(1)}, u32[]{:S(2)}, u32[]{:S(2)}) collective-permute-start(f32[32,128]{1,0:T(8,128)S(1)} %collective-permute-done.22.refs_1_), channel_id=1, source_target_pairs={{0,1},{1,0},{2,3},{3,2},{4,5},{5,4},{6,7},{7,6},{8,9},{9,8},{10,11... | collective-permute-start | bytes 49160 | tf_op jit(solution)/shard_map/ppermute | solution.py:167
  44.4 0.8 %collective-permute-done.25.refs_5_ = f32[32,128]{1,0:T(8,128)S(1)} collective-permute-done((f32[32,128]{1,0:T(8,128)S(1)}, f32[32,128]{1,0:T(8,128)S(1)}, u32[]{:S(2)}, u32[]{:S(2)}) %collective-permute-start.25) | collective-permute-done | bytes 16416 | tf_op jit(solution)/shard_map/ppermute | solution.py:167
  45.6 1.4 %shard_map.53 = f32[4,64,128]{2,1,0:T(8,128)} custom-call(s32[6]{0:T(128)S(1)} %stack.27.ids, f32[4,32,128]{2,1,0:T(8,128)S(1)} %get-tuple-element.72.refs_0_, f32[32,128]{1,0:T(8,128)S(1)} %collective-permute-done.22.refs_1_, f32[4,32,128]{2,1,0:T(8,128)S(1)} %collective-permute-done.21.refs_2_, f32[32,128]{1,0:T(8,128)S(1)} %collective-permute-done.23.refs_3_, ...), custom_call_target="tpu_custom_call" | custom-call | bytes 1000 | tf_op jit(solution)/shard_map/pallas_call | solution.py:287
  (55 shorter events, 3.6 us)
Async XLA Ops:
  0.0 1.5 %copy-start = (f32[4,64,128]{2,1,0:T(8,128)S(1)}, f32[4,64,128]{2,1,0:T(8,128)}, u32[]{:S(2)}) copy-start(f32[4,64,128]{2,1,0:T(8,128)} %own_sides.1) | copy-start | bytes 393220
  1.0 1.5 %collective-permute-start = (f32[64,512]{1,0:T(8,128)S(1)}, f32[64,512]{1,0:T(8,128)S(1)}, u32[]{:S(2)}, u32[]{:S(2)}) collective-permute-start(f32[64,512]{1,0:T(8,128)S(1)} %slice_bitcast_fusion.3.own), channel_id=1, source_target_pairs={{0,1},{1,0},{2,3},{3,2},{4,5},{5,4},{6,7},{7,6},{8,9},{9,8},{10,11... | collective-permute-start | bytes 393224 | tf_op jit(solution)/shard_map/ppermute | solution.py:167
  1.5 1.3 %collective-permute-start.1 = (f32[4,64,128]{2,1,0:T(8,128)S(1)}, f32[4,64,128]{2,1,0:T(8,128)S(1)}, u32[]{:S(2)}, u32[]{:S(2)}) collective-permute-start(f32[4,64,128]{2,1,0:T(8,128)S(1)} %copy-done), channel_id=1, source_target_pairs={{0,1},{1,0},{2,3},{3,2},{4,5},{5,4},{6,7},{7,6},{8,9},{9,8},{10,11... | collective-permute-start | bytes 393224 | tf_op jit(solution)/shard_map/ppermute | solution.py:167
  1.6 0.7 %copy-start.3 = (s32[3,1,2]{0,2,1:T(2,128)S(1)}, s32[3,1,2]{0,2,1:T(2,128)}, u32[]{:S(2)}) copy-start(s32[3,1,2]{0,2,1:T(2,128)} %param.7) | copy-start | bytes 76
  2.8 3.7 %copy-start.2 = (f32[3,64,256]{2,1,0:T(8,128)S(1)}, f32[3,64,256]{2,1,0:T(8,128)}, u32[]{:S(2)}) copy-start(f32[3,64,256]{2,1,0:T(8,128)} %param.6) | copy-start | bytes 589828
  3.7 2.9 %copy-start.1 = (f32[4,64,512]{2,1,0:T(8,128)S(1)}, f32[4,64,512]{2,1,0:T(8,128)}, u32[]{:S(2)}) copy-start(f32[4,64,512]{2,1,0:T(8,128)} %param.5) | copy-start | bytes 1572868
  3.7 5.5 %collective-permute-start.2 = (f32[136,128]{1,0:T(8,128)S(1)}, f32[136,128]{1,0:T(8,128)S(1)}, u32[]{:S(2)}, u32[]{:S(2)}) collective-permute-start(f32[136,128]{1,0:T(8,128)S(1)} %get-tuple-element.42), channel_id=1, source_target_pairs={{0,4},{4,0},{8,12},{12,8},{1,5},{5,1},{9,13},{13,9},{2,6},{6,2},{1... | collective-permute-start | bytes 208904 | tf_op jit(solution)/shard_map/ppermute | solution.py:170
  6.6 10.6 %collective-permute-start.4 = (f32[64,896]{1,0:T(8,128)S(1)}, f32[64,896]{1,0:T(8,128)S(1)}, u32[]{:S(2)}, u32[]{:S(2)}) collective-permute-start(f32[64,896]{1,0:T(8,128)S(1)} %pad_maximum_fusion.a0), channel_id=1, source_target_pairs={{0,1},{1,0},{2,3},{3,2},{4,5},{5,4},{6,7},{7,6},{8,9},{9,8},{10,11... | collective-permute-start | bytes 688136 | tf_op jit(solution)/shard_map/ppermute | solution.py:167
  6.7 9.8 %collective-permute-start.5 = (f32[64,896]{1,0:T(8,128)S(1)}, f32[64,896]{1,0:T(8,128)S(1)}, u32[]{:S(2)}, u32[]{:S(2)}) collective-permute-start(f32[64,896]{1,0:T(8,128)S(1)} %pad_maximum_fusion.a0), channel_id=1, source_target_pairs={{0,4},{4,0},{8,12},{12,8},{1,5},{5,1},{9,13},{13,9},{2,6},{6,2},{1... | collective-permute-start | bytes 688136 | tf_op jit(solution)/shard_map/ppermute | solution.py:170
  9.2 6.1 %collective-permute-start.3 = (f32[4,32,128]{2,1,0:T(8,128)S(1)}, f32[4,32,128]{2,1,0:T(8,128)S(1)}, u32[]{:S(2)}, u32[]{:S(2)}) collective-permute-start(f32[4,32,128]{2,1,0:T(8,128)S(1)} %add.15.refs_0_), channel_id=1, source_target_pairs={{0,8},{4,12},{8,0},{12,4},{1,9},{5,13},{9,1},{13,5},{2,10},{6,14},... | collective-permute-start | bytes 196616 | tf_op jit(solution)/shard_map/ppermute | solution.py:170
  12.0 10.3 %collective-permute-start.12 = (f32[64,896]{1,0:T(8,128)S(1)}, f32[64,896]{1,0:T(8,128)S(1)}, u32[]{:S(2)}, u32[]{:S(2)}) collective-permute-start(f32[64,896]{1,0:T(8,128)S(1)} %pad_maximum_fusion.1.a0), channel_id=1, source_target_pairs={{0,4},{4,0},{8,12},{12,8},{1,5},{5,1},{9,13},{13,9},{2,6},{6,2},{1... | collective-permute-start | bytes 688136 | tf_op jit(solution)/shard_map/ppermute | solution.py:170
  16.6 1.3 %collective-permute-start.9 = (f32[16,896]{1,0:T(8,128)S(1)}, f32[16,896]{1,0:T(8,128)S(1)}, u32[]{:S(2)}, u32[]{:S(2)}) collective-permute-start(f32[16,896]{1,0:T(8,128)S(1)} %get-tuple-element.86), channel_id=1, source_target_pairs={{0,1},{1,0},{2,3},{3,2},{4,5},{5,4},{6,7},{7,6},{8,9},{9,8},{10,11... | collective-permute-start | bytes 172040 | tf_op jit(solution)/shard_map/ppermute | solution.py:167
  16.7 1.4 %collective-permute-start.8 = (f32[16,896]{1,0:T(8,128)S(1)}, f32[16,896]{1,0:T(8,128)S(1)}, u32[]{:S(2)}, u32[]{:S(2)}) collective-permute-start(f32[16,896]{1,0:T(8,128)S(1)} %get-tuple-element.87), channel_id=1, source_target_pairs={{0,1},{1,0},{2,3},{3,2},{4,5},{5,4},{6,7},{7,6},{8,9},{9,8},{10,11... | collective-permute-start | bytes 172040 | tf_op jit(solution)/shard_map/ppermute | solution.py:167
  17.2 3.5 %collective-permute-start.7 = (f32[16,896]{1,0:T(8,128)S(1)}, f32[16,896]{1,0:T(8,128)S(1)}, u32[]{:S(2)}, u32[]{:S(2)}) collective-permute-start(f32[16,896]{1,0:T(8,128)S(1)} %get-tuple-element.88), channel_id=1, source_target_pairs={{0,1},{1,0},{2,3},{3,2},{4,5},{5,4},{6,7},{7,6},{8,9},{9,8},{10,11... | collective-permute-start | bytes 172040 | tf_op jit(solution)/shard_map/ppermute | solution.py:167
  17.3 3.4 %collective-permute-start.6 = (f32[16,896]{1,0:T(8,128)S(1)}, f32[16,896]{1,0:T(8,128)S(1)}, u32[]{:S(2)}, u32[]{:S(2)}) collective-permute-start(f32[16,896]{1,0:T(8,128)S(1)} %get-tuple-element.89), channel_id=1, source_target_pairs={{0,1},{1,0},{2,3},{3,2},{4,5},{5,4},{6,7},{7,6},{8,9},{9,8},{10,11... | collective-permute-start | bytes 172040 | tf_op jit(solution)/shard_map/ppermute | solution.py:167
  17.9 6.5 %collective-permute-start.11 = (f32[64,896]{1,0:T(8,128)S(1)}, f32[64,896]{1,0:T(8,128)S(1)}, u32[]{:S(2)}, u32[]{:S(2)}) collective-permute-start(f32[64,896]{1,0:T(8,128)S(1)} %pad_maximum_fusion.1.a0), channel_id=1, source_target_pairs={{0,1},{1,0},{2,3},{3,2},{4,5},{5,4},{6,7},{7,6},{8,9},{9,8},{10,11... | collective-permute-start | bytes 688136 | tf_op jit(solution)/shard_map/ppermute | solution.py:167
  18.1 11.2 %collective-permute-start.19 = (f32[64,896]{1,0:T(8,128)S(1)}, f32[64,896]{1,0:T(8,128)S(1)}, u32[]{:S(2)}, u32[]{:S(2)}) collective-permute-start(f32[64,896]{1,0:T(8,128)S(1)} %pad_maximum_fusion.2.a0), channel_id=1, source_target_pairs={{0,4},{4,0},{8,12},{12,8},{1,5},{5,1},{9,13},{13,9},{2,6},{6,2},{1... | collective-permute-start | bytes 688136 | tf_op jit(solution)/shard_map/ppermute | solution.py:170
  22.4 2.4 %collective-permute-start.16 = (f32[16,896]{1,0:T(8,128)S(1)}, f32[16,896]{1,0:T(8,128)S(1)}, u32[]{:S(2)}, u32[]{:S(2)}) collective-permute-start(f32[16,896]{1,0:T(8,128)S(1)} %get-tuple-element.82), channel_id=1, source_target_pairs={{0,1},{1,0},{2,3},{3,2},{4,5},{5,4},{6,7},{7,6},{8,9},{9,8},{10,11... | collective-permute-start | bytes 172040 | tf_op jit(solution)/shard_map/ppermute | solution.py:167
  22.5 5.8 %collective-permute-start.10 = (f32[4,32,128]{2,1,0:T(8,128)S(1)}, f32[4,32,128]{2,1,0:T(8,128)S(1)}, u32[]{:S(2)}, u32[]{:S(2)}) collective-permute-start(f32[4,32,128]{2,1,0:T(8,128)S(1)} %get-tuple-element.55.refs_1_), channel_id=1, source_target_pairs={{0,8},{4,12},{8,0},{12,4},{1,9},{5,13},{9,1},{13,5},{2,10},{6,14},... | collective-permute-start | bytes 196616 | tf_op jit(solution)/shard_map/ppermute | solution.py:170
  24.2 1.2 %collective-permute-start.15 = (f32[16,896]{1,0:T(8,128)S(1)}, f32[16,896]{1,0:T(8,128)S(1)}, u32[]{:S(2)}, u32[]{:S(2)}) collective-permute-start(f32[16,896]{1,0:T(8,128)S(1)} %get-tuple-element.83), channel_id=1, source_target_pairs={{0,1},{1,0},{2,3},{3,2},{4,5},{5,4},{6,7},{7,6},{8,9},{9,8},{10,11... | collective-permute-start | bytes 172040 | tf_op jit(solution)/shard_map/ppermute | solution.py:167
  24.4 1.2 %collective-permute-start.14 = (f32[16,896]{1,0:T(8,128)S(1)}, f32[16,896]{1,0:T(8,128)S(1)}, u32[]{:S(2)}, u32[]{:S(2)}) collective-permute-start(f32[16,896]{1,0:T(8,128)S(1)} %get-tuple-element.84), channel_id=1, source_target_pairs={{0,1},{1,0},{2,3},{3,2},{4,5},{5,4},{6,7},{7,6},{8,9},{9,8},{10,11... | collective-permute-start | bytes 172040 | tf_op jit(solution)/shard_map/ppermute | solution.py:167
  24.8 1.2 %collective-permute-start.13 = (f32[16,896]{1,0:T(8,128)S(1)}, f32[16,896]{1,0:T(8,128)S(1)}, u32[]{:S(2)}, u32[]{:S(2)}) collective-permute-start(f32[16,896]{1,0:T(8,128)S(1)} %get-tuple-element.85), channel_id=1, source_target_pairs={{0,1},{1,0},{2,3},{3,2},{4,5},{5,4},{6,7},{7,6},{8,9},{9,8},{10,11... | collective-permute-start | bytes 172040 | tf_op jit(solution)/shard_map/ppermute | solution.py:167
  25.5 6.4 %collective-permute-start.18 = (f32[64,896]{1,0:T(8,128)S(1)}, f32[64,896]{1,0:T(8,128)S(1)}, u32[]{:S(2)}, u32[]{:S(2)}) collective-permute-start(f32[64,896]{1,0:T(8,128)S(1)} %pad_maximum_fusion.2.a0), channel_id=1, source_target_pairs={{0,1},{1,0},{2,3},{3,2},{4,5},{5,4},{6,7},{7,6},{8,9},{9,8},{10,11... | collective-permute-start | bytes 688136 | tf_op jit(solution)/shard_map/ppermute | solution.py:167
  29.2 2.7 %collective-permute-start.20 = (f32[64,896]{1,0:T(8,128)S(1)}, f32[64,896]{1,0:T(8,128)S(1)}, u32[]{:S(2)}, u32[]{:S(2)}) collective-permute-start(f32[64,896]{1,0:T(8,128)S(1)} %collective-permute-done.19.a2), channel_id=1, source_target_pairs={{0,1},{1,0},{2,3},{3,2},{4,5},{5,4},{6,7},{7,6},{8,9},{9,8},{10,11... | collective-permute-start | bytes 688136 | tf_op jit(solution)/shard_map/ppermute | solution.py:167
  29.3 6.8 %collective-permute-start.17 = (f32[4,32,128]{2,1,0:T(8,128)S(1)}, f32[4,32,128]{2,1,0:T(8,128)S(1)}, u32[]{:S(2)}, u32[]{:S(2)}) collective-permute-start(f32[4,32,128]{2,1,0:T(8,128)S(1)} %get-tuple-element.64.refs_1_), channel_id=1, source_target_pairs={{0,8},{4,12},{8,0},{12,4},{1,9},{5,13},{9,1},{13,5},{2,10},{6,14},... | collective-permute-start | bytes 196616 | tf_op jit(solution)/shard_map/ppermute | solution.py:170
  37.1 6.8 %collective-permute-start.21 = (f32[4,32,128]{2,1,0:T(8,128)S(1)}, f32[4,32,128]{2,1,0:T(8,128)S(1)}, u32[]{:S(2)}, u32[]{:S(2)}) collective-permute-start(f32[4,32,128]{2,1,0:T(8,128)S(1)} %get-tuple-element.73), channel_id=1, source_target_pairs={{0,4},{4,0},{8,12},{12,8},{1,5},{5,1},{9,13},{13,9},{2,6},{6,2},{1... | collective-permute-start | bytes 196616 | tf_op jit(solution)/shard_map/ppermute | solution.py:170
  37.5 4.6 %collective-permute-start.22 = (f32[32,128]{1,0:T(8,128)S(1)}, f32[32,128]{1,0:T(8,128)S(1)}, u32[]{:S(2)}, u32[]{:S(2)}) collective-permute-start(f32[32,128]{1,0:T(8,128)S(1)} %get-tuple-element.74), channel_id=1, source_target_pairs={{0,8},{4,12},{8,0},{12,4},{1,9},{5,13},{9,1},{13,5},{2,10},{6,14},... | collective-permute-start | bytes 49160 | tf_op jit(solution)/shard_map/ppermute | solution.py:170
  38.3 5.5 %collective-permute-start.23 = (f32[32,128]{1,0:T(8,128)S(1)}, f32[32,128]{1,0:T(8,128)S(1)}, u32[]{:S(2)}, u32[]{:S(2)}) collective-permute-start(f32[32,128]{1,0:T(8,128)S(1)} %get-tuple-element.75), channel_id=1, source_target_pairs={{0,12},{4,8},{8,4},{12,0},{1,13},{5,9},{9,5},{13,1},{2,14},{6,10},... | collective-permute-start | bytes 49160 | tf_op jit(solution)/shard_map/ppermute | solution.py:170
  41.5 2.8 %collective-permute-start.24 = (f32[4,32,128]{2,1,0:T(8,128)S(1)}, f32[4,32,128]{2,1,0:T(8,128)S(1)}, u32[]{:S(2)}, u32[]{:S(2)}) collective-permute-start(f32[4,32,128]{2,1,0:T(8,128)S(1)} %get-tuple-element.72.refs_0_), channel_id=1, source_target_pairs={{0,1},{1,0},{2,3},{3,2},{4,5},{5,4},{6,7},{7,6},{8,9},{9,8},{10,11... | collective-permute-start | bytes 196616 | tf_op jit(solution)/shard_map/ppermute | solution.py:167
  43.9 1.7 %collective-permute-start.26 = (f32[4,32,128]{2,1,0:T(8,128)S(1)}, f32[4,32,128]{2,1,0:T(8,128)S(1)}, u32[]{:S(2)}, u32[]{:S(2)}) collective-permute-start(f32[4,32,128]{2,1,0:T(8,128)S(1)} %collective-permute-done.21.refs_2_), channel_id=1, source_target_pairs={{0,1},{1,0},{2,3},{3,2},{4,5},{5,4},{6,7},{7,6},{8,9},{9,8},{10,11... | collective-permute-start | bytes 196616 | tf_op jit(solution)/shard_map/ppermute | solution.py:167
  43.9 1.3 %collective-permute-start.25 = (f32[32,128]{1,0:T(8,128)S(1)}, f32[32,128]{1,0:T(8,128)S(1)}, u32[]{:S(2)}, u32[]{:S(2)}) collective-permute-start(f32[32,128]{1,0:T(8,128)S(1)} %collective-permute-done.22.refs_1_), channel_id=1, source_target_pairs={{0,1},{1,0},{2,3},{3,2},{4,5},{5,4},{6,7},{7,6},{8,9},{9,8},{10,11... | collective-permute-start | bytes 49160 | tf_op jit(solution)/shard_map/ppermute | solution.py:167
  44.4 1.2 %collective-permute-start.27 = (f32[32,128]{1,0:T(8,128)S(1)}, f32[32,128]{1,0:T(8,128)S(1)}, u32[]{:S(2)}, u32[]{:S(2)}) collective-permute-start(f32[32,128]{1,0:T(8,128)S(1)} %collective-permute-done.23.refs_3_), channel_id=1, source_target_pairs={{0,1},{1,0},{2,3},{3,2},{4,5},{5,4},{6,7},{7,6},{8,9},{9,8},{10,11... | collective-permute-start | bytes 49160 | tf_op jit(solution)/shard_map/ppermute | solution.py:167

commit v5 on v4

--- a/solution.py
+++ b/solution.py
@@ -7,7 +7,7 @@
 from jax.experimental.pallas import tpu as pltpu
 from jax.sharding import PartitionSpec as P
 
-K = {'first': 0.3, 'prep': [2, 0, 0], 'step': [0, 0.1, 0], 'bulk': ['send', 'share0', 'share0'], 'swap': ['recv0', 'share1', 'share2'], 'rest': ['send', 'send', 'send'], 'groups': [[1], [2], [3]], 'meet': 1, 'early': 0, 'cut': [4, 4, 1]}
+K = {'first': 0.3, 'prep': [2, 0, 0], 'step': [0, 0.1, 0], 'bulk': ['send', 'share0', 'share0'], 'swap': ['recv0', 'share1', 'share2'], 'rest': ['send', 'send', 'send'], 'groups': [[1], [2], [3]], 'meet': 0, 'early': 2, 'cut': [4, 4, 1]}
 S = 4
 BS = 128
 LANES = 128
@@ -46,7 +46,7 @@
     blocks = own.shape[1] // BS
     turned[...] = jnp.concatenate([own_sides[0], other_sides[0]], axis=0).T
     sides = turned[pl.ds(pl.multiple_of(ids[0] * 2 * quarter, 2 * quarter), 2 * quarter), :]
-    high, low = split(jnp.concatenate([own[...], other[...]], axis=0))
+    high, low = split(jnp.concatenate([own[...], other[0]], axis=0))
     share = product(sides, high, low)
     for i in range(blocks):
         terms[i] = share[:, i * BS : (i + 1) * BS]
@@ -103,6 +103,12 @@
         share[i] = result[:, i * BS : (i + 1) * BS]
 
 
+def whole_step_kernel(quarter, place, t, pieces, ids, lists, told, *refs):
+    taken, rest, between = refs[: 3 + pieces], refs[3 + pieces : -6], refs[-6:]
+    prepare_kernel(quarter, place, ids, *taken, *between)
+    step_kernel(t, lists, told, *rest[:-2], *between[:-1], *rest[-2:])
+
+
 def early_kernel(ids, solved, own, near):
     blocks = solved.shape[0] // own.shape[0]
     for t in range(own.shape[0]):
@@ -147,7 +153,7 @@
             parts = [quarters[2 * i][t - first] for i in range(4)]
         if t == S - 1:
             parts = [part + quarters[2 * i + 1][...] for i, part in enumerate(parts)]
-        out[t] = place(quarter, ids, parts, whole)
+        out[t] = place(quarter, ids, parts, whole.at[t])
 
 
 def body(count, right_sides, diag_inverse, factor_below, block_lists):
@@ -183,16 +189,18 @@
             bit *= 2
         return a, to_row(a, top)
 
+    ready_shapes = (
+        shape((2 * BS, width), bf16),
+        shape((2 * BS, width), bf16),
+        shape((2, depth, BS), bf16),
+        shape((2, depth, BS), bf16),
+        shape((2, quarter, BS), f32),
+    )
+
     def prepare(t, place, own, own_core, other, other_core):
         return call(
             functools.partial(prepare_kernel, quarter, place),
-            (
-                shape((2 * BS, width), bf16),
-                shape((2 * BS, width), bf16),
-                shape((2, depth, BS), bf16),
-                shape((2, depth, BS), bf16),
-                shape((2, quarter, BS), f32),
-            ),
+            ready_shapes,
             [pltpu.VMEM((4 * quarter, BS), f32)],
             K["prep"][t - 1],
         )(in_specs=[SMEM] + [VMEM] * (3 + len(other_core)))(ids, own, own_core, other, *other_core)
@@ -204,7 +212,7 @@
         [pltpu.VMEM((4 * quarter, BS), f32), pltpu.VMEM((blocks, 2 * quarter, BS), f32)],
         K["first"],
     )(in_specs=[SMEM, SMEM, VMEM, VMEM, VMEM, VMEM])(
-        ids, block_lists, diag_first, to_core(diag_first), right_sides, to_core(right_sides)
+        ids, block_lists, diag_first, to_core(diag_inverse), right_sides, to_core(right_sides)
     )
     got = to_row(send, 1)
 
@@ -244,6 +252,19 @@
             other_cores[u] = [to_core(gated[i : i + rows]) for i in range(0, gated.shape[0], rows)]
         gates[f"other{t}"] = other_cores[u][-1]
         bulk()
+        if t == 1 and top == 2:
+            pieces = other_cores[u]
+            operands = (rest[u], rest_core[u], others[u], *pieces, keep, recv)
+            kernel = functools.partial(whole_step_kernel, quarter, groups[u].index(t), t, len(pieces))
+            solved, share = call(
+                kernel,
+                (shape((blocks, quarter, BS), f32), piece),
+                [pltpu.VMEM(a.shape, a.dtype) for a in ready_shapes] + [pltpu.VMEM((4 * quarter, BS), f32)],
+                K["step"][0],
+            )(in_specs=[SMEM] * 3 + [VMEM] * len(operands))(ids, block_lists, told, *operands)
+            stored = (solved,)
+            gates["share1"] = share
+            continue
         ready = prepare(t, groups[u].index(t), rest[u], rest_core[u], others[u], other_cores[u])
         operands = (*stored, keep, recv, *ready)
         gates[f"prep{t}"] = operands[-1]
@@ -287,7 +308,7 @@
     return call(
         functools.partial(place_kernel, quarter, first),
         shape((S, BS // 2, 4 * quarter), f32),
-        [pltpu.VMEM((4 * quarter, BS), f32)],
+        [pltpu.VMEM((S, 4 * quarter, BS), f32)],
     )(in_specs=[SMEM] + [VMEM] * len(quarters))(ids, *quarters)
 
 

time: 47.1 us -> 46.9 us (level)
  waiting for transfers between devices: 13.8 us -> 11.9 us
  starting transfers between devices: 23.6 us -> 25.3 us
    ppermute x10 -> x11, starting transfers between devices: 20.1 us -> 21.7 us  [to_row(): return lax.ppermute(a, 'row', [(i, i ^ bit) for i in range(count)])]
    ppermute x10 -> x11, waiting for transfers between devices: 11.2 us -> 9.58 us  [to_row(): return lax.ppermute(a, 'row', [(i, i ^ bit) for i in range(count)])]
    pallas_call x2 -> x1, Pallas kernels: 1.83 us -> 0.91 us  [body(): call(functools.partial(step_kernel, t), (solved_shape, piece), (), K['ste...]
    pallas_call x3 -> x4, Pallas kernels: 2.3 us -> 3.14 us  [the longest x2 1.54 us: prepare(): call(functools.partial(prepare_kernel, quarter, place), ready_shapes, [pl...]
    ppermute x18 -> x20, waiting for transfers between devices: 2.63 us -> 2.29 us  [to_core(): return lax.ppermute(a, 'sub', [(0, 1), (1, 0)])]
    ppermute x18 -> x20, starting transfers between devices: 3.52 us -> 3.62 us  [to_core(): return lax.ppermute(a, 'sub', [(0, 1), (1, 0)])]
  transfers between devices with their start and end apart: 28 -> 31, of which waited for: 13 -> 12; matrix products, arithmetic and copies ran while one was open for 1% -> 3% of each run, Pallas kernels for 9% -> 11%
where the time goes in v5:
time: 46.9 us; the launch traced here: 46.7 us
  starting transfers between devices  25.3 us (54%)
  waiting for transfers between devices  11.9 us (25%)
  Pallas kernels  7.26 us (15%)
  local copies, waits for them, and re-layouts  1.99 us (4%)
    ppermute x11, starting transfers between devices, to_row(): return lax.ppermute(a, 'row', [(i, i ^ bit) for i in range(count)])  21.7 us
    ppermute x11, waiting for transfers between devices, to_row(): return lax.ppermute(a, 'row', [(i, i ^ bit) for i in range(count)])  9.58 us
    ppermute x20, starting transfers between devices, to_core(): return lax.ppermute(a, 'sub', [(0, 1), (1, 0)])  3.62 us
    ppermute x20, waiting for transfers between devices, to_core(): return lax.ppermute(a, 'sub', [(0, 1), (1, 0)])  2.29 us
    pallas_call x2, Pallas kernels, prepare(): call(functools.partial(prepare_kernel, quarter, place), ready_shapes, [pl...  1.54 us
    pallas_call x1, Pallas kernels, body(): call(functools.partial(place_kernel, quarter, first), shape((S, BS // 2,...  1.41 us
    pallas_call x1, Pallas kernels, body(): call(kernel, (shape((blocks, quarter, BS), f32), piece), [pltpu.VMEM(a.sh...  1.05 us
    squeeze x1, local copies, waits for them, and re-layouts, body(): diag_first = diag_inverse[0]  0.95 us
  transfers between devices with their start and end apart: 31, of which 12 were waited for; matrix products, arithmetic and copies ran while one was open for 3% of the time, Pallas kernels for 11%

profile of v5, /device:TPU:0, one launch (start us, length us, event | category | flops | bytes accessed | tf_op | source)
XLA Modules:
  0.0 46.7 jit_solution(3295271527505996864)
XLA Ops:
  0.0 0.5 collective-permute-start
  0.5 0.7 %copy-done.3 = s32[3,1,2]{0,2,1:T(2,128)S(1)} copy-done((s32[3,1,2]{0,2,1:T(2,128)S(1)}, s32[3,1,2]{0,2,1:T(2,128)}, u32[]{:S(2)}) %copy-start.3) | copy-done | bytes 48
  1.4 1.0 %slice_bitcast_fusion.3.own = f32[64,512]{1,0:T(8,128)S(1)} fusion(f32[4,64,512]{2,1,0:T(8,128)} %param.5), kind=kLoop, calls=%fused_computation.6 | loop fusion | bytes 262144 | tf_op jit(solution)/shard_map/squeeze | solution.py:208
  2.4 0.8 %shard_map.46 = (f32[4,32,128]{2,1,0:T(8,128)S(1)}, f32[136,128]{1,0:T(8,128)S(1)}) custom-call(s32[6]{0:T(128)S(1)} %stack.27.ids, s32[3,1,2]{2,1,0:T(1,128)S(1)} %copy.12.lists, f32[64,512]{1,0:T(8,128)S(1)} %slice_bitcast_fusion.3.own, f32[4,64,512]{2,1,0:T(8,128)S(1)} %collective-permute-done.other, f32[4,64,128]{2,1,0:T(8,128)S(1)} %copy-done, ...), custom_call_target="tpu_custom_call" | custom-call | flops 300000000 | bytes 1000 | tf_op jit(solution)/shard_map/pallas_call | solution.py:209
  3.3 3.1 %collective-permute-start.2 = (f32[136,128]{1,0:T(8,128)S(1)}, f32[136,128]{1,0:T(8,128)S(1)}, u32[]{:S(2)}, u32[]{:S(2)}) collective-permute-start(f32[136,128]{1,0:T(8,128)S(1)} %get-tuple-element.36), channel_id=1, source_target_pairs={{0,4},{4,0},{8,12},{12,8},{1,5},{5,1},{9,13},{13,9},{2,6},{6,2},{1... | collective-permute-start | bytes 208904 | tf_op jit(solution)/shard_map/ppermute | solution.py:176
  6.5 1.0 %collective-permute-start.4 = (f32[64,896]{1,0:T(8,128)S(1)}, f32[64,896]{1,0:T(8,128)S(1)}, u32[]{:S(2)}, u32[]{:S(2)}) collective-permute-start(f32[64,896]{1,0:T(8,128)S(1)} %pad_maximum_fusion.refs_0_), channel_id=1, source_target_pairs={{0,4},{4,0},{8,12},{12,8},{1,5},{5,1},{9,13},{13,9},{2,6},{6,2},{1... | collective-permute-start | bytes 688136 | tf_op jit(solution)/shard_map/ppermute | solution.py:176
  7.5 1.2 %collective-permute-done.2 = f32[136,128]{1,0:T(8,128)S(1)} collective-permute-done((f32[136,128]{1,0:T(8,128)S(1)}, f32[136,128]{1,0:T(8,128)S(1)}, u32[]{:S(2)}, u32[]{:S(2)}) %collective-permute-start.2) | collective-permute-done | bytes 69664 | tf_op jit(solution)/shard_map/ppermute | solution.py:176
  8.8 2.9 %collective-permute-start.5 = (f32[4,32,128]{2,1,0:T(8,128)S(1)}, f32[4,32,128]{2,1,0:T(8,128)S(1)}, u32[]{:S(2)}, u32[]{:S(2)}) collective-permute-start(f32[4,32,128]{2,1,0:T(8,128)S(1)} %add.15.refs_7_), channel_id=1, source_target_pairs={{0,8},{4,12},{8,0},{12,4},{1,9},{5,13},{9,1},{13,5},{2,10},{6,14},... | collective-permute-start | bytes 196616 | tf_op jit(solution)/shard_map/ppermute | solution.py:176
  11.8 1.8 %collective-permute-start.12 = (f32[64,896]{1,0:T(8,128)S(1)}, f32[64,896]{1,0:T(8,128)S(1)}, u32[]{:S(2)}, u32[]{:S(2)}) collective-permute-start(f32[64,896]{1,0:T(8,128)S(1)} %pad_maximum_fusion.1.a0), channel_id=1, source_target_pairs={{0,4},{4,0},{8,12},{12,8},{1,5},{5,1},{9,13},{13,9},{2,6},{6,2},{1... | collective-permute-start | bytes 688136 | tf_op jit(solution)/shard_map/ppermute | solution.py:176
  13.5 1.3 %collective-permute-done.5.refs_8_ = f32[4,32,128]{2,1,0:T(8,128)S(1)} collective-permute-done((f32[4,32,128]{2,1,0:T(8,128)S(1)}, f32[4,32,128]{2,1,0:T(8,128)S(1)}, u32[]{:S(2)}, u32[]{:S(2)}) %collective-permute-start.5) | collective-permute-done | bytes 65568 | tf_op jit(solution)/shard_map/ppermute | solution.py:176
  14.9 1.5 %collective-permute-done.4.refs_2_ = f32[64,896]{1,0:T(8,128)S(1)} collective-permute-done((f32[64,896]{1,0:T(8,128)S(1)}, f32[64,896]{1,0:T(8,128)S(1)}, u32[]{:S(2)}, u32[]{:S(2)}) %collective-permute-start.4) | collective-permute-done | bytes 229408 | tf_op jit(solution)/shard_map/ppermute | solution.py:176
  16.5 0.5 %collective-permute-start.8 = (f32[16,896]{1,0:T(8,128)S(1)}, f32[16,896]{1,0:T(8,128)S(1)}, u32[]{:S(2)}, u32[]{:S(2)}) collective-permute-start(f32[16,896]{1,0:T(8,128)S(1)} %get-tuple-element.75), channel_id=1, source_target_pairs={{0,1},{1,0},{2,3},{3,2},{4,5},{5,4},{6,7},{7,6},{8,9},{9,8},{10,11... | collective-permute-start | bytes 172040 | tf_op jit(solution)/shard_map/ppermute | solution.py:173
  17.9 2.6 %collective-permute-start.19 = (f32[64,896]{1,0:T(8,128)S(1)}, f32[64,896]{1,0:T(8,128)S(1)}, u32[]{:S(2)}, u32[]{:S(2)}) collective-permute-start(f32[64,896]{1,0:T(8,128)S(1)} %pad_maximum_fusion.2.a0), channel_id=1, source_target_pairs={{0,4},{4,0},{8,12},{12,8},{1,5},{5,1},{9,13},{13,9},{2,6},{6,2},{1... | collective-permute-start | bytes 688136 | tf_op jit(solution)/shard_map/ppermute | solution.py:176
  20.5 1.1 %shard_map.47 = (f32[4,32,128]{2,1,0:T(8,128)S(1)}, f32[4,32,128]{2,1,0:T(8,128)S(1)}) custom-call(s32[6]{0:T(128)S(1)} %stack.27.ids, s32[3,1,2]{2,1,0:T(1,128)S(1)} %copy.12.lists, s32[3,2]{1,0:T(4,128)S(1)} %convert_element_type.6.told, f32[64,896]{1,0:T(8,128)S(1)} %pad_maximum_fusion.refs_0_, f32[64,896]{1,0:T(8,128)S(1)} %collective-permute-done.3.refs_1_, ...), custom_call_target="tpu_custom_call" | custom-call | bytes 1000 | tf_op jit(solution)/shard_map/pallas_call | solution.py:259
  21.7 2.4 %collective-permute-start.10 = (f32[4,32,128]{2,1,0:T(8,128)S(1)}, f32[4,32,128]{2,1,0:T(8,128)S(1)}, u32[]{:S(2)}, u32[]{:S(2)}) collective-permute-start(f32[4,32,128]{2,1,0:T(8,128)S(1)} %get-tuple-element.44.refs_1_), channel_id=1, source_target_pairs={{0,8},{4,12},{8,0},{12,4},{1,9},{5,13},{9,1},{13,5},{2,10},{6,14},... | collective-permute-start | bytes 196616 | tf_op jit(solution)/shard_map/ppermute | solution.py:176
  24.7 0.6 %collective-permute-done.15.refs_2_ = f32[16,896]{1,0:T(8,128)S(1)} collective-permute-done((f32[16,896]{1,0:T(8,128)S(1)}, f32[16,896]{1,0:T(8,128)S(1)}, u32[]{:S(2)}, u32[]{:S(2)}) %collective-permute-start.15) | collective-permute-done | bytes 57376 | tf_op jit(solution)/shard_map/ppermute | solution.py:173
  25.8 0.8 %shard_map.48 = (bf16[256,512]{1,0:T(8,128)(2,1)S(1)}, bf16[256,512]{1,0:T(8,128)(2,1)S(1)}, bf16[2,256,128]{2,1,0:T(8,128)(2,1)S(1)}, bf16[2,256,128]{2,1,0:T(8,128)(2,1)S(1)}, f32[2,32,128]{2,1,0:T(8,128)S(1)}) custom-call(s32[6]{0:T(128)S(1)} %stack.27.ids, f32[64,896]{1,0:T(8,128)S(1)} %pad_maximum_fusion.1.a0, ...), custom_call_target="tpu_custom_call" | custom-call | bytes 1000 | tf_op jit(solution)/shard_map/pallas_call | solution.py:201
  26.6 0.7 %collective-permute-done.10.refs_2_ = f32[4,32,128]{2,1,0:T(8,128)S(1)} collective-permute-done((f32[4,32,128]{2,1,0:T(8,128)S(1)}, f32[4,32,128]{2,1,0:T(8,128)S(1)}, u32[]{:S(2)}, u32[]{:S(2)}) %collective-permute-start.10) | collective-permute-done | bytes 65568 | tf_op jit(solution)/shard_map/ppermute | solution.py:176
  27.3 0.9 %shard_map.49 = (f32[8,32,128]{2,1,0:T(8,128)S(1)}, f32[4,32,128]{2,1,0:T(8,128)S(1)}) custom-call(s32[3,1,2]{2,1,0:T(1,128)S(1)} %copy.12.lists, s32[3,2]{1,0:T(4,128)S(1)} %convert_element_type.6.told, f32[4,32,128]{2,1,0:T(8,128)S(1)} %get-tuple-element.43.refs_0_, f32[4,32,128]{2,1,0:T(8,128)S(1)} %get-tuple-element.44.refs_1_, ...), custom_call_target="tpu_custom_call" | custom-call | flops 100000000 | bytes 1000 | tf_op jit(solution)/shard_map/pallas_call | solution.py:274
  28.3 3.4 %collective-permute-start.17 = (f32[4,32,128]{2,1,0:T(8,128)S(1)}, f32[4,32,128]{2,1,0:T(8,128)S(1)}, u32[]{:S(2)}, u32[]{:S(2)}) collective-permute-start(f32[4,32,128]{2,1,0:T(8,128)S(1)} %get-tuple-element.53.refs_1_), channel_id=1, source_target_pairs={{0,8},{4,12},{8,0},{12,4},{1,9},{5,13},{9,1},{13,5},{2,10},{6,14},... | collective-permute-start | bytes 196616 | tf_op jit(solution)/shard_map/ppermute | solution.py:176
  31.7 0.5 %shard_map.52 = (f32[2,32,128]{2,1,0:T(8,128)S(1)}, f32[2,32,128]{2,1,0:T(8,128)S(1)}) custom-call(s32[6]{0:T(128)S(1)} %stack.27.ids, f32[8,32,128]{2,1,0:T(8,128)S(1)} %get-tuple-element.52.refs_0_.solved), custom_call_target="tpu_custom_call" | custom-call | bytes 1000 | tf_op jit(solution)/shard_map/pallas_call | solution.py:281
  32.6 0.8 %shard_map.50 = (bf16[256,512]{1,0:T(8,128)(2,1)S(1)}, bf16[256,512]{1,0:T(8,128)(2,1)S(1)}, bf16[2,256,128]{2,1,0:T(8,128)(2,1)S(1)}, bf16[2,256,128]{2,1,0:T(8,128)(2,1)S(1)}, f32[2,32,128]{2,1,0:T(8,128)S(1)}) custom-call(s32[6]{0:T(128)S(1)} %stack.27.ids, f32[64,896]{1,0:T(8,128)S(1)} %pad_maximum_fusion.2.a0, ...), custom_call_target="tpu_custom_call" | custom-call | bytes 1000 | tf_op jit(solution)/shard_map/pallas_call | solution.py:201
  33.4 2.1 %collective-permute-done.17.refs_2_ = f32[4,32,128]{2,1,0:T(8,128)S(1)} collective-permute-done((f32[4,32,128]{2,1,0:T(8,128)S(1)}, f32[4,32,128]{2,1,0:T(8,128)S(1)}, u32[]{:S(2)}, u32[]{:S(2)}) %collective-permute-start.17) | collective-permute-done | bytes 65568 | tf_op jit(solution)/shard_map/ppermute | solution.py:176
  35.5 0.9 %shard_map.51 = (f32[2,32,128]{2,1,0:T(8,128)S(1)}, f32[2,32,128]{2,1,0:T(8,128)S(1)}, f32[32,128]{1,0:T(8,128)S(1)}, f32[32,128]{1,0:T(8,128)S(1)}) custom-call(s32[6]{0:T(128)S(1)} %stack.27.ids, s32[3,1,2]{2,1,0:T(1,128)S(1)} %copy.12.lists, s32[3,2]{1,0:T(4,128)S(1)} %convert_element_type.6.told, f32[8,32,128]{2,1,0:T(8,128)S(1)} %get-tuple-element.52.refs_0_.solved, ...), custom_call_target="tpu_custom_call" | custom-call | bytes 1000 | tf_op jit(solution)/shard_map/pallas_call | solution.py:295
  36.5 1.1 %collective-permute-start.22 = (f32[2,32,128]{2,1,0:T(8,128)S(1)}, f32[2,32,128]{2,1,0:T(8,128)S(1)}, u32[]{:S(2)}, u32[]{:S(2)}) collective-permute-start(f32[2,32,128]{2,1,0:T(8,128)S(1)} %get-tuple-element.63), channel_id=1, source_target_pairs={{0,4},{4,0},{8,12},{12,8},{1,5},{5,1},{9,13},{13,9},{2,6},{6,2},{1... | collective-permute-start | bytes 98312 | tf_op jit(solution)/shard_map/ppermute | solution.py:176
  37.6 1.0 %collective-permute-start.21 = (f32[32,128]{1,0:T(8,128)S(1)}, f32[32,128]{1,0:T(8,128)S(1)}, u32[]{:S(2)}, u32[]{:S(2)}) collective-permute-start(f32[32,128]{1,0:T(8,128)S(1)} %get-tuple-element.62), channel_id=1, source_target_pairs={{0,8},{4,12},{8,0},{12,4},{1,9},{5,13},{9,1},{13,5},{2,10},{6,14},... | collective-permute-start | bytes 49160 | tf_op jit(solution)/shard_map/ppermute | solution.py:176
  38.6 2.3 %collective-permute-start.23 = (f32[32,128]{1,0:T(8,128)S(1)}, f32[32,128]{1,0:T(8,128)S(1)}, u32[]{:S(2)}, u32[]{:S(2)}) collective-permute-start(f32[32,128]{1,0:T(8,128)S(1)} %get-tuple-element.64), channel_id=1, source_target_pairs={{0,12},{4,8},{8,4},{12,0},{1,13},{5,9},{9,5},{13,1},{2,14},{6,10},... | collective-permute-start | bytes 49160 | tf_op jit(solution)/shard_map/ppermute | solution.py:176
  40.9 0.5 %collective-permute-start.26 = (f32[2,32,128]{2,1,0:T(8,128)S(1)}, f32[2,32,128]{2,1,0:T(8,128)S(1)}, u32[]{:S(2)}, u32[]{:S(2)}) collective-permute-start(f32[2,32,128]{2,1,0:T(8,128)S(1)} %collective-permute-done.22.refs_2_), channel_id=1, source_target_pairs={{0,1},{1,0},{2,3},{3,2},{4,5},{5,4},{6,7},{7,6},{8,9},{9,8},{10,11... | collective-permute-start | bytes 98312 | tf_op jit(solution)/shard_map/ppermute | solution.py:173
  41.4 0.9 %collective-permute-done.21.refs_1_ = f32[32,128]{1,0:T(8,128)S(1)} collective-permute-done((f32[32,128]{1,0:T(8,128)S(1)}, f32[32,128]{1,0:T(8,128)S(1)}, u32[]{:S(2)}, u32[]{:S(2)}) %collective-permute-start.21) | collective-permute-done | bytes 16416 | tf_op jit(solution)/shard_map/ppermute | solution.py:176
  42.4 1.8 %collective-permute-done.23.refs_3_ = f32[32,128]{1,0:T(8,128)S(1)} collective-permute-done((f32[32,128]{1,0:T(8,128)S(1)}, f32[32,128]{1,0:T(8,128)S(1)}, u32[]{:S(2)}, u32[]{:S(2)}) %collective-permute-start.23) | collective-permute-done | bytes 16416 | tf_op jit(solution)/shard_map/ppermute | solution.py:176
  44.1 1.2 %collective-permute-done.27.refs_7_ = f32[32,128]{1,0:T(8,128)S(1)} collective-permute-done((f32[32,128]{1,0:T(8,128)S(1)}, f32[32,128]{1,0:T(8,128)S(1)}, u32[]{:S(2)}, u32[]{:S(2)}) %collective-permute-start.27) | collective-permute-done | bytes 16416 | tf_op jit(solution)/shard_map/ppermute | solution.py:173
  45.3 1.4 %shard_map.53 = f32[4,64,128]{2,1,0:T(8,128)} custom-call(s32[6]{0:T(128)S(1)} %stack.27.ids, f32[2,32,128]{2,1,0:T(8,128)S(1)} %get-tuple-element.61.refs_0_, f32[32,128]{1,0:T(8,128)S(1)} %collective-permute-done.21.refs_1_, f32[2,32,128]{2,1,0:T(8,128)S(1)} %collective-permute-done.22.refs_2_, f32[32,128]{1,0:T(8,128)S(1)} %collective-permute-done.23.refs_3_, ...), custom_call_target="tpu_custom_call" | custom-call | bytes 1000 | tf_op jit(solution)/shard_map/pallas_call | solution.py:308
  (61 shorter events, 3.3 us)
Async XLA Ops:
  0.0 2.4 %collective-permute-start = (f32[4,64,512]{2,1,0:T(8,128)}, f32[4,64,512]{2,1,0:T(8,128)S(1)}, u32[]{:S(2)}, u32[]{:S(2)}) collective-permute-start(f32[4,64,512]{2,1,0:T(8,128)} %param.5), channel_id=1, source_target_pairs={{0,1},{1,0},{2,3},{3,2},{4,5},{5,4},{6,7},{7,6},{8,9},{9,8},{10,11... | collective-permute-start | bytes 1572872 | tf_op jit(solution)/shard_map/ppermute | solution.py:173
  0.5 1.9 %collective-permute-start.1 = (f32[4,64,128]{2,1,0:T(8,128)}, f32[4,64,128]{2,1,0:T(8,128)S(1)}, u32[]{:S(2)}, u32[]{:S(2)}) collective-permute-start(f32[4,64,128]{2,1,0:T(8,128)} %own_sides.1), channel_id=1, source_target_pairs={{0,1},{1,0},{2,3},{3,2},{4,5},{5,4},{6,7},{7,6},{8,9},{9,8},{10,11... | collective-permute-start | bytes 393224 | tf_op jit(solution)/shard_map/ppermute | solution.py:173
  2.4 3.9 %copy-start.2 = (f32[3,64,256]{2,1,0:T(8,128)S(1)}, f32[3,64,256]{2,1,0:T(8,128)}, u32[]{:S(2)}) copy-start(f32[3,64,256]{2,1,0:T(8,128)} %param.6) | copy-start | bytes 589828
  3.3 5.5 %collective-permute-start.2 = (f32[136,128]{1,0:T(8,128)S(1)}, f32[136,128]{1,0:T(8,128)S(1)}, u32[]{:S(2)}, u32[]{:S(2)}) collective-permute-start(f32[136,128]{1,0:T(8,128)S(1)} %get-tuple-element.36), channel_id=1, source_target_pairs={{0,4},{4,0},{8,12},{12,8},{1,5},{5,1},{9,13},{13,9},{2,6},{6,2},{1... | collective-permute-start | bytes 208904 | tf_op jit(solution)/shard_map/ppermute | solution.py:176
  6.4 10.6 %collective-permute-start.3 = (f32[64,896]{1,0:T(8,128)S(1)}, f32[64,896]{1,0:T(8,128)S(1)}, u32[]{:S(2)}, u32[]{:S(2)}) collective-permute-start(f32[64,896]{1,0:T(8,128)S(1)} %pad_maximum_fusion.refs_0_), channel_id=1, source_target_pairs={{0,1},{1,0},{2,3},{3,2},{4,5},{5,4},{6,7},{7,6},{8,9},{9,8},{10,11... | collective-permute-start | bytes 688136 | tf_op jit(solution)/shard_map/ppermute | solution.py:173
  6.5 9.9 %collective-permute-start.4 = (f32[64,896]{1,0:T(8,128)S(1)}, f32[64,896]{1,0:T(8,128)S(1)}, u32[]{:S(2)}, u32[]{:S(2)}) collective-permute-start(f32[64,896]{1,0:T(8,128)S(1)} %pad_maximum_fusion.refs_0_), channel_id=1, source_target_pairs={{0,4},{4,0},{8,12},{12,8},{1,5},{5,1},{9,13},{13,9},{2,6},{6,2},{1... | collective-permute-start | bytes 688136 | tf_op jit(solution)/shard_map/ppermute | solution.py:176
  8.8 6.1 %collective-permute-start.5 = (f32[4,32,128]{2,1,0:T(8,128)S(1)}, f32[4,32,128]{2,1,0:T(8,128)S(1)}, u32[]{:S(2)}, u32[]{:S(2)}) collective-permute-start(f32[4,32,128]{2,1,0:T(8,128)S(1)} %add.15.refs_7_), channel_id=1, source_target_pairs={{0,8},{4,12},{8,0},{12,4},{1,9},{5,13},{9,1},{13,5},{2,10},{6,14},... | collective-permute-start | bytes 196616 | tf_op jit(solution)/shard_map/ppermute | solution.py:176
  11.8 9.8 %collective-permute-start.12 = (f32[64,896]{1,0:T(8,128)S(1)}, f32[64,896]{1,0:T(8,128)S(1)}, u32[]{:S(2)}, u32[]{:S(2)}) collective-permute-start(f32[64,896]{1,0:T(8,128)S(1)} %pad_maximum_fusion.1.a0), channel_id=1, source_target_pairs={{0,4},{4,0},{8,12},{12,8},{1,5},{5,1},{9,13},{13,9},{2,6},{6,2},{1... | collective-permute-start | bytes 688136 | tf_op jit(solution)/shard_map/ppermute | solution.py:176
  16.4 1.3 %collective-permute-start.9 = (f32[16,896]{1,0:T(8,128)S(1)}, f32[16,896]{1,0:T(8,128)S(1)}, u32[]{:S(2)}, u32[]{:S(2)}) collective-permute-start(f32[16,896]{1,0:T(8,128)S(1)} %get-tuple-element.74), channel_id=1, source_target_pairs={{0,1},{1,0},{2,3},{3,2},{4,5},{5,4},{6,7},{7,6},{8,9},{9,8},{10,11... | collective-permute-start | bytes 172040 | tf_op jit(solution)/shard_map/ppermute | solution.py:173
  16.5 1.4 %collective-permute-start.8 = (f32[16,896]{1,0:T(8,128)S(1)}, f32[16,896]{1,0:T(8,128)S(1)}, u32[]{:S(2)}, u32[]{:S(2)}) collective-permute-start(f32[16,896]{1,0:T(8,128)S(1)} %get-tuple-element.75), channel_id=1, source_target_pairs={{0,1},{1,0},{2,3},{3,2},{4,5},{5,4},{6,7},{7,6},{8,9},{9,8},{10,11... | collective-permute-start | bytes 172040 | tf_op jit(solution)/shard_map/ppermute | solution.py:173
  17.0 3.5 %collective-permute-start.7 = (f32[16,896]{1,0:T(8,128)S(1)}, f32[16,896]{1,0:T(8,128)S(1)}, u32[]{:S(2)}, u32[]{:S(2)}) collective-permute-start(f32[16,896]{1,0:T(8,128)S(1)} %get-tuple-element.76), channel_id=1, source_target_pairs={{0,1},{1,0},{2,3},{3,2},{4,5},{5,4},{6,7},{7,6},{8,9},{9,8},{10,11... | collective-permute-start | bytes 172040 | tf_op jit(solution)/shard_map/ppermute | solution.py:173
  17.1 3.4 %collective-permute-start.6 = (f32[16,896]{1,0:T(8,128)S(1)}, f32[16,896]{1,0:T(8,128)S(1)}, u32[]{:S(2)}, u32[]{:S(2)}) collective-permute-start(f32[16,896]{1,0:T(8,128)S(1)} %get-tuple-element.77), channel_id=1, source_target_pairs={{0,1},{1,0},{2,3},{3,2},{4,5},{5,4},{6,7},{7,6},{8,9},{9,8},{10,11... | collective-permute-start | bytes 172040 | tf_op jit(solution)/shard_map/ppermute | solution.py:173
  17.7 6.5 %collective-permute-start.11 = (f32[64,896]{1,0:T(8,128)S(1)}, f32[64,896]{1,0:T(8,128)S(1)}, u32[]{:S(2)}, u32[]{:S(2)}) collective-permute-start(f32[64,896]{1,0:T(8,128)S(1)} %pad_maximum_fusion.1.a0), channel_id=1, source_target_pairs={{0,1},{1,0},{2,3},{3,2},{4,5},{5,4},{6,7},{7,6},{8,9},{9,8},{10,11... | collective-permute-start | bytes 688136 | tf_op jit(solution)/shard_map/ppermute | solution.py:173
  17.9 10.3 %collective-permute-start.19 = (f32[64,896]{1,0:T(8,128)S(1)}, f32[64,896]{1,0:T(8,128)S(1)}, u32[]{:S(2)}, u32[]{:S(2)}) collective-permute-start(f32[64,896]{1,0:T(8,128)S(1)} %pad_maximum_fusion.2.a0), channel_id=1, source_target_pairs={{0,4},{4,0},{8,12},{12,8},{1,5},{5,1},{9,13},{13,9},{2,6},{6,2},{1... | collective-permute-start | bytes 688136 | tf_op jit(solution)/shard_map/ppermute | solution.py:176
  21.6 3.0 %collective-permute-start.16 = (f32[16,896]{1,0:T(8,128)S(1)}, f32[16,896]{1,0:T(8,128)S(1)}, u32[]{:S(2)}, u32[]{:S(2)}) collective-permute-start(f32[16,896]{1,0:T(8,128)S(1)} %get-tuple-element.70), channel_id=1, source_target_pairs={{0,1},{1,0},{2,3},{3,2},{4,5},{5,4},{6,7},{7,6},{8,9},{9,8},{10,11... | collective-permute-start | bytes 172040 | tf_op jit(solution)/shard_map/ppermute | solution.py:173
  21.7 5.6 %collective-permute-start.10 = (f32[4,32,128]{2,1,0:T(8,128)S(1)}, f32[4,32,128]{2,1,0:T(8,128)S(1)}, u32[]{:S(2)}, u32[]{:S(2)}) collective-permute-start(f32[4,32,128]{2,1,0:T(8,128)S(1)} %get-tuple-element.44.refs_1_), channel_id=1, source_target_pairs={{0,8},{4,12},{8,0},{12,4},{1,9},{5,13},{9,1},{13,5},{2,10},{6,14},... | collective-permute-start | bytes 196616 | tf_op jit(solution)/shard_map/ppermute | solution.py:176
  24.1 1.2 %collective-permute-start.15 = (f32[16,896]{1,0:T(8,128)S(1)}, f32[16,896]{1,0:T(8,128)S(1)}, u32[]{:S(2)}, u32[]{:S(2)}) collective-permute-start(f32[16,896]{1,0:T(8,128)S(1)} %get-tuple-element.71), channel_id=1, source_target_pairs={{0,1},{1,0},{2,3},{3,2},{4,5},{5,4},{6,7},{7,6},{8,9},{9,8},{10,11... | collective-permute-start | bytes 172040 | tf_op jit(solution)/shard_map/ppermute | solution.py:173
  24.2 1.2 %collective-permute-start.14 = (f32[16,896]{1,0:T(8,128)S(1)}, f32[16,896]{1,0:T(8,128)S(1)}, u32[]{:S(2)}, u32[]{:S(2)}) collective-permute-start(f32[16,896]{1,0:T(8,128)S(1)} %get-tuple-element.72), channel_id=1, source_target_pairs={{0,1},{1,0},{2,3},{3,2},{4,5},{5,4},{6,7},{7,6},{8,9},{9,8},{10,11... | collective-permute-start | bytes 172040 | tf_op jit(solution)/shard_map/ppermute | solution.py:173
  24.6 1.2 %collective-permute-start.13 = (f32[16,896]{1,0:T(8,128)S(1)}, f32[16,896]{1,0:T(8,128)S(1)}, u32[]{:S(2)}, u32[]{:S(2)}) collective-permute-start(f32[16,896]{1,0:T(8,128)S(1)} %get-tuple-element.73), channel_id=1, source_target_pairs={{0,1},{1,0},{2,3},{3,2},{4,5},{5,4},{6,7},{7,6},{8,9},{9,8},{10,11... | collective-permute-start | bytes 172040 | tf_op jit(solution)/shard_map/ppermute | solution.py:173
  25.3 7.3 %collective-permute-start.18 = (f32[64,896]{1,0:T(8,128)S(1)}, f32[64,896]{1,0:T(8,128)S(1)}, u32[]{:S(2)}, u32[]{:S(2)}) collective-permute-start(f32[64,896]{1,0:T(8,128)S(1)} %pad_maximum_fusion.2.a0), channel_id=1, source_target_pairs={{0,1},{1,0},{2,3},{3,2},{4,5},{5,4},{6,7},{7,6},{8,9},{9,8},{10,11... | collective-permute-start | bytes 688136 | tf_op jit(solution)/shard_map/ppermute | solution.py:173
  28.2 4.4 %collective-permute-start.20 = (f32[64,896]{1,0:T(8,128)S(1)}, f32[64,896]{1,0:T(8,128)S(1)}, u32[]{:S(2)}, u32[]{:S(2)}) collective-permute-start(f32[64,896]{1,0:T(8,128)S(1)} %collective-permute-done.19.a2), channel_id=1, source_target_pairs={{0,1},{1,0},{2,3},{3,2},{4,5},{5,4},{6,7},{7,6},{8,9},{9,8},{10,11... | collective-permute-start | bytes 688136 | tf_op jit(solution)/shard_map/ppermute | solution.py:173
  28.3 7.2 %collective-permute-start.17 = (f32[4,32,128]{2,1,0:T(8,128)S(1)}, f32[4,32,128]{2,1,0:T(8,128)S(1)}, u32[]{:S(2)}, u32[]{:S(2)}) collective-permute-start(f32[4,32,128]{2,1,0:T(8,128)S(1)} %get-tuple-element.53.refs_1_), channel_id=1, source_target_pairs={{0,8},{4,12},{8,0},{12,4},{1,9},{5,13},{9,1},{13,5},{2,10},{6,14},... | collective-permute-start | bytes 196616 | tf_op jit(solution)/shard_map/ppermute | solution.py:176
  32.3 5.3 %collective-permute-start.28 = (f32[2,32,128]{2,1,0:T(8,128)S(1)}, f32[2,32,128]{2,1,0:T(8,128)S(1)}, u32[]{:S(2)}, u32[]{:S(2)}) collective-permute-start(f32[2,32,128]{2,1,0:T(8,128)S(1)} %get-tuple-element.66), channel_id=1, source_target_pairs={{0,4},{4,0},{8,12},{12,8},{1,5},{5,1},{9,13},{13,9},{2,6},{6,2},{1... | collective-permute-start | bytes 98312 | tf_op jit(solution)/shard_map/ppermute | solution.py:176
  32.3 8.6 %collective-permute-start.29 = (f32[2,32,128]{2,1,0:T(8,128)S(1)}, f32[2,32,128]{2,1,0:T(8,128)S(1)}, u32[]{:S(2)}, u32[]{:S(2)}) collective-permute-start(f32[2,32,128]{2,1,0:T(8,128)S(1)} %get-tuple-element.65.refs_8_), channel_id=1, source_target_pairs={{0,1},{1,0},{2,3},{3,2},{4,5},{5,4},{6,7},{7,6},{8,9},{9,8},{10,11... | collective-permute-start | bytes 98312 | tf_op jit(solution)/shard_map/ppermute | solution.py:173
  36.5 4.5 %collective-permute-start.22 = (f32[2,32,128]{2,1,0:T(8,128)S(1)}, f32[2,32,128]{2,1,0:T(8,128)S(1)}, u32[]{:S(2)}, u32[]{:S(2)}) collective-permute-start(f32[2,32,128]{2,1,0:T(8,128)S(1)} %get-tuple-element.63), channel_id=1, source_target_pairs={{0,4},{4,0},{8,12},{12,8},{1,5},{5,1},{9,13},{13,9},{2,6},{6,2},{1... | collective-permute-start | bytes 98312 | tf_op jit(solution)/shard_map/ppermute | solution.py:176
  37.6 6.6 %collective-permute-start.30 = (f32[2,32,128]{2,1,0:T(8,128)S(1)}, f32[2,32,128]{2,1,0:T(8,128)S(1)}, u32[]{:S(2)}, u32[]{:S(2)}) collective-permute-start(f32[2,32,128]{2,1,0:T(8,128)S(1)} %collective-permute-done.28.refs_9_), channel_id=1, source_target_pairs={{0,1},{1,0},{2,3},{3,2},{4,5},{5,4},{6,7},{7,6},{8,9},{9,8},{10,11... | collective-permute-start | bytes 98312 | tf_op jit(solution)/shard_map/ppermute | solution.py:173
  37.6 4.8 %collective-permute-start.21 = (f32[32,128]{1,0:T(8,128)S(1)}, f32[32,128]{1,0:T(8,128)S(1)}, u32[]{:S(2)}, u32[]{:S(2)}) collective-permute-start(f32[32,128]{1,0:T(8,128)S(1)} %get-tuple-element.62), channel_id=1, source_target_pairs={{0,8},{4,12},{8,0},{12,4},{1,9},{5,13},{9,1},{13,5},{2,10},{6,14},... | collective-permute-start | bytes 49160 | tf_op jit(solution)/shard_map/ppermute | solution.py:176
  38.6 5.5 %collective-permute-start.23 = (f32[32,128]{1,0:T(8,128)S(1)}, f32[32,128]{1,0:T(8,128)S(1)}, u32[]{:S(2)}, u32[]{:S(2)}) collective-permute-start(f32[32,128]{1,0:T(8,128)S(1)} %get-tuple-element.64), channel_id=1, source_target_pairs={{0,12},{4,8},{8,4},{12,0},{1,13},{5,9},{9,5},{13,1},{2,14},{6,10},... | collective-permute-start | bytes 49160 | tf_op jit(solution)/shard_map/ppermute | solution.py:176
  40.9 4.4 %collective-permute-start.24 = (f32[2,32,128]{2,1,0:T(8,128)S(1)}, f32[2,32,128]{2,1,0:T(8,128)S(1)}, u32[]{:S(2)}, u32[]{:S(2)}) collective-permute-start(f32[2,32,128]{2,1,0:T(8,128)S(1)} %get-tuple-element.61.refs_0_), channel_id=1, source_target_pairs={{0,1},{1,0},{2,3},{3,2},{4,5},{5,4},{6,7},{7,6},{8,9},{9,8},{10,11... | collective-permute-start | bytes 98312 | tf_op jit(solution)/shard_map/ppermute | solution.py:173
  40.9 4.4 %collective-permute-start.26 = (f32[2,32,128]{2,1,0:T(8,128)S(1)}, f32[2,32,128]{2,1,0:T(8,128)S(1)}, u32[]{:S(2)}, u32[]{:S(2)}) collective-permute-start(f32[2,32,128]{2,1,0:T(8,128)S(1)} %collective-permute-done.22.refs_2_), channel_id=1, source_target_pairs={{0,1},{1,0},{2,3},{3,2},{4,5},{5,4},{6,7},{7,6},{8,9},{9,8},{10,11... | collective-permute-start | bytes 98312 | tf_op jit(solution)/shard_map/ppermute | solution.py:173
  42.3 1.8 %collective-permute-start.25 = (f32[32,128]{1,0:T(8,128)S(1)}, f32[32,128]{1,0:T(8,128)S(1)}, u32[]{:S(2)}, u32[]{:S(2)}) collective-permute-start(f32[32,128]{1,0:T(8,128)S(1)} %collective-permute-done.21.refs_1_), channel_id=1, source_target_pairs={{0,1},{1,0},{2,3},{3,2},{4,5},{5,4},{6,7},{7,6},{8,9},{9,8},{10,11... | collective-permute-start | bytes 49160 | tf_op jit(solution)/shard_map/ppermute | solution.py:173
  44.1 1.2 %collective-permute-start.27 = (f32[32,128]{1,0:T(8,128)S(1)}, f32[32,128]{1,0:T(8,128)S(1)}, u32[]{:S(2)}, u32[]{:S(2)}) collective-permute-start(f32[32,128]{1,0:T(8,128)S(1)} %collective-permute-done.23.refs_3_), channel_id=1, source_target_pairs={{0,1},{1,0},{2,3},{3,2},{4,5},{5,4},{6,7},{7,6},{8,9},{9,8},{10,11... | collective-permute-start | bytes 49160 | tf_op jit(solution)/shard_map/ppermute | solution.py:173
  (3 other events, 4.8 us)

commit v6 on v5

--- a/solution.py
+++ b/solution.py
@@ -7,7 +7,7 @@
 from jax.experimental.pallas import tpu as pltpu
 from jax.sharding import PartitionSpec as P
 
-K = {'first': 0.3, 'prep': [2, 0, 0], 'step': [0, 0.1, 0], 'bulk': ['send', 'share0', 'share0'], 'swap': ['recv0', 'share1', 'share2'], 'rest': ['send', 'send', 'send'], 'groups': [[1], [2], [3]], 'meet': 0, 'early': 2, 'cut': [4, 4, 1]}
+K = {'first': 0.3, 'prep': [2, 0, 0], 'step': [0, 0.1, 0], 'bulk': ['none', 'share0', 'share0'], 'swap': ['recv0', 'share1', 'share2'], 'rest': ['send', 'send', 'send'], 'groups': [[1], [2], [3]], 'meet': 0, 'early': 2, 'cut': [4, 2, 4]}
 S = 4
 BS = 128
 LANES = 128

time: 46.9 us -> 46.4 us (0.989)
  starting transfers between devices: 25.3 us -> 24.8 us
    ppermute x11, starting transfers between devices: 21.7 us -> 20.6 us  [to_row(): return lax.ppermute(a, 'row', [(i, i ^ bit) for i in range(count)])]
    ppermute x11, waiting for transfers between devices: 9.58 us -> 10.4 us  [to_row(): return lax.ppermute(a, 'row', [(i, i ^ bit) for i in range(count)])]
    ppermute x20 -> x21, waiting for transfers between devices: 2.29 us -> 1.48 us  [to_core(): return lax.ppermute(a, 'sub', [(0, 1), (1, 0)])]
    ppermute x20 -> x21, starting transfers between devices: 3.62 us -> 4.23 us  [to_core(): return lax.ppermute(a, 'sub', [(0, 1), (1, 0)])]
  transfers between devices with their start and end apart: 31 -> 32, of which waited for: 12 -> 10; matrix products, arithmetic and copies ran while one was open for 3% -> 3% of each run, Pallas kernels for 11% -> 11%
where the time goes in v6:
time: 46.4 us; the launch traced here: 46.3 us
  starting transfers between devices  24.8 us (53%)
  waiting for transfers between devices  11.9 us (26%)
  Pallas kernels  7.27 us (16%)
  local copies, waits for them, and re-layouts  2.01 us (4%)
    ppermute x11, starting transfers between devices, to_row(): return lax.ppermute(a, 'row', [(i, i ^ bit) for i in range(count)])  20.6 us
    ppermute x11, waiting for transfers between devices, to_row(): return lax.ppermute(a, 'row', [(i, i ^ bit) for i in range(count)])  10.4 us
    ppermute x21, starting transfers between devices, to_core(): return lax.ppermute(a, 'sub', [(0, 1), (1, 0)])  4.23 us
    pallas_call x2, Pallas kernels, prepare(): call(functools.partial(prepare_kernel, quarter, place), ready_shapes, [pl...  1.54 us
    ppermute x21, waiting for transfers between devices, to_core(): return lax.ppermute(a, 'sub', [(0, 1), (1, 0)])  1.48 us
    pallas_call x1, Pallas kernels, body(): call(functools.partial(place_kernel, quarter, first), shape((S, BS // 2,...  1.42 us
    pallas_call x1, Pallas kernels, body(): call(kernel, (shape((blocks, quarter, BS), f32), piece), [pltpu.VMEM(a.sh...  1.05 us
    squeeze x1, local copies, waits for them, and re-layouts, body(): diag_first = diag_inverse[0]  0.95 us
  transfers between devices with their start and end apart: 32, of which 10 were waited for; matrix products, arithmetic and copies ran while one was open for 3% of the time, Pallas kernels for 11%

profile of v6, /device:TPU:0, one launch (start us, length us, event | category | flops | bytes accessed | tf_op | source)
XLA Modules:
  0.0 46.3 jit_solution(5792095962060037122)
XLA Ops:
  0.0 0.5 collective-permute-start
  0.5 0.7 %copy-done.3 = s32[3,1,2]{0,2,1:T(2,128)S(1)} copy-done((s32[3,1,2]{0,2,1:T(2,128)S(1)}, s32[3,1,2]{0,2,1:T(2,128)}, u32[]{:S(2)}) %copy-start.3) | copy-done | bytes 48
  1.4 1.0 %slice_bitcast_fusion.3.own = f32[64,512]{1,0:T(8,128)S(1)} fusion(f32[4,64,512]{2,1,0:T(8,128)} %param.5), kind=kLoop, calls=%fused_computation.6 | loop fusion | bytes 262144 | tf_op jit(solution)/shard_map/squeeze | solution.py:208
  2.4 0.8 %shard_map.46 = (f32[4,32,128]{2,1,0:T(8,128)S(1)}, f32[136,128]{1,0:T(8,128)S(1)}) custom-call(s32[6]{0:T(128)S(1)} %stack.27.ids, s32[3,1,2]{2,1,0:T(1,128)S(1)} %copy.12.lists, f32[64,512]{1,0:T(8,128)S(1)} %slice_bitcast_fusion.3.own, f32[4,64,512]{2,1,0:T(8,128)S(1)} %collective-permute-done.other, f32[4,64,128]{2,1,0:T(8,128)S(1)} %copy-done, ...), custom_call_target="tpu_custom_call" | custom-call | flops 300000000 | bytes 1000 | tf_op jit(solution)/shard_map/pallas_call | solution.py:209
  3.3 3.1 %collective-permute-start.2 = (f32[136,128]{1,0:T(8,128)S(1)}, f32[136,128]{1,0:T(8,128)S(1)}, u32[]{:S(2)}, u32[]{:S(2)}) collective-permute-start(f32[136,128]{1,0:T(8,128)S(1)} %get-tuple-element.35), channel_id=1, source_target_pairs={{0,4},{4,0},{8,12},{12,8},{1,5},{5,1},{9,13},{13,9},{2,6},{6,2},{1... | collective-permute-start | bytes 208904 | tf_op jit(solution)/shard_map/ppermute | solution.py:176
  6.4 1.0 %collective-permute-start.4 = (f32[64,896]{1,0:T(8,128)S(1)}, f32[64,896]{1,0:T(8,128)S(1)}, u32[]{:S(2)}, u32[]{:S(2)}) collective-permute-start(f32[64,896]{1,0:T(8,128)S(1)} %pad_maximum_fusion.refs_0_), channel_id=1, source_target_pairs={{0,4},{4,0},{8,12},{12,8},{1,5},{5,1},{9,13},{13,9},{2,6},{6,2},{1... | collective-permute-start | bytes 688136 | tf_op jit(solution)/shard_map/ppermute | solution.py:176
  7.5 1.3 %collective-permute-done.2 = f32[136,128]{1,0:T(8,128)S(1)} collective-permute-done((f32[136,128]{1,0:T(8,128)S(1)}, f32[136,128]{1,0:T(8,128)S(1)}, u32[]{:S(2)}, u32[]{:S(2)}) %collective-permute-start.2) | collective-permute-done | bytes 69664 | tf_op jit(solution)/shard_map/ppermute | solution.py:176
  8.8 3.2 %collective-permute-start.5 = (f32[4,32,128]{2,1,0:T(8,128)S(1)}, f32[4,32,128]{2,1,0:T(8,128)S(1)}, u32[]{:S(2)}, u32[]{:S(2)}) collective-permute-start(f32[4,32,128]{2,1,0:T(8,128)S(1)} %add.15.refs_7_), channel_id=1, source_target_pairs={{0,8},{4,12},{8,0},{12,4},{1,9},{5,13},{9,1},{13,5},{2,10},{6,14},... | collective-permute-start | bytes 196616 | tf_op jit(solution)/shard_map/ppermute | solution.py:176
  12.0 2.0 %collective-permute-start.12 = (f32[64,896]{1,0:T(8,128)S(1)}, f32[64,896]{1,0:T(8,128)S(1)}, u32[]{:S(2)}, u32[]{:S(2)}) collective-permute-start(f32[64,896]{1,0:T(8,128)S(1)} %pad_maximum_fusion.1.a0), channel_id=1, source_target_pairs={{0,4},{4,0},{8,12},{12,8},{1,5},{5,1},{9,13},{13,9},{2,6},{6,2},{1... | collective-permute-start | bytes 688136 | tf_op jit(solution)/shard_map/ppermute | solution.py:176
  13.9 1.1 %collective-permute-done.5.refs_8_ = f32[4,32,128]{2,1,0:T(8,128)S(1)} collective-permute-done((f32[4,32,128]{2,1,0:T(8,128)S(1)}, f32[4,32,128]{2,1,0:T(8,128)S(1)}, u32[]{:S(2)}, u32[]{:S(2)}) %collective-permute-start.5) | collective-permute-done | bytes 65568 | tf_op jit(solution)/shard_map/ppermute | solution.py:176
  15.0 1.4 %collective-permute-done.4.refs_2_ = f32[64,896]{1,0:T(8,128)S(1)} collective-permute-done((f32[64,896]{1,0:T(8,128)S(1)}, f32[64,896]{1,0:T(8,128)S(1)}, u32[]{:S(2)}, u32[]{:S(2)}) %collective-permute-start.4) | collective-permute-done | bytes 229408 | tf_op jit(solution)/shard_map/ppermute | solution.py:176
  16.5 0.5 %collective-permute-start.8 = (f32[16,896]{1,0:T(8,128)S(1)}, f32[16,896]{1,0:T(8,128)S(1)}, u32[]{:S(2)}, u32[]{:S(2)}) collective-permute-start(f32[16,896]{1,0:T(8,128)S(1)} %get-tuple-element.75), channel_id=1, source_target_pairs={{0,1},{1,0},{2,3},{3,2},{4,5},{5,4},{6,7},{7,6},{8,9},{9,8},{10,11... | collective-permute-start | bytes 172040 | tf_op jit(solution)/shard_map/ppermute | solution.py:173
  17.9 2.6 %collective-permute-start.17 = (f32[64,896]{1,0:T(8,128)S(1)}, f32[64,896]{1,0:T(8,128)S(1)}, u32[]{:S(2)}, u32[]{:S(2)}) collective-permute-start(f32[64,896]{1,0:T(8,128)S(1)} %pad_maximum_fusion.2.a0), channel_id=1, source_target_pairs={{0,4},{4,0},{8,12},{12,8},{1,5},{5,1},{9,13},{13,9},{2,6},{6,2},{1... | collective-permute-start | bytes 688136 | tf_op jit(solution)/shard_map/ppermute | solution.py:176
  20.5 1.1 %shard_map.47 = (f32[4,32,128]{2,1,0:T(8,128)S(1)}, f32[4,32,128]{2,1,0:T(8,128)S(1)}) custom-call(s32[6]{0:T(128)S(1)} %stack.27.ids, s32[3,1,2]{2,1,0:T(1,128)S(1)} %copy.12.lists, s32[3,2]{1,0:T(4,128)S(1)} %convert_element_type.6.told, f32[64,896]{1,0:T(8,128)S(1)} %pad_maximum_fusion.refs_0_, f32[64,896]{1,0:T(8,128)S(1)} %collective-permute-done.3.refs_1_, ...), custom_call_target="tpu_custom_call" | custom-call | bytes 1000 | tf_op jit(solution)/shard_map/pallas_call | solution.py:259
  21.7 0.4 collective-permute-start.13
  22.2 1.3 %collective-permute-start.10 = (f32[4,32,128]{2,1,0:T(8,128)S(1)}, f32[4,32,128]{2,1,0:T(8,128)S(1)}, u32[]{:S(2)}, u32[]{:S(2)}) collective-permute-start(f32[4,32,128]{2,1,0:T(8,128)S(1)} %get-tuple-element.42.refs_1_), channel_id=1, source_target_pairs={{0,8},{4,12},{8,0},{12,4},{1,9},{5,13},{9,1},{13,5},{2,10},{6,14},... | collective-permute-start | bytes 196616 | tf_op jit(solution)/shard_map/ppermute | solution.py:176
  23.5 0.8 %shard_map.48 = (bf16[256,512]{1,0:T(8,128)(2,1)S(1)}, bf16[256,512]{1,0:T(8,128)(2,1)S(1)}, bf16[2,256,128]{2,1,0:T(8,128)(2,1)S(1)}, bf16[2,256,128]{2,1,0:T(8,128)(2,1)S(1)}, f32[2,32,128]{2,1,0:T(8,128)S(1)}) custom-call(s32[6]{0:T(128)S(1)} %stack.27.ids, f32[64,896]{1,0:T(8,128)S(1)} %pad_maximum_fusion.1.a0, ...), custom_call_target="tpu_custom_call" | custom-call | bytes 1000 | tf_op jit(solution)/shard_map/pallas_call | solution.py:201
  24.3 3.6 %collective-permute-done.10.refs_2_ = f32[4,32,128]{2,1,0:T(8,128)S(1)} collective-permute-done((f32[4,32,128]{2,1,0:T(8,128)S(1)}, f32[4,32,128]{2,1,0:T(8,128)S(1)}, u32[]{:S(2)}, u32[]{:S(2)}) %collective-permute-start.10) | collective-permute-done | bytes 65568 | tf_op jit(solution)/shard_map/ppermute | solution.py:176
  27.8 0.9 %shard_map.49 = (f32[8,32,128]{2,1,0:T(8,128)S(1)}, f32[4,32,128]{2,1,0:T(8,128)S(1)}) custom-call(s32[3,1,2]{2,1,0:T(1,128)S(1)} %copy.12.lists, s32[3,2]{1,0:T(4,128)S(1)} %convert_element_type.6.told, f32[4,32,128]{2,1,0:T(8,128)S(1)} %get-tuple-element.41.refs_0_, f32[4,32,128]{2,1,0:T(8,128)S(1)} %get-tuple-element.42.refs_1_, ...), custom_call_target="tpu_custom_call" | custom-call | flops 100000000 | bytes 1000 | tf_op jit(solution)/shard_map/pallas_call | solution.py:274
  28.8 2.8 %collective-permute-start.15 = (f32[4,32,128]{2,1,0:T(8,128)S(1)}, f32[4,32,128]{2,1,0:T(8,128)S(1)}, u32[]{:S(2)}, u32[]{:S(2)}) collective-permute-start(f32[4,32,128]{2,1,0:T(8,128)S(1)} %get-tuple-element.51.refs_1_), channel_id=1, source_target_pairs={{0,8},{4,12},{8,0},{12,4},{1,9},{5,13},{9,1},{13,5},{2,10},{6,14},... | collective-permute-start | bytes 196616 | tf_op jit(solution)/shard_map/ppermute | solution.py:176
  31.7 0.5 %collective-permute-start.20 = (f32[16,896]{1,0:T(8,128)S(1)}, f32[16,896]{1,0:T(8,128)S(1)}, u32[]{:S(2)}, u32[]{:S(2)}) collective-permute-start(f32[16,896]{1,0:T(8,128)S(1)} %get-tuple-element.69), channel_id=1, source_target_pairs={{0,1},{1,0},{2,3},{3,2},{4,5},{5,4},{6,7},{7,6},{8,9},{9,8},{10,11... | collective-permute-start | bytes 172040 | tf_op jit(solution)/shard_map/ppermute | solution.py:173
  32.7 0.5 %shard_map.52 = (f32[2,32,128]{2,1,0:T(8,128)S(1)}, f32[2,32,128]{2,1,0:T(8,128)S(1)}) custom-call(s32[6]{0:T(128)S(1)} %stack.27.ids, f32[8,32,128]{2,1,0:T(8,128)S(1)} %get-tuple-element.50.refs_0_.solved), custom_call_target="tpu_custom_call" | custom-call | bytes 1000 | tf_op jit(solution)/shard_map/pallas_call | solution.py:281
  33.6 0.8 %shard_map.50 = (bf16[256,512]{1,0:T(8,128)(2,1)S(1)}, bf16[256,512]{1,0:T(8,128)(2,1)S(1)}, bf16[2,256,128]{2,1,0:T(8,128)(2,1)S(1)}, bf16[2,256,128]{2,1,0:T(8,128)(2,1)S(1)}, f32[2,32,128]{2,1,0:T(8,128)S(1)}) custom-call(s32[6]{0:T(128)S(1)} %stack.27.ids, f32[64,896]{1,0:T(8,128)S(1)} %pad_maximum_fusion.2.a0, ...), custom_call_target="tpu_custom_call" | custom-call | bytes 1000 | tf_op jit(solution)/shard_map/pallas_call | solution.py:201
  34.4 0.9 %shard_map.51 = (f32[2,32,128]{2,1,0:T(8,128)S(1)}, f32[2,32,128]{2,1,0:T(8,128)S(1)}, f32[32,128]{1,0:T(8,128)S(1)}, f32[32,128]{1,0:T(8,128)S(1)}) custom-call(s32[6]{0:T(128)S(1)} %stack.27.ids, s32[3,1,2]{2,1,0:T(1,128)S(1)} %copy.12.lists, s32[3,2]{1,0:T(4,128)S(1)} %convert_element_type.6.told, f32[8,32,128]{2,1,0:T(8,128)S(1)} %get-tuple-element.50.refs_0_.solved, ...), custom_call_target="tpu_custom_call" | custom-call | bytes 1000 | tf_op jit(solution)/shard_map/pallas_call | solution.py:295
  35.3 1.9 %collective-permute-start.23 = (f32[2,32,128]{2,1,0:T(8,128)S(1)}, f32[2,32,128]{2,1,0:T(8,128)S(1)}, u32[]{:S(2)}, u32[]{:S(2)}) collective-permute-start(f32[2,32,128]{2,1,0:T(8,128)S(1)} %get-tuple-element.61), channel_id=1, source_target_pairs={{0,4},{4,0},{8,12},{12,8},{1,5},{5,1},{9,13},{13,9},{2,6},{6,2},{1... | collective-permute-start | bytes 98312 | tf_op jit(solution)/shard_map/ppermute | solution.py:176
  37.4 0.7 %collective-permute-start.22 = (f32[32,128]{1,0:T(8,128)S(1)}, f32[32,128]{1,0:T(8,128)S(1)}, u32[]{:S(2)}, u32[]{:S(2)}) collective-permute-start(f32[32,128]{1,0:T(8,128)S(1)} %get-tuple-element.60), channel_id=1, source_target_pairs={{0,8},{4,12},{8,0},{12,4},{1,9},{5,13},{9,1},{13,5},{2,10},{6,14},... | collective-permute-start | bytes 49160 | tf_op jit(solution)/shard_map/ppermute | solution.py:176
  38.1 2.0 %collective-permute-start.24 = (f32[32,128]{1,0:T(8,128)S(1)}, f32[32,128]{1,0:T(8,128)S(1)}, u32[]{:S(2)}, u32[]{:S(2)}) collective-permute-start(f32[32,128]{1,0:T(8,128)S(1)} %get-tuple-element.62), channel_id=1, source_target_pairs={{0,12},{4,8},{8,4},{12,0},{1,13},{5,9},{9,5},{13,1},{2,14},{6,10},... | collective-permute-start | bytes 49160 | tf_op jit(solution)/shard_map/ppermute | solution.py:176
  40.2 0.5 %collective-permute-start.27 = (f32[2,32,128]{2,1,0:T(8,128)S(1)}, f32[2,32,128]{2,1,0:T(8,128)S(1)}, u32[]{:S(2)}, u32[]{:S(2)}) collective-permute-start(f32[2,32,128]{2,1,0:T(8,128)S(1)} %collective-permute-done.23.refs_2_), channel_id=1, source_target_pairs={{0,1},{1,0},{2,3},{3,2},{4,5},{5,4},{6,7},{7,6},{8,9},{9,8},{10,11... | collective-permute-start | bytes 98312 | tf_op jit(solution)/shard_map/ppermute | solution.py:173
  40.7 1.4 %collective-permute-done.22.refs_1_ = f32[32,128]{1,0:T(8,128)S(1)} collective-permute-done((f32[32,128]{1,0:T(8,128)S(1)}, f32[32,128]{1,0:T(8,128)S(1)}, u32[]{:S(2)}, u32[]{:S(2)}) %collective-permute-start.22) | collective-permute-done | bytes 16416 | tf_op jit(solution)/shard_map/ppermute | solution.py:176
  42.1 1.6 %collective-permute-done.24.refs_3_ = f32[32,128]{1,0:T(8,128)S(1)} collective-permute-done((f32[32,128]{1,0:T(8,128)S(1)}, f32[32,128]{1,0:T(8,128)S(1)}, u32[]{:S(2)}, u32[]{:S(2)}) %collective-permute-start.24) | collective-permute-done | bytes 16416 | tf_op jit(solution)/shard_map/ppermute | solution.py:176
  43.7 1.2 %collective-permute-done.28.refs_7_ = f32[32,128]{1,0:T(8,128)S(1)} collective-permute-done((f32[32,128]{1,0:T(8,128)S(1)}, f32[32,128]{1,0:T(8,128)S(1)}, u32[]{:S(2)}, u32[]{:S(2)}) %collective-permute-start.28) | collective-permute-done | bytes 16416 | tf_op jit(solution)/shard_map/ppermute | solution.py:173
  44.9 1.4 %shard_map.53 = f32[4,64,128]{2,1,0:T(8,128)} custom-call(s32[6]{0:T(128)S(1)} %stack.27.ids, f32[2,32,128]{2,1,0:T(8,128)S(1)} %get-tuple-element.59.refs_0_, f32[32,128]{1,0:T(8,128)S(1)} %collective-permute-done.22.refs_1_, f32[2,32,128]{2,1,0:T(8,128)S(1)} %collective-permute-done.23.refs_2_, f32[32,128]{1,0:T(8,128)S(1)} %collective-permute-done.24.refs_3_, ...), custom_call_target="tpu_custom_call" | custom-call | bytes 1000 | tf_op jit(solution)/shard_map/pallas_call | solution.py:308
  (64 shorter events, 2.7 us)
Async XLA Ops:
  0.0 2.4 %collective-permute-start = (f32[4,64,512]{2,1,0:T(8,128)}, f32[4,64,512]{2,1,0:T(8,128)S(1)}, u32[]{:S(2)}, u32[]{:S(2)}) collective-permute-start(f32[4,64,512]{2,1,0:T(8,128)} %param.5), channel_id=1, source_target_pairs={{0,1},{1,0},{2,3},{3,2},{4,5},{5,4},{6,7},{7,6},{8,9},{9,8},{10,11... | collective-permute-start | bytes 1572872 | tf_op jit(solution)/shard_map/ppermute | solution.py:173
  0.5 1.9 %collective-permute-start.1 = (f32[4,64,128]{2,1,0:T(8,128)}, f32[4,64,128]{2,1,0:T(8,128)S(1)}, u32[]{:S(2)}, u32[]{:S(2)}) collective-permute-start(f32[4,64,128]{2,1,0:T(8,128)} %own_sides.1), channel_id=1, source_target_pairs={{0,1},{1,0},{2,3},{3,2},{4,5},{5,4},{6,7},{7,6},{8,9},{9,8},{10,11... | collective-permute-start | bytes 393224 | tf_op jit(solution)/shard_map/ppermute | solution.py:173
  3.3 5.5 %collective-permute-start.2 = (f32[136,128]{1,0:T(8,128)S(1)}, f32[136,128]{1,0:T(8,128)S(1)}, u32[]{:S(2)}, u32[]{:S(2)}) collective-permute-start(f32[136,128]{1,0:T(8,128)S(1)} %get-tuple-element.35), channel_id=1, source_target_pairs={{0,4},{4,0},{8,12},{12,8},{1,5},{5,1},{9,13},{13,9},{2,6},{6,2},{1... | collective-permute-start | bytes 208904 | tf_op jit(solution)/shard_map/ppermute | solution.py:176
  6.4 10.0 %collective-permute-start.4 = (f32[64,896]{1,0:T(8,128)S(1)}, f32[64,896]{1,0:T(8,128)S(1)}, u32[]{:S(2)}, u32[]{:S(2)}) collective-permute-start(f32[64,896]{1,0:T(8,128)S(1)} %pad_maximum_fusion.refs_0_), channel_id=1, source_target_pairs={{0,4},{4,0},{8,12},{12,8},{1,5},{5,1},{9,13},{13,9},{2,6},{6,2},{1... | collective-permute-start | bytes 688136 | tf_op jit(solution)/shard_map/ppermute | solution.py:176
  7.4 9.7 %collective-permute-start.3 = (f32[64,896]{1,0:T(8,128)S(1)}, f32[64,896]{1,0:T(8,128)S(1)}, u32[]{:S(2)}, u32[]{:S(2)}) collective-permute-start(f32[64,896]{1,0:T(8,128)S(1)} %pad_maximum_fusion.refs_0_), channel_id=1, source_target_pairs={{0,1},{1,0},{2,3},{3,2},{4,5},{5,4},{6,7},{7,6},{8,9},{9,8},{10,11... | collective-permute-start | bytes 688136 | tf_op jit(solution)/shard_map/ppermute | solution.py:173
  8.8 6.2 %collective-permute-start.5 = (f32[4,32,128]{2,1,0:T(8,128)S(1)}, f32[4,32,128]{2,1,0:T(8,128)S(1)}, u32[]{:S(2)}, u32[]{:S(2)}) collective-permute-start(f32[4,32,128]{2,1,0:T(8,128)S(1)} %add.15.refs_7_), channel_id=1, source_target_pairs={{0,8},{4,12},{8,0},{12,4},{1,9},{5,13},{9,1},{13,5},{2,10},{6,14},... | collective-permute-start | bytes 196616 | tf_op jit(solution)/shard_map/ppermute | solution.py:176
  12.0 9.6 %collective-permute-start.12 = (f32[64,896]{1,0:T(8,128)S(1)}, f32[64,896]{1,0:T(8,128)S(1)}, u32[]{:S(2)}, u32[]{:S(2)}) collective-permute-start(f32[64,896]{1,0:T(8,128)S(1)} %pad_maximum_fusion.1.a0), channel_id=1, source_target_pairs={{0,4},{4,0},{8,12},{12,8},{1,5},{5,1},{9,13},{13,9},{2,6},{6,2},{1... | collective-permute-start | bytes 688136 | tf_op jit(solution)/shard_map/ppermute | solution.py:176
  16.4 1.3 %collective-permute-start.9 = (f32[16,896]{1,0:T(8,128)S(1)}, f32[16,896]{1,0:T(8,128)S(1)}, u32[]{:S(2)}, u32[]{:S(2)}) collective-permute-start(f32[16,896]{1,0:T(8,128)S(1)} %get-tuple-element.74), channel_id=1, source_target_pairs={{0,1},{1,0},{2,3},{3,2},{4,5},{5,4},{6,7},{7,6},{8,9},{9,8},{10,11... | collective-permute-start | bytes 172040 | tf_op jit(solution)/shard_map/ppermute | solution.py:173
  16.5 1.4 %collective-permute-start.8 = (f32[16,896]{1,0:T(8,128)S(1)}, f32[16,896]{1,0:T(8,128)S(1)}, u32[]{:S(2)}, u32[]{:S(2)}) collective-permute-start(f32[16,896]{1,0:T(8,128)S(1)} %get-tuple-element.75), channel_id=1, source_target_pairs={{0,1},{1,0},{2,3},{3,2},{4,5},{5,4},{6,7},{7,6},{8,9},{9,8},{10,11... | collective-permute-start | bytes 172040 | tf_op jit(solution)/shard_map/ppermute | solution.py:173
  17.0 3.5 %collective-permute-start.7 = (f32[16,896]{1,0:T(8,128)S(1)}, f32[16,896]{1,0:T(8,128)S(1)}, u32[]{:S(2)}, u32[]{:S(2)}) collective-permute-start(f32[16,896]{1,0:T(8,128)S(1)} %get-tuple-element.76), channel_id=1, source_target_pairs={{0,1},{1,0},{2,3},{3,2},{4,5},{5,4},{6,7},{7,6},{8,9},{9,8},{10,11... | collective-permute-start | bytes 172040 | tf_op jit(solution)/shard_map/ppermute | solution.py:173
  17.1 3.4 %collective-permute-start.6 = (f32[16,896]{1,0:T(8,128)S(1)}, f32[16,896]{1,0:T(8,128)S(1)}, u32[]{:S(2)}, u32[]{:S(2)}) collective-permute-start(f32[16,896]{1,0:T(8,128)S(1)} %get-tuple-element.77), channel_id=1, source_target_pairs={{0,1},{1,0},{2,3},{3,2},{4,5},{5,4},{6,7},{7,6},{8,9},{9,8},{10,11... | collective-permute-start | bytes 172040 | tf_op jit(solution)/shard_map/ppermute | solution.py:173
  17.7 5.7 %collective-permute-start.11 = (f32[64,896]{1,0:T(8,128)S(1)}, f32[64,896]{1,0:T(8,128)S(1)}, u32[]{:S(2)}, u32[]{:S(2)}) collective-permute-start(f32[64,896]{1,0:T(8,128)S(1)} %pad_maximum_fusion.1.a0), channel_id=1, source_target_pairs={{0,1},{1,0},{2,3},{3,2},{4,5},{5,4},{6,7},{7,6},{8,9},{9,8},{10,11... | collective-permute-start | bytes 688136 | tf_op jit(solution)/shard_map/ppermute | solution.py:173
  17.9 13.7 %collective-permute-start.17 = (f32[64,896]{1,0:T(8,128)S(1)}, f32[64,896]{1,0:T(8,128)S(1)}, u32[]{:S(2)}, u32[]{:S(2)}) collective-permute-start(f32[64,896]{1,0:T(8,128)S(1)} %pad_maximum_fusion.2.a0), channel_id=1, source_target_pairs={{0,4},{4,0},{8,12},{12,8},{1,5},{5,1},{9,13},{13,9},{2,6},{6,2},{1... | collective-permute-start | bytes 688136 | tf_op jit(solution)/shard_map/ppermute | solution.py:176
  21.6 1.9 %collective-permute-start.14 = (f32[32,896]{1,0:T(8,128)S(1)}, f32[32,896]{1,0:T(8,128)S(1)}, u32[]{:S(2)}, u32[]{:S(2)}) collective-permute-start(f32[32,896]{1,0:T(8,128)S(1)} %get-tuple-element.72), channel_id=1, source_target_pairs={{0,1},{1,0},{2,3},{3,2},{4,5},{5,4},{6,7},{7,6},{8,9},{9,8},{10,11... | collective-permute-start | bytes 344072 | tf_op jit(solution)/shard_map/ppermute | solution.py:173
  21.7 1.8 %collective-permute-start.13 = (f32[32,896]{1,0:T(8,128)S(1)}, f32[32,896]{1,0:T(8,128)S(1)}, u32[]{:S(2)}, u32[]{:S(2)}) collective-permute-start(f32[32,896]{1,0:T(8,128)S(1)} %get-tuple-element.73), channel_id=1, source_target_pairs={{0,1},{1,0},{2,3},{3,2},{4,5},{5,4},{6,7},{7,6},{8,9},{9,8},{10,11... | collective-permute-start | bytes 344072 | tf_op jit(solution)/shard_map/ppermute | solution.py:173
  22.2 5.7 %collective-permute-start.10 = (f32[4,32,128]{2,1,0:T(8,128)S(1)}, f32[4,32,128]{2,1,0:T(8,128)S(1)}, u32[]{:S(2)}, u32[]{:S(2)}) collective-permute-start(f32[4,32,128]{2,1,0:T(8,128)S(1)} %get-tuple-element.42.refs_1_), channel_id=1, source_target_pairs={{0,8},{4,12},{8,0},{12,4},{1,9},{5,13},{9,1},{13,5},{2,10},{6,14},... | collective-permute-start | bytes 196616 | tf_op jit(solution)/shard_map/ppermute | solution.py:176
  23.5 8.8 %collective-permute-start.16 = (f32[64,896]{1,0:T(8,128)S(1)}, f32[64,896]{1,0:T(8,128)S(1)}, u32[]{:S(2)}, u32[]{:S(2)}) collective-permute-start(f32[64,896]{1,0:T(8,128)S(1)} %pad_maximum_fusion.2.a0), channel_id=1, source_target_pairs={{0,1},{1,0},{2,3},{3,2},{4,5},{5,4},{6,7},{7,6},{8,9},{9,8},{10,11... | collective-permute-start | bytes 688136 | tf_op jit(solution)/shard_map/ppermute | solution.py:173
  28.8 5.6 %collective-permute-start.15 = (f32[4,32,128]{2,1,0:T(8,128)S(1)}, f32[4,32,128]{2,1,0:T(8,128)S(1)}, u32[]{:S(2)}, u32[]{:S(2)}) collective-permute-start(f32[4,32,128]{2,1,0:T(8,128)S(1)} %get-tuple-element.51.refs_1_), channel_id=1, source_target_pairs={{0,8},{4,12},{8,0},{12,4},{1,9},{5,13},{9,1},{13,5},{2,10},{6,14},... | collective-permute-start | bytes 196616 | tf_op jit(solution)/shard_map/ppermute | solution.py:176
  31.6 1.6 %collective-permute-start.21 = (f32[16,896]{1,0:T(8,128)S(1)}, f32[16,896]{1,0:T(8,128)S(1)}, u32[]{:S(2)}, u32[]{:S(2)}) collective-permute-start(f32[16,896]{1,0:T(8,128)S(1)} %get-tuple-element.68), channel_id=1, source_target_pairs={{0,1},{1,0},{2,3},{3,2},{4,5},{5,4},{6,7},{7,6},{8,9},{9,8},{10,11... | collective-permute-start | bytes 172040 | tf_op jit(solution)/shard_map/ppermute | solution.py:173
  31.7 1.7 %collective-permute-start.20 = (f32[16,896]{1,0:T(8,128)S(1)}, f32[16,896]{1,0:T(8,128)S(1)}, u32[]{:S(2)}, u32[]{:S(2)}) collective-permute-start(f32[16,896]{1,0:T(8,128)S(1)} %get-tuple-element.69), channel_id=1, source_target_pairs={{0,1},{1,0},{2,3},{3,2},{4,5},{5,4},{6,7},{7,6},{8,9},{9,8},{10,11... | collective-permute-start | bytes 172040 | tf_op jit(solution)/shard_map/ppermute | solution.py:173
  32.2 1.3 %collective-permute-start.19 = (f32[16,896]{1,0:T(8,128)S(1)}, f32[16,896]{1,0:T(8,128)S(1)}, u32[]{:S(2)}, u32[]{:S(2)}) collective-permute-start(f32[16,896]{1,0:T(8,128)S(1)} %get-tuple-element.70), channel_id=1, source_target_pairs={{0,1},{1,0},{2,3},{3,2},{4,5},{5,4},{6,7},{7,6},{8,9},{9,8},{10,11... | collective-permute-start | bytes 172040 | tf_op jit(solution)/shard_map/ppermute | solution.py:173
  32.3 1.3 %collective-permute-start.18 = (f32[16,896]{1,0:T(8,128)S(1)}, f32[16,896]{1,0:T(8,128)S(1)}, u32[]{:S(2)}, u32[]{:S(2)}) collective-permute-start(f32[16,896]{1,0:T(8,128)S(1)} %get-tuple-element.71), channel_id=1, source_target_pairs={{0,1},{1,0},{2,3},{3,2},{4,5},{5,4},{6,7},{7,6},{8,9},{9,8},{10,11... | collective-permute-start | bytes 172040 | tf_op jit(solution)/shard_map/ppermute | solution.py:173
  33.3 4.0 %collective-permute-start.29 = (f32[2,32,128]{2,1,0:T(8,128)S(1)}, f32[2,32,128]{2,1,0:T(8,128)S(1)}, u32[]{:S(2)}, u32[]{:S(2)}) collective-permute-start(f32[2,32,128]{2,1,0:T(8,128)S(1)} %get-tuple-element.64), channel_id=1, source_target_pairs={{0,4},{4,0},{8,12},{12,8},{1,5},{5,1},{9,13},{13,9},{2,6},{6,2},{1... | collective-permute-start | bytes 98312 | tf_op jit(solution)/shard_map/ppermute | solution.py:176
  33.4 6.8 %collective-permute-start.30 = (f32[2,32,128]{2,1,0:T(8,128)S(1)}, f32[2,32,128]{2,1,0:T(8,128)S(1)}, u32[]{:S(2)}, u32[]{:S(2)}) collective-permute-start(f32[2,32,128]{2,1,0:T(8,128)S(1)} %get-tuple-element.63.refs_8_), channel_id=1, source_target_pairs={{0,1},{1,0},{2,3},{3,2},{4,5},{5,4},{6,7},{7,6},{8,9},{9,8},{10,11... | collective-permute-start | bytes 98312 | tf_op jit(solution)/shard_map/ppermute | solution.py:173
  35.3 4.8 %collective-permute-start.23 = (f32[2,32,128]{2,1,0:T(8,128)S(1)}, f32[2,32,128]{2,1,0:T(8,128)S(1)}, u32[]{:S(2)}, u32[]{:S(2)}) collective-permute-start(f32[2,32,128]{2,1,0:T(8,128)S(1)} %get-tuple-element.61), channel_id=1, source_target_pairs={{0,4},{4,0},{8,12},{12,8},{1,5},{5,1},{9,13},{13,9},{2,6},{6,2},{1... | collective-permute-start | bytes 98312 | tf_op jit(solution)/shard_map/ppermute | solution.py:176
  37.2 6.4 %collective-permute-start.31 = (f32[2,32,128]{2,1,0:T(8,128)S(1)}, f32[2,32,128]{2,1,0:T(8,128)S(1)}, u32[]{:S(2)}, u32[]{:S(2)}) collective-permute-start(f32[2,32,128]{2,1,0:T(8,128)S(1)} %collective-permute-done.29.refs_9_), channel_id=1, source_target_pairs={{0,1},{1,0},{2,3},{3,2},{4,5},{5,4},{6,7},{7,6},{8,9},{9,8},{10,11... | collective-permute-start | bytes 98312 | tf_op jit(solution)/shard_map/ppermute | solution.py:173
  37.4 4.6 %collective-permute-start.22 = (f32[32,128]{1,0:T(8,128)S(1)}, f32[32,128]{1,0:T(8,128)S(1)}, u32[]{:S(2)}, u32[]{:S(2)}) collective-permute-start(f32[32,128]{1,0:T(8,128)S(1)} %get-tuple-element.60), channel_id=1, source_target_pairs={{0,8},{4,12},{8,0},{12,4},{1,9},{5,13},{9,1},{13,5},{2,10},{6,14},... | collective-permute-start | bytes 49160 | tf_op jit(solution)/shard_map/ppermute | solution.py:176
  38.1 5.5 %collective-permute-start.24 = (f32[32,128]{1,0:T(8,128)S(1)}, f32[32,128]{1,0:T(8,128)S(1)}, u32[]{:S(2)}, u32[]{:S(2)}) collective-permute-start(f32[32,128]{1,0:T(8,128)S(1)} %get-tuple-element.62), channel_id=1, source_target_pairs={{0,12},{4,8},{8,4},{12,0},{1,13},{5,9},{9,5},{13,1},{2,14},{6,10},... | collective-permute-start | bytes 49160 | tf_op jit(solution)/shard_map/ppermute | solution.py:176
  40.1 4.7 %collective-permute-start.25 = (f32[2,32,128]{2,1,0:T(8,128)S(1)}, f32[2,32,128]{2,1,0:T(8,128)S(1)}, u32[]{:S(2)}, u32[]{:S(2)}) collective-permute-start(f32[2,32,128]{2,1,0:T(8,128)S(1)} %get-tuple-element.59.refs_0_), channel_id=1, source_target_pairs={{0,1},{1,0},{2,3},{3,2},{4,5},{5,4},{6,7},{7,6},{8,9},{9,8},{10,11... | collective-permute-start | bytes 98312 | tf_op jit(solution)/shard_map/ppermute | solution.py:173
  40.2 4.7 %collective-permute-start.27 = (f32[2,32,128]{2,1,0:T(8,128)S(1)}, f32[2,32,128]{2,1,0:T(8,128)S(1)}, u32[]{:S(2)}, u32[]{:S(2)}) collective-permute-start(f32[2,32,128]{2,1,0:T(8,128)S(1)} %collective-permute-done.23.refs_2_), channel_id=1, source_target_pairs={{0,1},{1,0},{2,3},{3,2},{4,5},{5,4},{6,7},{7,6},{8,9},{9,8},{10,11... | collective-permute-start | bytes 98312 | tf_op jit(solution)/shard_map/ppermute | solution.py:173
  42.1 1.6 %collective-permute-start.26 = (f32[32,128]{1,0:T(8,128)S(1)}, f32[32,128]{1,0:T(8,128)S(1)}, u32[]{:S(2)}, u32[]{:S(2)}) collective-permute-start(f32[32,128]{1,0:T(8,128)S(1)} %collective-permute-done.22.refs_1_), channel_id=1, source_target_pairs={{0,1},{1,0},{2,3},{3,2},{4,5},{5,4},{6,7},{7,6},{8,9},{9,8},{10,11... | collective-permute-start | bytes 49160 | tf_op jit(solution)/shard_map/ppermute | solution.py:173
  43.7 1.2 %collective-permute-start.28 = (f32[32,128]{1,0:T(8,128)S(1)}, f32[32,128]{1,0:T(8,128)S(1)}, u32[]{:S(2)}, u32[]{:S(2)}) collective-permute-start(f32[32,128]{1,0:T(8,128)S(1)} %collective-permute-done.24.refs_3_), channel_id=1, source_target_pairs={{0,1},{1,0},{2,3},{3,2},{4,5},{5,4},{6,7},{7,6},{8,9},{9,8},{10,11... | collective-permute-start | bytes 49160 | tf_op jit(solution)/shard_map/ppermute | solution.py:173
  (4 other events, 8.8 us)
